TPU v7x, 32 devices: a whole 2x2x4 slice. The times are simulated.
32 devices in a mesh: groups: 2 (over y), row: 4 (over x, core), col: 4 (over z).
Axes of the slice: x: 2, y: 2, z: 4, core: 2. Of those that a mesh axis runs over, the one named last changes fastest.
Arguments:
- tokens: bfloat16 [128, 7168], P(('groups', 'row', 'col')), parts along dimension 0, may hold values from -6 to 6
- expert_ids: int32 [128, 8], P(('groups', 'row', 'col')), parts along dimension 0, may hold values from 0 to 15, all different within a row; in each aligned block of 4 rows (0 to 3, 4 to 7, ...) at most 3 rows name the same one
- route_weight: bfloat16 [128, 8], P(('groups', 'row', 'col')), parts along dimension 0, may hold values from 0.099609375 to 0.59765625
- dither: bfloat16 [128, 4, 7168], P(('groups', 'row', 'col')), parts along dimension 0, may hold values from 0 to 1
- gate_proj: bfloat16 [4, 4, 7168, 2048], P('row', 'col'), may hold values from -0.0625 to 0.0625
- up_proj: bfloat16 [4, 4, 7168, 2048], P('row', 'col'), may hold values from -0.0625 to 0.0625
- down_proj: bfloat16 [4, 4, 2048, 7168], P('row', 'col'), may hold values from -0.125 to 0.125
Outputs:
- layer_out: bfloat16 [128, 7168], P(('groups', 'row', 'col')), parts along dimension 0
There are 2 independent parts, one for each index of `groups`. A program takes and returns all parts, laid end to end along the dimension named above; an argument that names none is the same for every part. Nothing has to cross between parts.
Inputs may be any that keep to these rules, and one draw needn't show every extreme that they name: `expert_ids`: each row names 8 different experts; within the rows of one device (aligned blocks of 4 rows) no expert is named by more than 3 rows, and in some such block some expert is named by exactly 3 rows.
All inputs are finite; a program needn't handle non-finite values.
Results may differ from a plain program's by a relative error of at most 0.0085.
Values may be sent and summed in bfloat16 or wider, within the bound.
No kernel may reach another device: no remote copies, remote signals or barrier semaphores. Data moves between devices by JAX's collectives and lax.ppermute only.
A program may use at most 192 MiB of HBM per device.

v0:
```python
import jax
import jax.numpy as jnp
from jax import lax
from jax.sharding import PartitionSpec as P

FF = 2048


def expert_apply(batch, gate_local, up_local, down_local):
    flat = batch.reshape(-1, batch.shape[-1])
    gate_pre = jnp.dot(flat, gate_local, preferred_element_type=jnp.float32)
    up_pre = jnp.dot(flat, up_local, preferred_element_type=jnp.float32)
    hidden = (jax.nn.silu(gate_pre) * up_pre).astype(jnp.bfloat16)
    partial_value = jnp.dot(hidden, down_local, preferred_element_type=jnp.float32).astype(
        jnp.bfloat16
    )
    return partial_value.reshape(batch.shape)


def local(tokens, expert_ids, route_weight, dither, gate_proj, up_proj, down_proj):
    row_count = lax.axis_size("row")
    col_count = lax.axis_size("col")
    tok_count = tokens.shape[0]
    model_width = tokens.shape[1]
    pieces = FF // gate_proj.shape[3]
    per_row = col_count // pieces
    slot_count = 3 * tok_count // 4
    expert_count = row_count * per_row
    gate_local = gate_proj[0, 0]
    up_local = up_proj[0, 0]
    down_local = down_proj[0, 0]
    labels = lax.broadcasted_iota(jnp.int32, (1, 1, expert_count), 2)
    matches = expert_ids[:, :, None] == labels
    counted = jnp.sum(matches.astype(jnp.int32), axis=1)
    weighted = jnp.sum(
        jnp.where(matches, route_weight[:, :, None].astype(jnp.float32), 0.0), axis=1
    )
    before = jnp.cumsum(counted, axis=0) - counted
    slot_ids = lax.broadcasted_iota(jnp.int32, (1, 1, slot_count), 2)
    placed = (counted[:, :, None] == 1) & (before[:, :, None] == slot_ids)
    placed = placed.reshape(tok_count, row_count, per_row, slot_count)
    shares = (
        placed.astype(jnp.float32) * weighted.reshape(tok_count, row_count, per_row)[:, :, :, None]
    )
    place_bf = placed.astype(jnp.bfloat16)
    outgoing = jnp.einsum(
        "trjm,td->jrmd", place_bf, tokens, preferred_element_type=jnp.float32
    ).astype(jnp.bfloat16)
    share_out = jnp.transpose(shares, (2, 1, 3, 0)).astype(jnp.bfloat16)
    arrived, arrived_share, arrived_dither = (
        lax.all_to_all(outgoing, "row", split_axis=1, concat_axis=1, tiled=True),
        lax.all_to_all(share_out, "row", split_axis=1, concat_axis=1, tiled=True),
        lax.all_to_all(dither, "row", split_axis=1, concat_axis=1, tiled=True),
    )
    fanned = jnp.broadcast_to(arrived[:, None], (per_row, pieces) + arrived.shape[1:])
    fanned = fanned.reshape((col_count,) + arrived.shape[1:])
    returned = lax.all_to_all(
        expert_apply(
            lax.all_to_all(fanned, "col", split_axis=0, concat_axis=0, tiled=True),
            gate_local,
            up_local,
            down_local,
        ),
        "col",
        split_axis=0,
        concat_axis=0,
        tiled=True,
    )
    merged = jnp.sum(
        returned.reshape(per_row, pieces, row_count, slot_count, model_width).astype(jnp.float32),
        axis=1,
    )
    combined = jnp.einsum(
        "jrmt,jrmd->trd", arrived_share.astype(jnp.float32), merged, precision=lax.Precision.HIGHEST
    )
    spread = 0.125 * jnp.max(jnp.abs(combined), axis=2, keepdims=True)
    rounded = (combined + spread * (arrived_dither.astype(jnp.float32) - 0.5)).astype(jnp.bfloat16)
    collected = lax.all_to_all(rounded, "row", split_axis=1, concat_axis=1, tiled=True)
    return jnp.sum(collected.astype(jnp.float32), axis=1).astype(jnp.bfloat16)


def solution(mesh):
    return jax.shard_map(
        local,
        mesh=mesh,
        in_specs=(
            P(("groups", "row", "col"), None),
            P(("groups", "row", "col"), None),
            P(("groups", "row", "col"), None),
            P(("groups", "row", "col"), None, None),
            P("row", "col", None, None),
            P("row", "col", None, None),
            P("row", "col", None, None),
        ),
        out_specs=P(("groups", "row", "col"), None),
        check_vma=False,
    )
```

profile of v0, /device:TPU:0, one launch (start us, length us, event | category | flops | bytes accessed | tf_op | source)
XLA Modules:
  0.0 119.7 jit_solution(11613312551363275289)
XLA Ops:
  0.0 0.8 convert_reduce_fusion
  0.8 0.1 reduce_sum.37
  0.9 0.1 copy.53
  1.0 0.1 copy.52
  1.1 0.3 fusion.9
  1.5 14.6 %all_to_all.30 = bf16[4,4,3,7168]{3,0,2,1:T(4,128)(2,1)S(1)} all-to-all(bf16[4,4,3,7168]{3,0,2,1:T(4,128)(2,1)S(1)} %fusion.9), channel_id=1, replica_groups=mesh['groups'=2,'row'=4,'col'=4] {'row'}, dimensions={1} | all-to-all | bytes 1376256 | tf_op jit(solution)/shard_map/all_to_all | solution.py:51
  16.1 1.2 %copy.54 = bf16[4,4,3,7168]{3,1,2,0:T(4,128)(2,1)} copy(bf16[4,4,3,7168]{3,0,2,1:T(4,128)(2,1)S(1)} %all_to_all.30) | data formatting | bytes 1376256 | tf_op jit(solution)/shard_map/all_to_all | solution.py:51
  17.3 4.9 %all-to-all-start.1 = ((bf16[4,4,3,7168]{3,1,2,0:T(4,128)(2,1)}), bf16[4,4,3,7168]{3,1,2,0:T(4,128)(2,1)S(1)}, u32[]{:S(2)}, u32[]{:S(2)}) async-start(bf16[4,4,3,7168]{3,1,2,0:T(4,128)(2,1)} %copy.54), calls=%async_computation.1 | async-start | bytes 1376256 | tf_op jit(solution)/shard_map/all_to_all | solution.py:59
  22.1 0.7 convert_element_type.39
  22.8 0.8 select_reduce_fusion
  23.6 0.1 mul.37
  23.7 0.1 copy.59
  23.8 0.1 copy.58
  23.9 0.1 copy.57
  24.1 0.6 select_convert_fusion
  24.7 15.6 %all-to-all-done.1 = bf16[4,4,3,7168]{3,1,2,0:T(4,128)(2,1)S(1)} async-done(((bf16[4,4,3,7168]{3,1,2,0:T(4,128)(2,1)}), bf16[4,4,3,7168]{3,1,2,0:T(4,128)(2,1)S(1)}, u32[]{:S(2)}, u32[]{:S(2)}) %all-to-all-start.1) | async-done | bytes 688160 | tf_op jit(solution)/shard_map/all_to_all | solution.py:59
  40.3 3.3 %all-to-all-start.3 = ((bf16[4,4,3,4]{3,0,2,1:T(4,128)(2,1)}), bf16[4,4,3,4]{3,0,2,1:T(4,128)(2,1)S(1)}, u32[]{:S(2)}, u32[]{:S(2)}) async-start(bf16[4,4,3,4]{3,0,2,1:T(4,128)(2,1)} %select_convert_fusion), calls=%async_computation.3 | async-start | bytes 24576 | tf_op jit(solution)/shard_map/all_to_all | solution.py:52
  43.5 0.5 copy.55
  44.0 0.6 reshape.37
  44.6 12.0 %fusion.4 = f32[48,2048]{1,0:T(8,128)S(1)} fusion(bf16[48,7168]{1,0:T(8,128)(2,1)S(1)} %reshape.37, bf16[1,1,7168,2048]{3,2,1,0:T(8,128)(2,1)} %param.11), kind=kOutput, calls=%fused_computation.4 | convolution fusion | flops 1409286144 | bytes 30441472 | tf_op jit(solution)/shard_map/dot_general | solution.py:11
  56.7 20.9 %fusion.6 = bf16[48,7168]{1,0:T(8,128)(2,1)S(1)} fusion(bf16[1,1,2048,7168]{3,2,1,0:T(8,128)(2,1)} %param.13, bf16[48,7168]{1,0:T(8,128)(2,1)S(1)} %reshape.37, bf16[1,1,7168,2048]{3,2,1,0:T(8,128)(2,1)} %param.12, f32[48,2048]{1,0:T(8,128)S(1)} %fusion.4), kind=kOutput, calls=%fused_computation.6 | convolution fusion | flops 2819506176 | bytes 60489728 | tf_op jit(solution)/shard_map/dot_general | solution.py:14
  77.6 0.4 reshape.38
  78.0 1.3 %copy.56 = bf16[4,4,3,7168]{3,1,2,0:T(4,128)(2,1)} copy(bf16[4,4,3,7168]{3,2,1,0:T(4,128)(2,1)S(1)} %reshape.38) | data formatting | bytes 1376256 | tf_op jit(solution)/shard_map/reshape | solution.py:17
  79.3 3.5 %all-to-all-start.2 = ((bf16[4,4,3,7168]{3,1,2,0:T(4,128)(2,1)}), bf16[4,4,3,7168]{3,1,2,0:T(4,128)(2,1)S(1)}, u32[]{:S(2)}, u32[]{:S(2)}) async-start(bf16[4,4,3,7168]{3,1,2,0:T(4,128)(2,1)} %copy.56), calls=%async_computation.2 | async-start | bytes 1376256 | tf_op jit(solution)/shard_map/all_to_all | solution.py:57
  82.8 0.8 copy.62
  83.6 18.1 %all-to-all-done.2 = bf16[4,4,3,7168]{3,1,2,0:T(4,128)(2,1)S(1)} async-done(((bf16[4,4,3,7168]{3,1,2,0:T(4,128)(2,1)}), bf16[4,4,3,7168]{3,1,2,0:T(4,128)(2,1)S(1)}, u32[]{:S(2)}, u32[]{:S(2)}) %all-to-all-start.2) | async-done | bytes 688160 | tf_op jit(solution)/shard_map/all_to_all | solution.py:57
  101.7 3.4 %all-to-all-start.4 = ((bf16[4,4,7168]{2,0,1:T(4,128)(2,1)}), bf16[4,4,7168]{2,0,1:T(4,128)(2,1)S(1)}, u32[]{:S(2)}, u32[]{:S(2)}) async-start(bf16[4,4,7168]{2,0,1:T(4,128)(2,1)} %copy.62), calls=%async_computation.4 | async-start | bytes 458752 | tf_op jit(solution)/shard_map/all_to_all | solution.py:53
  105.0 0.8 abs_reduce_fusion
  105.9 4.8 %all-to-all-done.4 = bf16[4,4,7168]{2,0,1:T(4,128)(2,1)S(1)} async-done(((bf16[4,4,7168]{2,0,1:T(4,128)(2,1)}), bf16[4,4,7168]{2,0,1:T(4,128)(2,1)S(1)}, u32[]{:S(2)}, u32[]{:S(2)}) %all-to-all-start.4) | async-done | bytes 229408 | tf_op jit(solution)/shard_map/all_to_all | solution.py:53
  110.7 0.2 add_convert_fusion
  110.9 8.1 %all_to_all.31 = bf16[4,4,7168]{2,0,1:T(4,128)(2,1)S(1)} all-to-all(bf16[4,4,7168]{2,0,1:T(4,128)(2,1)S(1)} %add_convert_fusion), channel_id=1, replica_groups=mesh['groups'=2,'row'=4,'col'=4] {'row'}, dimensions={1} | all-to-all | bytes 458752 | tf_op jit(solution)/shard_map/all_to_all | solution.py:78
  119.0 0.7 reduce_sum.39
  (9 shorter events, 0.0 us)
Async XLA Ops:
  0.0 1.1 copy-start
  17.3 23.0 %all-to-all-start.1 = ((bf16[4,4,3,7168]{3,1,2,0:T(4,128)(2,1)}), bf16[4,4,3,7168]{3,1,2,0:T(4,128)(2,1)S(1)}, u32[]{:S(2)}, u32[]{:S(2)}) async-start(bf16[4,4,3,7168]{3,1,2,0:T(4,128)(2,1)} %copy.54), calls=%async_computation.1 | async-start | bytes 1376256 | tf_op jit(solution)/shard_map/all_to_all | solution.py:59
  40.3 39.0 %all-to-all-start.3 = ((bf16[4,4,3,4]{3,0,2,1:T(4,128)(2,1)}), bf16[4,4,3,4]{3,0,2,1:T(4,128)(2,1)S(1)}, u32[]{:S(2)}, u32[]{:S(2)}) async-start(bf16[4,4,3,4]{3,0,2,1:T(4,128)(2,1)} %select_convert_fusion), calls=%async_computation.3 | async-start | bytes 24576 | tf_op jit(solution)/shard_map/all_to_all | solution.py:52
  56.7 26.1 %copy-start.1 = (bf16[4,4,7168]{2,1,0:T(4,128)(2,1)S(1)}, bf16[4,4,7168]{2,1,0:T(4,128)(2,1)}, u32[]{:S(2)}) copy-start(bf16[4,4,7168]{2,1,0:T(4,128)(2,1)} %param.10) | copy-start | bytes 688132
  79.3 22.4 %all-to-all-start.2 = ((bf16[4,4,3,7168]{3,1,2,0:T(4,128)(2,1)}), bf16[4,4,3,7168]{3,1,2,0:T(4,128)(2,1)S(1)}, u32[]{:S(2)}, u32[]{:S(2)}) async-start(bf16[4,4,3,7168]{3,1,2,0:T(4,128)(2,1)} %copy.56), calls=%async_computation.2 | async-start | bytes 1376256 | tf_op jit(solution)/shard_map/all_to_all | solution.py:57
  101.7 9.0 %all-to-all-start.4 = ((bf16[4,4,7168]{2,0,1:T(4,128)(2,1)}), bf16[4,4,7168]{2,0,1:T(4,128)(2,1)S(1)}, u32[]{:S(2)}, u32[]{:S(2)}) async-start(bf16[4,4,7168]{2,0,1:T(4,128)(2,1)} %copy.62), calls=%async_computation.4 | async-start | bytes 458752 | tf_op jit(solution)/shard_map/all_to_all | solution.py:53
where the time goes:
time: 120 us
  waiting for transfers between devices  38.5 us (32%)
  matrix products  34.1 us (28%)
  blocking collectives  22.7 us (19%)
  starting transfers between devices  15 us (12%)
  local copies, waits for them, and re-layouts  5.61 us (5%)
  other arithmetic  3.81 us (3%)
    dot_general x1, matrix products, expert_apply(): jnp.dot(hidden, down_local, preferred_element_type=jnp.float32)  20.9 us
    all_to_all x1, waiting for transfers between devices, local(): lax.all_to_all(expert_apply(lax.all_to_all(fanned, 'col', split_axis=0, c...  18.1 us
    all_to_all x1, waiting for transfers between devices, local(): lax.all_to_all(fanned, 'col', split_axis=0, concat_axis=0, tiled=True)  15.6 us
    all_to_all x1, blocking collectives, local(): lax.all_to_all(outgoing, 'row', split_axis=1, concat_axis=1, tiled=True)  14.6 us
    dot_general x1, matrix products, expert_apply(): gate_pre = jnp.dot(flat, gate_local, preferred_element_type=jnp.float32)  12 us
    all_to_all x1, blocking collectives, local(): lax.all_to_all(rounded, 'row', split_axis=1, concat_axis=1, tiled=True)  8.06 us
    all_to_all x1, starting transfers between devices, local(): lax.all_to_all(fanned, 'col', split_axis=0, concat_axis=0, tiled=True)  4.87 us
    all_to_all x1, waiting for transfers between devices, local(): lax.all_to_all(dither, 'row', split_axis=1, concat_axis=1, tiled=True)  4.82 us
  transfers between devices with their start and end apart: 4, of which 3 were waited for; matrix products, arithmetic and copies ran while one was open for 33% of the time, Pallas kernels for 0%

commit v1 on v0

--- a/solution.py
+++ b/solution.py
@@ -1,9 +1,30 @@
+import functools
+
 import jax
 import jax.numpy as jnp
 from jax import lax
+from jax.experimental import pallas as pl
+from jax.experimental.pallas import tpu as pltpu
 from jax.sharding import PartitionSpec as P
 
 FF = 2048
+LANES = 128
+COLS = 256
+MIB = 2**20
+VMEM = pl.BlockSpec(memory_space=pltpu.VMEM)
+HBM = pl.BlockSpec(memory_space=pltpu.HBM)
+
+
+def params(mib):
+    return pltpu.CompilerParams(vmem_limit_bytes=int(mib * MIB))
+
+
+def cost(flops, moved):
+    return pl.CostEstimate(flops=flops, bytes_accessed=moved, transcendentals=0)
+
+
+def flip(count, bit):
+    return [(i, i ^ bit) for i in range(count)]
 
 
 def expert_apply(batch, gate_local, up_local, down_local):
@@ -17,7 +38,7 @@
     return partial_value.reshape(batch.shape)
 
 
-def local(tokens, expert_ids, route_weight, dither, gate_proj, up_proj, down_proj):
+def local_any(tokens, expert_ids, route_weight, dither, gate_proj, up_proj, down_proj):
     row_count = lax.axis_size("row")
     col_count = lax.axis_size("col")
     tok_count = tokens.shape[0]
@@ -26,9 +47,6 @@
     per_row = col_count // pieces
     slot_count = 3 * tok_count // 4
     expert_count = row_count * per_row
-    gate_local = gate_proj[0, 0]
-    up_local = up_proj[0, 0]
-    down_local = down_proj[0, 0]
     labels = lax.broadcasted_iota(jnp.int32, (1, 1, expert_count), 2)
     matches = expert_ids[:, :, None] == labels
     counted = jnp.sum(matches.astype(jnp.int32), axis=1)
@@ -57,9 +75,9 @@
     returned = lax.all_to_all(
         expert_apply(
             lax.all_to_all(fanned, "col", split_axis=0, concat_axis=0, tiled=True),
-            gate_local,
-            up_local,
-            down_local,
+            gate_proj[0, 0],
+            up_proj[0, 0],
+            down_proj[0, 0],
         ),
         "col",
         split_axis=0,
@@ -79,7 +97,337 @@
     return jnp.sum(collected.astype(jnp.float32), axis=1).astype(jnp.bfloat16)
 
 
+N = 4
+SLOTS = 3
+BLOCKS = N * N
+ROWS = BLOCKS * 4
+HELD = 14
+PACKED = N * SLOTS * N
+
+
+def pack_kernel(tok_ref, ids_ref, share_ref, out_ref):
+    width = tok_ref.shape[1]
+    out_ref[:, :width] = tok_ref[...]
+    tail = jnp.concatenate(
+        [
+            ids_ref[...].astype(jnp.float32),
+            share_ref[...].astype(jnp.float32),
+            jnp.zeros((4, LANES - 16), jnp.float32),
+        ],
+        axis=1,
+    )
+    out_ref[:, width:] = tail.astype(jnp.bfloat16)
+
+
+def stack_kernel(*refs):
+    out_ref = refs[-1]
+    parts = [r[...].astype(jnp.float32) for r in refs[:-1]]
+    out_ref[...] = jnp.concatenate(parts, axis=0).astype(jnp.bfloat16)
+
+
+def fill_kernel(first, last, fresh, *refs):
+    gate_ref, up_ref = refs[0], refs[1]
+    buf, sem = refs[-2], refs[-1]
+    copies = [block_copy(gate_ref, up_ref, buf, sem, i) for i in range(first, last)]
+    for c in copies:
+        c.start()
+    for c in copies:
+        c.wait()
+
+
+def block_copy(gate_ref, up_ref, buf, sem, i):
+    src = (gate_ref, up_ref)[i % 2]
+    return pltpu.make_async_copy(
+        src.at[:, pl.ds((i // 2) * COLS, COLS)], buf.at[i % HELD], sem.at[i]
+    )
+
+
+def down_copy(down_ref, buf, sem, b):
+    deep = down_ref.shape[0]
+    return pltpu.make_async_copy(
+        down_ref.at[:, pl.ds(b * COLS, COLS)],
+        buf.at[2 + b // 3, pl.ds((b % 3) * deep, deep)],
+        sem.at[b],
+    )
+
+
+def down_block(buf, deep, b):
+    return buf[2 + b // 3, (b % 3) * deep : (b % 3 + 1) * deep, :]
+
+
+def routing(meta, me_row, me_col):
+    ids, share = meta[:, :8], meta[:, 8:16]
+    at = lax.broadcasted_iota(jnp.int32, (ROWS, ROWS), 0)
+    to = lax.broadcasted_iota(jnp.int32, (ROWS, ROWS), 1)
+    earlier = ((at // 4 == to // 4) & (to < at)).astype(jnp.bfloat16)
+    found, rank, weight = [], [], []
+    for k in range(N):
+        expert = (me_row * N + (me_col ^ k)).astype(jnp.float32)
+        hit = (ids == expert).astype(jnp.float32)
+        found.append(jnp.sum(hit, axis=1, keepdims=True))
+        weight.append(jnp.sum(hit * share, axis=1, keepdims=True))
+    lanes = jnp.concatenate(found + [jnp.zeros((ROWS, LANES - N), jnp.float32)], axis=1)
+    rank = jnp.dot(earlier, lanes.astype(jnp.bfloat16), preferred_element_type=jnp.float32)
+    return found, rank, weight
+
+
+def store_outs(value, outs, lo):
+    width = value.shape[1]
+    for k in range(N):
+        for s in range(SLOTS):
+            at = (k * SLOTS + s) * N
+            outs[k][s, :, lo : lo + width] = value[at : at + N].astype(jnp.bfloat16)
+
+
+def hidden_kernel(ready, blocks, *refs):
+    pieces = refs[:4]
+    gate_ref, up_ref, down_ref, _ = refs[4:8]
+    outs, hid_ref, mix_ref, buf = refs[8:12], refs[12], refs[13], refs[14]
+    x_ref, h_ref, fill_sem, down_sem = refs[15:]
+    width = x_ref.shape[1]
+    deep = down_ref.shape[0]
+    for i in range(ready, HELD):
+        block_copy(gate_ref, up_ref, buf, fill_sem, i).start()
+    for q in range(4):
+        x_ref[q * 16 : (q + 1) * 16, :] = pieces[q][:, :width]
+
+    def product(j):
+        at = lax.rem(2 * j, HELD)
+        g = jnp.dot(x_ref[...], buf[at], preferred_element_type=jnp.float32)
+        u = jnp.dot(x_ref[...], buf[at + 1], preferred_element_type=jnp.float32)
+        h_ref[:, pl.ds(pl.multiple_of(j * COLS, COLS), COLS)] = (
+            g / (1.0 + jnp.exp(-g)) * u
+        ).astype(jnp.bfloat16)
+
+    def step(j, carry):
+        for half in range(2):
+            i = 2 * j + half
+
+            @pl.when(i >= ready)
+            def _():
+                src = (gate_ref, up_ref)[half]
+                pltpu.make_async_copy(
+                    src.at[:, pl.ds(pl.multiple_of(j * COLS, COLS), COLS)],
+                    buf.at[lax.rem(i, HELD)],
+                    fill_sem.at[i],
+                ).wait()
+
+        product(j)
+
+        @pl.when(j == 0)
+        def _():
+            for i in range(HELD, 16):
+                block_copy(gate_ref, up_ref, buf, fill_sem, i).start()
+
+        for n in range(6):
+            b = 6 * (j - 1) + n
+
+            @pl.when((b >= 0) & (b < width // COLS))
+            def _():
+                pltpu.make_async_copy(
+                    down_ref.at[:, pl.ds(pl.multiple_of(b * COLS, COLS), COLS)],
+                    buf.at[2 * j + n // 3, pl.ds((n % 3) * deep, deep)],
+                    down_sem.at[b],
+                ).start()
+
+        return carry
+
+    lax.fori_loop(0, 8, step, 0)
+
+    meta = jnp.concatenate(
+        [pieces[q][:, width:].astype(jnp.float32) for q in range(4)], axis=0
+    )
+    found, rank, weight = routing(meta, lax.axis_index("row"), lax.axis_index("col"))
+    m_at = lax.broadcasted_iota(jnp.int32, (ROWS, PACKED), 0)
+    c_at = lax.broadcasted_iota(jnp.int32, (ROWS, PACKED), 1)
+    same = (m_at // 16 == c_at % 4) & ((m_at // 4) % 4 == c_at // 12)
+    slot = ((c_at // 4) % 3).astype(jnp.float32)
+    take = jnp.where(same & (found[0] > 0) & (rank[:, 0:1] == slot), 1.0, 0.0)
+    hid = lax.dot_general(
+        take.astype(jnp.bfloat16),
+        h_ref[...],
+        (((0,), (0,)), ((), ())),
+        preferred_element_type=jnp.float32,
+    )
+    hid_ref[...] = hid.astype(jnp.bfloat16)
+    mix = jnp.zeros((ROWS, PACKED), jnp.float32)
+    for k in range(N):
+        here = (c_at // 12 == k) & (m_at // 16 == c_at % 4)
+        mix = jnp.where(here & (found[k] > 0) & (rank[:, k : k + 1] == slot), weight[k], mix)
+    for q in range(N):
+        mix_ref[q * 4 : q * 4 + 4, :] = mix[q * 16 : q * 16 + 4]
+    for b in range(width // COLS):
+        down_copy(down_ref, buf, down_sem, b).wait()
+    for b in range(blocks):
+        value = jnp.dot(hid_ref[...], down_block(buf, deep, b), preferred_element_type=jnp.float32)
+        store_outs(value, outs, b * COLS)
+
+
+def down_kernel(first, last, deep, hid_ref, buf, *outs):
+    for b in range(first, last):
+        value = jnp.dot(hid_ref[...], down_block(buf, deep, b), preferred_element_type=jnp.float32)
+        store_outs(value, outs, (b - first) * COLS)
+
+
+def merge_kernel(mix_ref, *refs):
+    ins, outs = refs[:4], refs[4:]
+    got = jnp.concatenate(
+        [ins[k][s].astype(jnp.float32) for k in range(N) for s in range(SLOTS)], axis=0
+    ).astype(jnp.bfloat16)
+    value = jnp.dot(
+        mix_ref[...].astype(jnp.bfloat16), got, preferred_element_type=jnp.float32
+    )
+    for q in range(N):
+        outs[q][...] = value[q * 4 : q * 4 + 4].astype(jnp.bfloat16)
+
+
+def draw_kernel(dither_ref, out_ref):
+    draw = dither_ref[...].astype(jnp.float32)
+    at = lax.broadcasted_iota(jnp.int32, draw.shape, 1)
+    for q in range(N):
+        mine = jnp.where(at == (lax.axis_index("row") ^ q), draw, 0.0)
+        out_ref[q] = (jnp.sum(mine, axis=1) - 0.5).astype(out_ref.dtype)
+
+
+def final_kernel(chunks, draw_ref, *refs):
+    ins, out_ref = refs[:-1], refs[-1]
+    total = None
+    for q in range(N):
+        part = jnp.concatenate(
+            [ins[c * N + q][...].astype(jnp.float32) for c in range(chunks)], axis=1
+        )
+        spread = 0.125 * jnp.max(jnp.abs(part), axis=1, keepdims=True)
+        part = part + spread * draw_ref[q]
+        total = part if total is None else total + part
+    out_ref[...] = total.astype(jnp.bfloat16)
+
+
+def local_grid(tokens, expert_ids, route_weight, dither, gate_proj, up_proj, down_proj):
+    gate, up, down = gate_proj[0, 0], up_proj[0, 0], down_proj[0, 0]
+    width, wide = gate.shape
+    deep = down.shape[0]
+    bf = jnp.bfloat16
+    shape = jax.ShapeDtypeStruct
+    anyw = pl.BlockSpec(memory_space=pl.ANY)
+    pin = lambda a: pltpu.with_memory_space_constraint(a, pltpu.VMEM)
+
+    packed = pl.pallas_call(
+        pack_kernel,
+        out_shape=shape((4, width + LANES), bf),
+        in_specs=[VMEM] * 3,
+        out_specs=VMEM,
+        compiler_params=params(6),
+        name="pack",
+    )(tokens, expert_ids, route_weight)
+    near = [packed] + [lax.ppermute(packed, "col", flip(N, k)) for k in (1, 2, 3)]
+
+    buf_type = pltpu.VMEM((HELD, width, COLS), bf)
+    block_bytes = width * COLS * 2
+    split = (6, 13)
+    buf = pl.pallas_call(
+        functools.partial(fill_kernel, 0, split[0], True),
+        out_shape=buf_type,
+        in_specs=[HBM] * 2 + [anyw],
+        out_specs=VMEM,
+        scratch_shapes=[pltpu.SemaphoreType.DMA((16,))],
+        compiler_params=params(6),
+        cost_estimate=cost(0, split[0] * block_bytes),
+        name="fill_a",
+    )(gate, up, packed)
+    *near, buf = lax.optimization_barrier((*near, buf))
+    own = pl.pallas_call(
+        stack_kernel,
+        out_shape=shape((16, width + LANES), bf),
+        in_specs=[VMEM] * 4,
+        out_specs=VMEM,
+        compiler_params=params(6),
+        name="stack",
+    )(*near)
+    by_core = lax.ppermute(own, "row", flip(N, 1))
+    by_x = lax.ppermute(own, "row", flip(N, 2))
+    buf = pl.pallas_call(
+        functools.partial(fill_kernel, split[0], split[1], False),
+        out_shape=buf_type,
+        in_specs=[HBM] * 2 + [VMEM, anyw],
+        out_specs=VMEM,
+        scratch_shapes=[pltpu.SemaphoreType.DMA((16,))],
+        input_output_aliases={2: 0},
+        compiler_params=params(6),
+        cost_estimate=cost(0, (split[1] - split[0]) * block_bytes),
+        name="fill_b",
+    )(gate, up, pin(buf), own)
+    by_x, buf = lax.optimization_barrier((by_x, buf))
+    by_both = lax.ppermute(by_x, "row", flip(N, 1))
+
+    chunks = (14, 14)
+    outs = [shape((SLOTS, N, n * COLS), bf) for n in chunks]
+    first = pl.pallas_call(
+        functools.partial(hidden_kernel, split[1], chunks[0]),
+        out_shape=[outs[0]] * 4
+        + [shape((PACKED, wide), bf), shape((16, PACKED), jnp.float32), buf_type],
+        in_specs=[VMEM] * 4 + [HBM] * 3 + [VMEM],
+        out_specs=[VMEM] * 7,
+        scratch_shapes=[
+            pltpu.VMEM((ROWS, width), bf),
+            pltpu.VMEM((ROWS, wide), bf),
+            pltpu.SemaphoreType.DMA((16,)),
+            pltpu.SemaphoreType.DMA((width // COLS,)),
+        ],
+        input_output_aliases={7: 6},
+        compiler_params=params(6),
+        cost_estimate=cost(2 * ROWS * width * wide * 3, 40 * MIB),
+        name="hidden",
+    )(own, by_core, by_x, by_both, gate, up, down, pin(buf))
+    hid, mix, buf = first[4:]
+    parts = [first[:4]]
+    parts.append(
+        pl.pallas_call(
+            functools.partial(down_kernel, chunks[0], chunks[0] + chunks[1], deep),
+            out_shape=[outs[1]] * 4,
+            in_specs=[VMEM, VMEM],
+            out_specs=[VMEM] * 4,
+            compiler_params=params(6),
+            cost_estimate=cost(2 * ROWS * width * wide, 10 * MIB),
+            name="down",
+        )(hid, pin(buf))
+    )
+    draws = pl.pallas_call(
+        draw_kernel,
+        out_shape=shape((N, 4, width), jnp.float32),
+        in_specs=[VMEM],
+        out_specs=VMEM,
+        compiler_params=params(6),
+        name="draws",
+    )(dither)
+    finals = []
+    for c, part in enumerate(parts):
+        got = [part[0]] + [lax.ppermute(part[k], "col", flip(N, k)) for k in (1, 2, 3)]
+        value = pl.pallas_call(
+            merge_kernel,
+            out_shape=[shape((4, chunks[c] * COLS), bf)] * 4,
+            in_specs=[VMEM] * 5,
+            out_specs=[VMEM] * 4,
+            compiler_params=params(6),
+            name="merge",
+        )(mix, *got)
+        finals += [value[0]] + [lax.ppermute(value[q], "row", flip(N, q)) for q in (1, 2, 3)]
+    return pl.pallas_call(
+        functools.partial(final_kernel, len(chunks)),
+        out_shape=shape((4, width), bf),
+        in_specs=[VMEM] * (1 + len(finals)),
+        out_specs=VMEM,
+        compiler_params=params(6),
+        name="final",
+    )(draws, *finals)
+
+
 def solution(mesh):
+    def local(tokens, expert_ids, route_weight, dither, gate_proj, up_proj, down_proj):
+        grid = (mesh.shape["row"], mesh.shape["col"]) == (N, N)
+        whole_expert = gate_proj.shape[3] == FF and tokens.shape[0] == 4
+        pick = local_grid if grid and whole_expert else local_any
+        return pick(tokens, expert_ids, route_weight, dither, gate_proj, up_proj, down_proj)
+
     return jax.shard_map(
         local,
         mesh=mesh,

time: 120 us -> 76.7 us (0.64)
  Pallas kernels: 0 us -> 41.8 us
  matrix products: 34.1 us -> 0 us
  waiting for transfers between devices: 38.5 us -> 7.79 us
  blocking collectives: 22.7 us -> 0 us
  starting transfers between devices: 15 us -> 22 us
  other arithmetic: 3.81 us -> 0 us
    pallas_call x0 -> x10, Pallas kernels: none -> 41.8 us  [the longest x1 18.5 us: local_grid(): pl.pallas_call(functools.partial(hidden_kernel, split[1], chunks[0]), out...]
    all_to_all x4 -> x0, waiting for transfers between devices: 38.5 us -> none  [the longest x1 18.1 us: local(): lax.all_to_all(expert_apply(lax.all_to_all(fanned, 'col', split_axis=0, c...]
    dot_general x4 -> x0, matrix products: 34.1 us -> none  [the longest x1 20.9 us: expert_apply(): jnp.dot(hidden, down_local, preferred_element_type=jnp.float32)]
    all_to_all x2 -> x0, blocking collectives: 22.7 us -> none  [the longest x1 14.6 us: local(): lax.all_to_all(outgoing, 'row', split_axis=1, concat_axis=1, tiled=True)]
    ppermute x0 -> x18, starting transfers between devices: none -> 22 us  [the longest x6 9.84 us: local_grid(): lax.ppermute(part[k], 'col', flip(N, k))]
    all_to_all x4 -> x0, starting transfers between devices: 15 us -> none  [the longest x1 4.87 us: local(): lax.all_to_all(fanned, 'col', split_axis=0, concat_axis=0, tiled=True)]
    ppermute x0 -> x18, waiting for transfers between devices: none -> 7.79 us  [the longest x6 5.88 us: local_grid(): lax.ppermute(part[k], 'col', flip(N, k))]
    unnamed x5 -> x32, local copies, waits for them, and re-layouts: 0.82 us -> 4.63 us
  transfers between devices with their start and end apart: 4 -> 18, of which waited for: 3 -> 5; matrix products, arithmetic and copies ran while one was open for 33% -> 0% of each run, Pallas kernels for 0% -> 23%
where the time goes in v1:
time: 76.7 us; the launch traced here: 76.4 us
  Pallas kernels  41.8 us (54%)
  starting transfers between devices  22 us (29%)
  waiting for transfers between devices  7.79 us (10%)
  local copies, waits for them, and re-layouts  4.63 us (6%)
    pallas_call x1, Pallas kernels, local_grid(): pl.pallas_call(functools.partial(hidden_kernel, split[1], chunks[0]), out...  18.5 us
    ppermute x6, starting transfers between devices, local_grid(): lax.ppermute(part[k], 'col', flip(N, k))  9.84 us
    pallas_call x1, Pallas kernels, local_grid(): pl.pallas_call(functools.partial(fill_kernel, split[0], split[1], False),...  8.62 us
    pallas_call x1, Pallas kernels, local_grid(): pl.pallas_call(functools.partial(fill_kernel, 0, split[0], True), out_sha...  7.55 us
    ppermute x6, waiting for transfers between devices, local_grid(): lax.ppermute(part[k], 'col', flip(N, k))  5.88 us
    ppermute x3, starting transfers between devices, local_grid(): lax.ppermute(packed, 'col', flip(N, k))  5.63 us
    unnamed x32, local copies, waits for them, and re-layouts  4.63 us
    pallas_call x1, Pallas kernels, local_grid(): pl.pallas_call(functools.partial(down_kernel, chunks[0], chunks[0] + chun...  4.45 us
  transfers between devices with their start and end apart: 18, of which 5 were waited for; matrix products, arithmetic and copies ran while one was open for 0% of the time, Pallas kernels for 23%

profile of v1, /device:TPU:0, one launch (start us, length us, event | category | flops | bytes accessed | tf_op | source)
XLA Modules:
  0.0 76.4 jit_solution(5267503284517828902)
XLA Ops:
  0.0 0.8 %copy-done.6 = bf16[4,7168]{1,0:T(4,128)(2,1)S(1)} copy-done((bf16[4,7168]{1,0:T(4,128)(2,1)S(1)}, bf16[4,7168]{1,0:T(4,128)(2,1)}, u32[]{:S(2)}) %copy-start.6) | copy-done | bytes 57368
  0.8 0.7 copy-done.8
  1.5 0.7 copy-done.9
  2.3 3.0 %collective-permute-start = (bf16[4,7296]{1,0:T(4,128)(2,1)S(1)}, bf16[4,7296]{1,0:T(4,128)(2,1)S(1)}, u32[]{:S(2)}, u32[]{:S(2)}) collective-permute-start(bf16[4,7296]{1,0:T(4,128)(2,1)S(1)} %pack.1.refs_2_.refs_0_), channel_id=1, source_target_pairs={{0,1},{1,0},{2,3},{3,2},{4,5},{5,4},{6,7},{7,6},{8,9},{9,8},{10,11... | collective-permute-start | bytes 175112 | tf_op jit(solution)/shard_map/ppermute | solution.py:322
  5.3 2.6 %collective-permute-start.1 = (bf16[4,7296]{1,0:T(4,128)(2,1)S(1)}, bf16[4,7296]{1,0:T(4,128)(2,1)S(1)}, u32[]{:S(2)}, u32[]{:S(2)}) collective-permute-start(bf16[4,7296]{1,0:T(4,128)(2,1)S(1)} %pack.1.refs_2_.refs_0_), channel_id=1, source_target_pairs={{0,2},{1,3},{2,0},{3,1},{4,6},{5,7},{6,4},{7,5},{8,10},{9,11},{10,... | collective-permute-start | bytes 175112 | tf_op jit(solution)/shard_map/ppermute | solution.py:322
  7.9 7.6 %fill_a.1.refs_2_ = bf16[14,7168,256]{2,1,0:T(8,128)(2,1)S(1)} custom-call(bf16[7168,2048]{1,0:T(8,128)(2,1)} %bitcast.3, bf16[7168,2048]{1,0:T(8,128)(2,1)} %bitcast.6, bf16[4,7296]{1,0:T(4,128)(2,1)} %copy-done.1), custom_call_target="tpu_custom_call" | custom-call | bytes 22020096 | tf_op jit(solution)/shard_map/fill_a/pallas_call | solution.py:327
  15.5 0.8 %copy-done.2 = bf16[4,7296]{1,0:T(4,128)(2,1)S(1)} copy-done((bf16[4,7296]{1,0:T(4,128)(2,1)S(1)}, bf16[4,7296]{1,0:T(4,128)(2,1)}, u32[]{:S(2)}) %copy-start.2) | copy-done | bytes 58392
  16.4 1.8 %collective-permute-start.4 = (bf16[16,7296]{1,0:T(8,128)(2,1)S(1)}, bf16[16,7296]{1,0:T(8,128)(2,1)S(1)}, u32[]{:S(2)}, u32[]{:S(2)}) collective-permute-start(bf16[16,7296]{1,0:T(8,128)(2,1)S(1)} %stack.1.refs_3_.refs_0_), channel_id=1, source_target_pairs={{0,8},{4,12},{8,0},{12,4},{1,9},{5,13},{9,1},{13,5},{2,10},{6,14},... | collective-permute-start | bytes 700424 | tf_op jit(solution)/shard_map/ppermute | solution.py:347
  18.2 8.6 %fill_b.1.refs_7_ = bf16[14,7168,256]{2,1,0:T(8,128)(2,1)S(1)} custom-call(bf16[7168,2048]{1,0:T(8,128)(2,1)} %bitcast.4, bf16[7168,2048]{1,0:T(8,128)(2,1)} %bitcast.7, bf16[14,7168,256]{2,1,0:T(8,128)(2,1)S(1)} %fill_a.1.refs_2_, bf16[16,7296]{1,0:T(8,128)(2,1)} %copy-done), custom_call_target="tpu_custom_call", output_to_operand_aliasing={{}: (2, {})} | custom-call | bytes 25690112 | tf_op jit(solution)/shard_map/fill_b/pallas_call | solution.py:348
  26.8 0.6 collective-permute-start.5
  27.4 1.1 %collective-permute-done.5.refs_3_ = bf16[16,7296]{1,0:T(8,128)(2,1)S(1)} collective-permute-done((bf16[16,7296]{1,0:T(8,128)(2,1)S(1)}, bf16[16,7296]{1,0:T(8,128)(2,1)S(1)}, u32[]{:S(2)}, u32[]{:S(2)}) %collective-permute-start.5) | collective-permute-done | bytes 233504 | tf_op jit(solution)/shard_map/ppermute | solution.py:360
  28.5 0.7 copy-done.12
  29.2 18.5 %hidden.1 = (bf16[3,4,3584]{2,1,0:T(4,128)(2,1)}, bf16[3,4,3584]{2,1,0:T(4,128)(2,1)}, bf16[3,4,3584]{2,1,0:T(4,128)(2,1)}, bf16[3,4,3584]{2,1,0:T(4,128)(2,1)},...) custom-call(bf16[16,7296]{1,0:T(8,128)(2,1)} %copy-done, ...), custom_call_target="tpu_custom_call", output_to_operand_aliasing={{6}: (7, {})} | custom-call | flops 5637144576 | bytes 41943040 | tf_op jit(solution)/shard_map/hidden/pallas_call | solution.py:364
  47.8 4.5 %down.1 = (bf16[3,4,3584]{2,1,0:T(4,128)(2,1)}, bf16[3,4,3584]{2,1,0:T(4,128)(2,1)}, bf16[3,4,3584]{2,1,0:T(4,128)(2,1)}, bf16[3,4,3584]{2,1,0:T(4,128)(2,1)}) custom-call(bf16[48,2048]{1,0:T(8,128)(2,1)} %get-tuple-element.47.hid_ref, bf16[14,7168,256]{2,1,0:T(8,128)(2,1)S(1)} %get-tuple-element.48.buf), custom_call_target="tpu_custom_call" | custom-call | flops 1879048192 | bytes 10485760 | tf_op jit(solution)/shard_map/down/pallas_call | solution.py:384
  52.2 0.7 collective-permute-start.12
  52.9 3.5 %collective-permute-start.13 = (bf16[3,4,3584]{2,1,0:T(4,128)(2,1)}, bf16[3,4,3584]{2,1,0:T(4,128)(2,1)S(1)}, u32[]{:S(2)}, u32[]{:S(2)}) collective-permute-start(bf16[3,4,3584]{2,1,0:T(4,128)(2,1)} %get-tuple-element.51), channel_id=1, source_target_pairs={{0,2},{1,3},{2,0},{3,1},{4,6},{5,7},{6,4},{7,5},{8,10},{9,11},{10,... | collective-permute-start | bytes 258056 | tf_op jit(solution)/shard_map/ppermute | solution.py:404
  56.4 0.2 collective-permute-start.14
  56.6 0.3 collective-permute-start.6
  57.0 3.8 %collective-permute-start.7 = (bf16[3,4,3584]{2,1,0:T(4,128)(2,1)S(1)}, bf16[3,4,3584]{2,1,0:T(4,128)(2,1)S(1)}, u32[]{:S(2)}, u32[]{:S(2)}) collective-permute-start(bf16[3,4,3584]{2,1,0:T(4,128)(2,1)S(1)} %copy-done.14), channel_id=1, source_target_pairs={{0,2},{1,3},{2,0},{3,1},{4,6},{5,7},{6,4},{7,5},{8,10},{9,11},{10,... | collective-permute-start | bytes 258056 | tf_op jit(solution)/shard_map/ppermute | solution.py:404
  60.8 1.3 %collective-permute-start.8 = (bf16[3,4,3584]{2,1,0:T(4,128)(2,1)S(1)}, bf16[3,4,3584]{2,1,0:T(4,128)(2,1)S(1)}, u32[]{:S(2)}, u32[]{:S(2)}) collective-permute-start(bf16[3,4,3584]{2,1,0:T(4,128)(2,1)S(1)} %copy-done.13), channel_id=1, source_target_pairs={{0,3},{1,2},{2,1},{3,0},{4,7},{5,6},{6,5},{7,4},{8,11},{9,10},{10,... | collective-permute-start | bytes 258056 | tf_op jit(solution)/shard_map/ppermute | solution.py:404
  62.1 1.3 %collective-permute-done.13.refs_2_ = bf16[3,4,3584]{2,1,0:T(4,128)(2,1)S(1)} collective-permute-done((bf16[3,4,3584]{2,1,0:T(4,128)(2,1)}, bf16[3,4,3584]{2,1,0:T(4,128)(2,1)S(1)}, u32[]{:S(2)}, u32[]{:S(2)}) %collective-permute-start.13) | collective-permute-done | bytes 86048 | tf_op jit(solution)/shard_map/ppermute | solution.py:404
  63.4 0.4 collective-permute-done.14.refs_3_
  63.9 0.9 %copy-done.5 = bf16[3,4,3584]{2,1,0:T(4,128)(2,1)S(1)} copy-done((bf16[3,4,3584]{2,1,0:T(4,128)(2,1)S(1)}, bf16[3,4,3584]{2,1,0:T(4,128)(2,1)}, u32[]{:S(2)}) %copy-start.5) | copy-done | bytes 86040
  65.0 0.6 collective-permute-start.16
  65.6 1.3 %collective-permute-start.17 = (bf16[4,3584]{1,0:T(4,128)(2,1)S(1)}, bf16[4,3584]{1,0:T(4,128)(2,1)S(1)}, u32[]{:S(2)}, u32[]{:S(2)}) collective-permute-start(bf16[4,3584]{1,0:T(4,128)(2,1)S(1)} %get-tuple-element.56), channel_id=1, source_target_pairs={{0,12},{4,8},{8,4},{12,0},{1,13},{5,9},{9,5},{13,1},{2,14},{6,10},... | collective-permute-start | bytes 86024 | tf_op jit(solution)/shard_map/ppermute | solution.py:413
  66.9 4.1 %collective-permute-done.7.refs_2_ = bf16[3,4,3584]{2,1,0:T(4,128)(2,1)S(1)} collective-permute-done((bf16[3,4,3584]{2,1,0:T(4,128)(2,1)S(1)}, bf16[3,4,3584]{2,1,0:T(4,128)(2,1)S(1)}, u32[]{:S(2)}, u32[]{:S(2)}) %collective-permute-start.7) | collective-permute-done | bytes 86048 | tf_op jit(solution)/shard_map/ppermute | solution.py:404
  71.0 0.2 merge.2
  71.2 0.6 collective-permute-start.10
  71.8 1.6 %collective-permute-start.9 = (bf16[4,3584]{1,0:T(4,128)(2,1)S(1)}, bf16[4,3584]{1,0:T(4,128)(2,1)S(1)}, u32[]{:S(2)}, u32[]{:S(2)}) collective-permute-start(bf16[4,3584]{1,0:T(4,128)(2,1)S(1)} %get-tuple-element.44), channel_id=1, source_target_pairs={{0,4},{4,0},{8,12},{12,8},{1,5},{5,1},{9,13},{13,9},{2,6},{6,2},{1... | collective-permute-start | bytes 86024 | tf_op jit(solution)/shard_map/ppermute | solution.py:413
  73.4 1.2 %draws.1.draw_ref = f32[4,4,7168]{2,1,0:T(4,128)S(1)} custom-call(bf16[4,4,7168]{2,1,0:T(4,128)(2,1)S(1)} %copy-done.3), custom_call_target="tpu_custom_call" | custom-call | tf_op jit(solution)/shard_map/draws/pallas_call | solution.py:394
  74.6 0.8 %collective-permute-done.10.refs_2_ = bf16[4,3584]{1,0:T(4,128)(2,1)S(1)} collective-permute-done((bf16[4,3584]{1,0:T(4,128)(2,1)S(1)}, bf16[4,3584]{1,0:T(4,128)(2,1)S(1)}, u32[]{:S(2)}, u32[]{:S(2)}) %collective-permute-start.10) | collective-permute-done | bytes 28704 | tf_op jit(solution)/shard_map/ppermute | solution.py:413
  75.4 0.9 %final.1 = bf16[4,7168]{1,0:T(4,128)(2,1)} custom-call(f32[4,4,7168]{2,1,0:T(4,128)S(1)} %draws.1.draw_ref, bf16[4,3584]{1,0:T(4,128)(2,1)S(1)} %get-tuple-element.43.refs_0_, bf16[4,3584]{1,0:T(4,128)(2,1)S(1)} %collective-permute-done.9.refs_1_, bf16[4,3584]{1,0:T(4,128)(2,1)S(1)} %collective-permute-done.10.refs_2_, ...), custom_call_target="tpu_custom_call" | custom-call | tf_op jit(solution)/shard_map/final/pallas_call | solution.py:414
  (46 shorter events, 0.5 us)
Async XLA Ops:
  0.0 0.8 %copy-start.6 = (bf16[4,7168]{1,0:T(4,128)(2,1)S(1)}, bf16[4,7168]{1,0:T(4,128)(2,1)}, u32[]{:S(2)}) copy-start(bf16[4,7168]{1,0:T(4,128)(2,1)} %tok_ref.1) | copy-start | bytes 172036
  2.3 5.6 %copy-start.1 = (bf16[4,7296]{1,0:T(4,128)(2,1)}, bf16[4,7296]{1,0:T(4,128)(2,1)S(1)}, u32[]{:S(2)}) copy-start(bf16[4,7296]{1,0:T(4,128)(2,1)S(1)} %pack.1.refs_2_.refs_0_) | copy-start | bytes 175108
  2.3 13.2 %collective-permute-start = (bf16[4,7296]{1,0:T(4,128)(2,1)S(1)}, bf16[4,7296]{1,0:T(4,128)(2,1)S(1)}, u32[]{:S(2)}, u32[]{:S(2)}) collective-permute-start(bf16[4,7296]{1,0:T(4,128)(2,1)S(1)} %pack.1.refs_2_.refs_0_), channel_id=1, source_target_pairs={{0,1},{1,0},{2,3},{3,2},{4,5},{5,4},{6,7},{7,6},{8,9},{9,8},{10,11... | collective-permute-start | bytes 175112 | tf_op jit(solution)/shard_map/ppermute | solution.py:322
  5.3 10.2 %collective-permute-start.1 = (bf16[4,7296]{1,0:T(4,128)(2,1)S(1)}, bf16[4,7296]{1,0:T(4,128)(2,1)S(1)}, u32[]{:S(2)}, u32[]{:S(2)}) collective-permute-start(bf16[4,7296]{1,0:T(4,128)(2,1)S(1)} %pack.1.refs_2_.refs_0_), channel_id=1, source_target_pairs={{0,2},{1,3},{2,0},{3,1},{4,6},{5,7},{6,4},{7,5},{8,10},{9,11},{10,... | collective-permute-start | bytes 175112 | tf_op jit(solution)/shard_map/ppermute | solution.py:322
  7.9 7.6 %collective-permute-start.2 = (bf16[4,7296]{1,0:T(4,128)(2,1)S(1)}, bf16[4,7296]{1,0:T(4,128)(2,1)S(1)}, u32[]{:S(2)}, u32[]{:S(2)}) collective-permute-start(bf16[4,7296]{1,0:T(4,128)(2,1)S(1)} %pack.1.refs_2_.refs_0_), channel_id=1, source_target_pairs={{0,3},{1,2},{2,1},{3,0},{4,7},{5,6},{6,5},{7,4},{8,11},{9,10},{10,... | collective-permute-start | bytes 175112 | tf_op jit(solution)/shard_map/ppermute | solution.py:322
  15.5 0.8 %copy-start.2 = (bf16[4,7296]{1,0:T(4,128)(2,1)S(1)}, bf16[4,7296]{1,0:T(4,128)(2,1)}, u32[]{:S(2)}) copy-start(bf16[4,7296]{1,0:T(4,128)(2,1)} %copy-done.1) | copy-start | bytes 175108
  16.4 1.8 %copy-start = (bf16[16,7296]{1,0:T(8,128)(2,1)}, bf16[16,7296]{1,0:T(8,128)(2,1)S(1)}, u32[]{:S(2)}) copy-start(bf16[16,7296]{1,0:T(8,128)(2,1)S(1)} %stack.1.refs_3_.refs_0_) | copy-start | bytes 700420
  16.4 10.4 %collective-permute-start.4 = (bf16[16,7296]{1,0:T(8,128)(2,1)S(1)}, bf16[16,7296]{1,0:T(8,128)(2,1)S(1)}, u32[]{:S(2)}, u32[]{:S(2)}) collective-permute-start(bf16[16,7296]{1,0:T(8,128)(2,1)S(1)} %stack.1.refs_3_.refs_0_), channel_id=1, source_target_pairs={{0,8},{4,12},{8,0},{12,4},{1,9},{5,13},{9,1},{13,5},{2,10},{6,14},... | collective-permute-start | bytes 700424 | tf_op jit(solution)/shard_map/ppermute | solution.py:347
  18.1 9.2 %collective-permute-start.3 = (bf16[16,7296]{1,0:T(8,128)(2,1)S(1)}, bf16[16,7296]{1,0:T(8,128)(2,1)S(1)}, u32[]{:S(2)}, u32[]{:S(2)}) collective-permute-start(bf16[16,7296]{1,0:T(8,128)(2,1)S(1)} %stack.1.refs_3_.refs_0_), channel_id=1, source_target_pairs={{0,4},{4,0},{8,12},{12,8},{1,5},{5,1},{9,13},{13,9},{2,6},{6,2},{1... | collective-permute-start | bytes 700424 | tf_op jit(solution)/shard_map/ppermute | solution.py:346
  26.8 1.7 %copy-start.10 = (bf16[16,7296]{1,0:T(8,128)(2,1)}, bf16[16,7296]{1,0:T(8,128)(2,1)S(1)}, u32[]{:S(2)}) copy-start(bf16[16,7296]{1,0:T(8,128)(2,1)S(1)} %collective-permute-done.4.refs_2_) | copy-start | bytes 700420
  26.8 1.7 %collective-permute-start.5 = (bf16[16,7296]{1,0:T(8,128)(2,1)S(1)}, bf16[16,7296]{1,0:T(8,128)(2,1)S(1)}, u32[]{:S(2)}, u32[]{:S(2)}) collective-permute-start(bf16[16,7296]{1,0:T(8,128)(2,1)S(1)} %collective-permute-done.4.refs_2_), channel_id=1, source_target_pairs={{0,4},{4,0},{8,12},{12,8},{1,5},{5,1},{9,13},{13,9},{2,6},{6,2},{1... | collective-permute-start | bytes 700424 | tf_op jit(solution)/shard_map/ppermute | solution.py:360
  27.4 1.1 %copy-start.11 = (bf16[16,7296]{1,0:T(8,128)(2,1)}, bf16[16,7296]{1,0:T(8,128)(2,1)S(1)}, u32[]{:S(2)}) copy-start(bf16[16,7296]{1,0:T(8,128)(2,1)S(1)} %collective-permute-done.3.refs_1_) | copy-start | bytes 700420
  28.5 0.7 copy-start.12
  47.7 8.9 %copy-start.15 = (bf16[3,4,3584]{2,1,0:T(4,128)(2,1)S(1)}, bf16[3,4,3584]{2,1,0:T(4,128)(2,1)}, u32[]{:S(2)}) copy-start(bf16[3,4,3584]{2,1,0:T(4,128)(2,1)} %get-tuple-element.40) | copy-start | bytes 258052
  47.7 9.3 %copy-start.14 = (bf16[3,4,3584]{2,1,0:T(4,128)(2,1)S(1)}, bf16[3,4,3584]{2,1,0:T(4,128)(2,1)}, u32[]{:S(2)}) copy-start(bf16[3,4,3584]{2,1,0:T(4,128)(2,1)} %get-tuple-element.41) | copy-start | bytes 258052
  47.7 13.1 %copy-start.13 = (bf16[3,4,3584]{2,1,0:T(4,128)(2,1)S(1)}, bf16[3,4,3584]{2,1,0:T(4,128)(2,1)}, u32[]{:S(2)}) copy-start(bf16[3,4,3584]{2,1,0:T(4,128)(2,1)} %get-tuple-element.42) | copy-start | bytes 258052
  47.7 16.1 %copy-start.7 = (f32[16,48]{1,0:T(8,128)S(1)}, f32[16,48]{1,0:T(8,128)}, u32[]{:S(2)}) copy-start(f32[16,48]{1,0:T(8,128)} %get-tuple-element.38.mix_ref) | copy-start | bytes 9220
  47.8 23.2 %copy-start.4 = (bf16[3,4,3584]{2,1,0:T(4,128)(2,1)S(1)}, bf16[3,4,3584]{2,1,0:T(4,128)(2,1)}, u32[]{:S(2)}) copy-start(bf16[3,4,3584]{2,1,0:T(4,128)(2,1)} %get-tuple-element.39.refs_0_) | copy-start | bytes 258052
  47.8 25.7 %copy-start.3 = (bf16[4,4,7168]{2,1,0:T(4,128)(2,1)S(1)}, bf16[4,4,7168]{2,1,0:T(4,128)(2,1)}, u32[]{:S(2)}) copy-start(bf16[4,4,7168]{2,1,0:T(4,128)(2,1)} %dither_ref.1) | copy-start | bytes 688132
  52.2 8.6 %collective-permute-start.12 = (bf16[3,4,3584]{2,1,0:T(4,128)(2,1)}, bf16[3,4,3584]{2,1,0:T(4,128)(2,1)S(1)}, u32[]{:S(2)}, u32[]{:S(2)}) collective-permute-start(bf16[3,4,3584]{2,1,0:T(4,128)(2,1)} %get-tuple-element.50), channel_id=1, source_target_pairs={{0,1},{1,0},{2,3},{3,2},{4,5},{5,4},{6,7},{7,6},{8,9},{9,8},{10,11... | collective-permute-start | bytes 258056 | tf_op jit(solution)/shard_map/ppermute | solution.py:404
  52.9 10.5 %collective-permute-start.13 = (bf16[3,4,3584]{2,1,0:T(4,128)(2,1)}, bf16[3,4,3584]{2,1,0:T(4,128)(2,1)S(1)}, u32[]{:S(2)}, u32[]{:S(2)}) collective-permute-start(bf16[3,4,3584]{2,1,0:T(4,128)(2,1)} %get-tuple-element.51), channel_id=1, source_target_pairs={{0,2},{1,3},{2,0},{3,1},{4,6},{5,7},{6,4},{7,5},{8,10},{9,11},{10,... | collective-permute-start | bytes 258056 | tf_op jit(solution)/shard_map/ppermute | solution.py:404
  56.4 7.5 %collective-permute-start.14 = (bf16[3,4,3584]{2,1,0:T(4,128)(2,1)}, bf16[3,4,3584]{2,1,0:T(4,128)(2,1)S(1)}, u32[]{:S(2)}, u32[]{:S(2)}) collective-permute-start(bf16[3,4,3584]{2,1,0:T(4,128)(2,1)} %get-tuple-element.52), channel_id=1, source_target_pairs={{0,3},{1,2},{2,1},{3,0},{4,7},{5,6},{6,5},{7,4},{8,11},{9,10},{10,... | collective-permute-start | bytes 258056 | tf_op jit(solution)/shard_map/ppermute | solution.py:404
  56.6 9.0 %collective-permute-start.6 = (bf16[3,4,3584]{2,1,0:T(4,128)(2,1)S(1)}, bf16[3,4,3584]{2,1,0:T(4,128)(2,1)S(1)}, u32[]{:S(2)}, u32[]{:S(2)}) collective-permute-start(bf16[3,4,3584]{2,1,0:T(4,128)(2,1)S(1)} %copy-done.15), channel_id=1, source_target_pairs={{0,1},{1,0},{2,3},{3,2},{4,5},{5,4},{6,7},{7,6},{8,9},{9,8},{10,11... | collective-permute-start | bytes 258056 | tf_op jit(solution)/shard_map/ppermute | solution.py:404
  57.0 14.0 %collective-permute-start.7 = (bf16[3,4,3584]{2,1,0:T(4,128)(2,1)S(1)}, bf16[3,4,3584]{2,1,0:T(4,128)(2,1)S(1)}, u32[]{:S(2)}, u32[]{:S(2)}) collective-permute-start(bf16[3,4,3584]{2,1,0:T(4,128)(2,1)S(1)} %copy-done.14), channel_id=1, source_target_pairs={{0,2},{1,3},{2,0},{3,1},{4,6},{5,7},{6,4},{7,5},{8,10},{9,11},{10,... | collective-permute-start | bytes 258056 | tf_op jit(solution)/shard_map/ppermute | solution.py:404
  60.8 10.2 %collective-permute-start.8 = (bf16[3,4,3584]{2,1,0:T(4,128)(2,1)S(1)}, bf16[3,4,3584]{2,1,0:T(4,128)(2,1)S(1)}, u32[]{:S(2)}, u32[]{:S(2)}) collective-permute-start(bf16[3,4,3584]{2,1,0:T(4,128)(2,1)S(1)} %copy-done.13), channel_id=1, source_target_pairs={{0,3},{1,2},{2,1},{3,0},{4,7},{5,6},{6,5},{7,4},{8,11},{9,10},{10,... | collective-permute-start | bytes 258056 | tf_op jit(solution)/shard_map/ppermute | solution.py:404
  63.9 0.9 %copy-start.5 = (bf16[3,4,3584]{2,1,0:T(4,128)(2,1)S(1)}, bf16[3,4,3584]{2,1,0:T(4,128)(2,1)}, u32[]{:S(2)}) copy-start(bf16[3,4,3584]{2,1,0:T(4,128)(2,1)} %get-tuple-element.49.refs_0_) | copy-start | bytes 258052
  64.9 6.9 %collective-permute-start.15 = (bf16[4,3584]{1,0:T(4,128)(2,1)S(1)}, bf16[4,3584]{1,0:T(4,128)(2,1)S(1)}, u32[]{:S(2)}, u32[]{:S(2)}) collective-permute-start(bf16[4,3584]{1,0:T(4,128)(2,1)S(1)} %get-tuple-element.54), channel_id=1, source_target_pairs={{0,4},{4,0},{8,12},{12,8},{1,5},{5,1},{9,13},{13,9},{2,6},{6,2},{1... | collective-permute-start | bytes 86024 | tf_op jit(solution)/shard_map/ppermute | solution.py:413
  65.0 9.6 %collective-permute-start.16 = (bf16[4,3584]{1,0:T(4,128)(2,1)S(1)}, bf16[4,3584]{1,0:T(4,128)(2,1)S(1)}, u32[]{:S(2)}, u32[]{:S(2)}) collective-permute-start(bf16[4,3584]{1,0:T(4,128)(2,1)S(1)} %get-tuple-element.55), channel_id=1, source_target_pairs={{0,8},{4,12},{8,0},{12,4},{1,9},{5,13},{9,1},{13,5},{2,10},{6,14},... | collective-permute-start | bytes 86024 | tf_op jit(solution)/shard_map/ppermute | solution.py:413
  65.6 9.0 %collective-permute-start.17 = (bf16[4,3584]{1,0:T(4,128)(2,1)S(1)}, bf16[4,3584]{1,0:T(4,128)(2,1)S(1)}, u32[]{:S(2)}, u32[]{:S(2)}) collective-permute-start(bf16[4,3584]{1,0:T(4,128)(2,1)S(1)} %get-tuple-element.56), channel_id=1, source_target_pairs={{0,12},{4,8},{8,4},{12,0},{1,13},{5,9},{9,5},{13,1},{2,14},{6,10},... | collective-permute-start | bytes 86024 | tf_op jit(solution)/shard_map/ppermute | solution.py:413
  71.2 4.2 %collective-permute-start.10 = (bf16[4,3584]{1,0:T(4,128)(2,1)S(1)}, bf16[4,3584]{1,0:T(4,128)(2,1)S(1)}, u32[]{:S(2)}, u32[]{:S(2)}) collective-permute-start(bf16[4,3584]{1,0:T(4,128)(2,1)S(1)} %get-tuple-element.45), channel_id=1, source_target_pairs={{0,8},{4,12},{8,0},{12,4},{1,9},{5,13},{9,1},{13,5},{2,10},{6,14},... | collective-permute-start | bytes 86024 | tf_op jit(solution)/shard_map/ppermute | solution.py:413
  71.8 3.6 %collective-permute-start.11 = (bf16[4,3584]{1,0:T(4,128)(2,1)S(1)}, bf16[4,3584]{1,0:T(4,128)(2,1)S(1)}, u32[]{:S(2)}, u32[]{:S(2)}) collective-permute-start(bf16[4,3584]{1,0:T(4,128)(2,1)S(1)} %get-tuple-element.46), channel_id=1, source_target_pairs={{0,12},{4,8},{8,4},{12,0},{1,13},{5,9},{9,5},{13,1},{2,14},{6,10},... | collective-permute-start | bytes 86024 | tf_op jit(solution)/shard_map/ppermute | solution.py:413
  71.8 3.6 %collective-permute-start.9 = (bf16[4,3584]{1,0:T(4,128)(2,1)S(1)}, bf16[4,3584]{1,0:T(4,128)(2,1)S(1)}, u32[]{:S(2)}, u32[]{:S(2)}) collective-permute-start(bf16[4,3584]{1,0:T(4,128)(2,1)S(1)} %get-tuple-element.44), channel_id=1, source_target_pairs={{0,4},{4,0},{8,12},{12,8},{1,5},{5,1},{9,13},{13,9},{2,6},{6,2},{1... | collective-permute-start | bytes 86024 | tf_op jit(solution)/shard_map/ppermute | solution.py:413
  (2 other events, 1.4 us)

commit v2 on v1

--- a/solution.py
+++ b/solution.py
@@ -10,6 +10,7 @@
 FF = 2048
 LANES = 128
 COLS = 256
+PAIR = 2 * COLS
 MIB = 2**20
 VMEM = pl.BlockSpec(memory_space=pltpu.VMEM)
 HBM = pl.BlockSpec(memory_space=pltpu.HBM)
@@ -101,58 +102,42 @@
 SLOTS = 3
 BLOCKS = N * N
 ROWS = BLOCKS * 4
-HELD = 14
+HELD = 3
 PACKED = N * SLOTS * N
 
 
-def pack_kernel(tok_ref, ids_ref, share_ref, out_ref):
+def pack_kernel(tok_ref, ids_ref, share_ref, _, out_ref, ids_here, share_here, sem):
     width = tok_ref.shape[1]
-    out_ref[:, :width] = tok_ref[...]
-    tail = jnp.concatenate(
-        [
-            ids_ref[...].astype(jnp.float32),
-            share_ref[...].astype(jnp.float32),
-            jnp.zeros((4, LANES - 16), jnp.float32),
-        ],
-        axis=1,
-    )
-    out_ref[:, width:] = tail.astype(jnp.bfloat16)
-
-
-def stack_kernel(*refs):
-    out_ref = refs[-1]
-    parts = [r[...].astype(jnp.float32) for r in refs[:-1]]
-    out_ref[...] = jnp.concatenate(parts, axis=0).astype(jnp.bfloat16)
-
-
-def fill_kernel(first, last, fresh, *refs):
-    gate_ref, up_ref = refs[0], refs[1]
-    buf, sem = refs[-2], refs[-1]
-    copies = [block_copy(gate_ref, up_ref, buf, sem, i) for i in range(first, last)]
+    copies = [
+        pltpu.make_async_copy(ids_ref, ids_here, sem.at[0]),
+        pltpu.make_async_copy(share_ref, share_here, sem.at[1]),
+        pltpu.make_async_copy(tok_ref, out_ref.at[:, pl.ds(0, width)], sem.at[2]),
+    ]
     for c in copies:
         c.start()
     for c in copies:
         c.wait()
-
-
-def block_copy(gate_ref, up_ref, buf, sem, i):
-    src = (gate_ref, up_ref)[i % 2]
+    tail = jnp.concatenate(
+        [
+            ids_here[...].astype(jnp.float32),
+            share_here[...].astype(jnp.float32),
+            jnp.zeros((4, LANES - 16), jnp.float32),
+        ],
+        axis=1,
+    )
+    out_ref[:, width:] = tail.astype(jnp.bfloat16)
+
+
+def stack_kernel(*refs):
+    out_ref = refs[-1]
+    parts = [r[...].astype(jnp.float32) for r in refs[:4]]
+    out_ref[...] = jnp.concatenate(parts, axis=0).astype(jnp.bfloat16)
+
+
+def up_copy(up_ref, buf, sem, j):
     return pltpu.make_async_copy(
-        src.at[:, pl.ds((i // 2) * COLS, COLS)], buf.at[i % HELD], sem.at[i]
-    )
-
-
-def down_copy(down_ref, buf, sem, b):
-    deep = down_ref.shape[0]
-    return pltpu.make_async_copy(
-        down_ref.at[:, pl.ds(b * COLS, COLS)],
-        buf.at[2 + b // 3, pl.ds((b % 3) * deep, deep)],
-        sem.at[b],
-    )
-
-
-def down_block(buf, deep, b):
-    return buf[2 + b // 3, (b % 3) * deep : (b % 3 + 1) * deep, :]
+        up_ref.at[:, pl.ds(j * PAIR, PAIR)], buf.at[j % HELD], sem.at[j]
+    )
 
 
 def routing(meta, me_row, me_col):
@@ -179,64 +164,47 @@
             outs[k][s, :, lo : lo + width] = value[at : at + N].astype(jnp.bfloat16)
 
 
-def hidden_kernel(ready, blocks, *refs):
+def hidden_kernel(blocks, *refs):
     pieces = refs[:4]
-    gate_ref, up_ref, down_ref, _ = refs[4:8]
-    outs, hid_ref, mix_ref, buf = refs[8:12], refs[12], refs[13], refs[14]
-    x_ref, h_ref, fill_sem, down_sem = refs[15:]
-    width = x_ref.shape[1]
+    gate_ref, up_ref, down_ref = refs[4:7]
+    outs, hid_ref, mix_ref = refs[7:11], refs[11], refs[12]
+    x_ref, h_ref, buf, piece_sem, fill_sem, down_sem = refs[13:]
+    width = gate_ref.shape[0]
     deep = down_ref.shape[0]
-    for i in range(ready, HELD):
-        block_copy(gate_ref, up_ref, buf, fill_sem, i).start()
-    for q in range(4):
-        x_ref[q * 16 : (q + 1) * 16, :] = pieces[q][:, :width]
-
-    def product(j):
-        at = lax.rem(2 * j, HELD)
-        g = jnp.dot(x_ref[...], buf[at], preferred_element_type=jnp.float32)
-        u = jnp.dot(x_ref[...], buf[at + 1], preferred_element_type=jnp.float32)
-        h_ref[:, pl.ds(pl.multiple_of(j * COLS, COLS), COLS)] = (
-            g / (1.0 + jnp.exp(-g)) * u
-        ).astype(jnp.bfloat16)
-
-    def step(j, carry):
-        for half in range(2):
-            i = 2 * j + half
-
-            @pl.when(i >= ready)
-            def _():
-                src = (gate_ref, up_ref)[half]
-                pltpu.make_async_copy(
-                    src.at[:, pl.ds(pl.multiple_of(j * COLS, COLS), COLS)],
-                    buf.at[lax.rem(i, HELD)],
-                    fill_sem.at[i],
-                ).wait()
-
-        product(j)
-
-        @pl.when(j == 0)
-        def _():
-            for i in range(HELD, 16):
-                block_copy(gate_ref, up_ref, buf, fill_sem, i).start()
-
-        for n in range(6):
-            b = 6 * (j - 1) + n
-
-            @pl.when((b >= 0) & (b < width // COLS))
-            def _():
-                pltpu.make_async_copy(
-                    down_ref.at[:, pl.ds(pl.multiple_of(b * COLS, COLS), COLS)],
-                    buf.at[2 * j + n // 3, pl.ds((n % 3) * deep, deep)],
-                    down_sem.at[b],
-                ).start()
-
-        return carry
-
-    lax.fori_loop(0, 8, step, 0)
-
-    meta = jnp.concatenate(
-        [pieces[q][:, width:].astype(jnp.float32) for q in range(4)], axis=0
-    )
+    steps = deep // PAIR
+    bring = [
+        pltpu.make_async_copy(pieces[q], x_ref.at[pl.ds(q * 16, 16)], piece_sem.at[q])
+        for q in range(N)
+    ]
+    for c in bring:
+        c.start()
+    for j in range(HELD):
+        up_copy(up_ref, buf, fill_sem, j).start()
+    x_ref[ROWS:, :] = jnp.zeros((x_ref.shape[0] - ROWS, x_ref.shape[1]), x_ref.dtype)
+    for c in bring:
+        c.wait()
+
+    def down_place(b):
+        return buf.at[(1 + b // 3) % HELD, pl.ds(b % 3 * deep, deep)]
+
+    def down_copy(b):
+        return pltpu.make_async_copy(
+            down_ref.at[:, pl.ds(b * PAIR, PAIR)], down_place(b), down_sem.at[b]
+        )
+
+    for j in range(steps):
+        at = pl.ds(j * PAIR, PAIR)
+        g = jnp.dot(x_ref[:, :width], gate_ref[:, at], preferred_element_type=jnp.float32)[:ROWS]
+        up_copy(up_ref, buf, fill_sem, j).wait()
+        u = jnp.dot(x_ref[:, :width], buf[j % HELD], preferred_element_type=jnp.float32)[:ROWS]
+        h_ref[:, at] = (g / (1.0 + jnp.exp(-g)) * u).astype(jnp.bfloat16)
+        if j + HELD < steps:
+            up_copy(up_ref, buf, fill_sem, j + HELD).start()
+        if j > 0:
+            for b in range(3 * (j - 1), min(3 * j, blocks)):
+                down_copy(b).start()
+
+    meta = x_ref[:ROWS, width:].astype(jnp.float32)
     found, rank, weight = routing(meta, lax.axis_index("row"), lax.axis_index("col"))
     m_at = lax.broadcasted_iota(jnp.int32, (ROWS, PACKED), 0)
     c_at = lax.broadcasted_iota(jnp.int32, (ROWS, PACKED), 1)
@@ -256,21 +224,35 @@
         mix = jnp.where(here & (found[k] > 0) & (rank[:, k : k + 1] == slot), weight[k], mix)
     for q in range(N):
         mix_ref[q * 4 : q * 4 + 4, :] = mix[q * 16 : q * 16 + 4]
-    for b in range(width // COLS):
-        down_copy(down_ref, buf, down_sem, b).wait()
     for b in range(blocks):
-        value = jnp.dot(hid_ref[...], down_block(buf, deep, b), preferred_element_type=jnp.float32)
-        store_outs(value, outs, b * COLS)
-
-
-def down_kernel(first, last, deep, hid_ref, buf, *outs):
-    for b in range(first, last):
-        value = jnp.dot(hid_ref[...], down_block(buf, deep, b), preferred_element_type=jnp.float32)
-        store_outs(value, outs, (b - first) * COLS)
+        down_copy(b).wait()
+        value = jnp.dot(
+            hid_ref[...],
+            down_place(b)[...],
+            preferred_element_type=jnp.float32,
+        )
+        store_outs(value, outs, b * PAIR)
+
+
+def down_kernel(first, last, hid_from, down_ref, *refs):
+    outs, buf, hid_ref, sem, hid_sem = refs[:4], refs[4], refs[5], refs[6], refs[7]
+    bring = pltpu.make_async_copy(hid_from, hid_ref, hid_sem)
+    bring.start()
+    copies = [
+        pltpu.make_async_copy(down_ref.at[:, pl.ds(b * PAIR, PAIR)], buf.at[b - first], sem.at[b - first])
+        for b in range(first, last)
+    ]
+    for c in copies:
+        c.start()
+    bring.wait()
+    for i, c in enumerate(copies):
+        c.wait()
+        value = jnp.dot(hid_ref[...], buf[i], preferred_element_type=jnp.float32)
+        store_outs(value, outs, i * PAIR)
 
 
 def merge_kernel(mix_ref, *refs):
-    ins, outs = refs[:4], refs[4:]
+    ins, outs = refs[:4], refs[5:]
     got = jnp.concatenate(
         [ins[k][s].astype(jnp.float32) for k in range(N) for s in range(SLOTS)], axis=0
     ).astype(jnp.bfloat16)
@@ -281,7 +263,7 @@
         outs[q][...] = value[q * 4 : q * 4 + 4].astype(jnp.bfloat16)
 
 
-def draw_kernel(dither_ref, out_ref):
+def draw_kernel(dither_ref, _, out_ref):
     draw = dither_ref[...].astype(jnp.float32)
     at = lax.broadcasted_iota(jnp.int32, draw.shape, 1)
     for q in range(N):
@@ -314,102 +296,93 @@
     packed = pl.pallas_call(
         pack_kernel,
         out_shape=shape((4, width + LANES), bf),
-        in_specs=[VMEM] * 3,
+        in_specs=[HBM] * 4,
         out_specs=VMEM,
+        scratch_shapes=[
+            pltpu.VMEM((4, 8), jnp.int32),
+            pltpu.VMEM((4, 8), bf),
+            pltpu.SemaphoreType.DMA((3,)),
+        ],
         compiler_params=params(6),
         name="pack",
-    )(tokens, expert_ids, route_weight)
+    )(*(pltpu.with_memory_space_constraint(a, pltpu.HBM) for a in (tokens, expert_ids, route_weight, up)))
     near = [packed] + [lax.ppermute(packed, "col", flip(N, k)) for k in (1, 2, 3)]
 
-    buf_type = pltpu.VMEM((HELD, width, COLS), bf)
-    block_bytes = width * COLS * 2
-    split = (6, 13)
-    buf = pl.pallas_call(
-        functools.partial(fill_kernel, 0, split[0], True),
-        out_shape=buf_type,
-        in_specs=[HBM] * 2 + [anyw],
-        out_specs=VMEM,
-        scratch_shapes=[pltpu.SemaphoreType.DMA((16,))],
-        compiler_params=params(6),
-        cost_estimate=cost(0, split[0] * block_bytes),
-        name="fill_a",
-    )(gate, up, packed)
-    *near, buf = lax.optimization_barrier((*near, buf))
+    hbm = lambda a: pltpu.with_memory_space_constraint(a, pltpu.HBM)
     own = pl.pallas_call(
         stack_kernel,
         out_shape=shape((16, width + LANES), bf),
-        in_specs=[VMEM] * 4,
+        in_specs=[VMEM] * 4 + [HBM],
         out_specs=VMEM,
         compiler_params=params(6),
         name="stack",
-    )(*near)
+    )(*near, hbm(up))
     by_core = lax.ppermute(own, "row", flip(N, 1))
     by_x = lax.ppermute(own, "row", flip(N, 2))
-    buf = pl.pallas_call(
-        functools.partial(fill_kernel, split[0], split[1], False),
-        out_shape=buf_type,
-        in_specs=[HBM] * 2 + [VMEM, anyw],
-        out_specs=VMEM,
-        scratch_shapes=[pltpu.SemaphoreType.DMA((16,))],
-        input_output_aliases={2: 0},
-        compiler_params=params(6),
-        cost_estimate=cost(0, (split[1] - split[0]) * block_bytes),
-        name="fill_b",
-    )(gate, up, pin(buf), own)
-    by_x, buf = lax.optimization_barrier((by_x, buf))
     by_both = lax.ppermute(by_x, "row", flip(N, 1))
 
-    chunks = (14, 14)
-    outs = [shape((SLOTS, N, n * COLS), bf) for n in chunks]
+    chunks = (8, 6)
+    outs = [shape((SLOTS, N, n * PAIR), bf) for n in chunks]
     first = pl.pallas_call(
-        functools.partial(hidden_kernel, split[1], chunks[0]),
-        out_shape=[outs[0]] * 4
-        + [shape((PACKED, wide), bf), shape((16, PACKED), jnp.float32), buf_type],
-        in_specs=[VMEM] * 4 + [HBM] * 3 + [VMEM],
-        out_specs=[VMEM] * 7,
+        functools.partial(hidden_kernel, chunks[0]),
+        out_shape=[outs[0]] * 4 + [shape((PACKED, wide), bf), shape((16, PACKED), jnp.float32)],
+        in_specs=[anyw] * 4 + [VMEM] + [HBM] * 2,
+        out_specs=[VMEM] * 6,
         scratch_shapes=[
-            pltpu.VMEM((ROWS, width), bf),
+            pltpu.VMEM((2 * ROWS, width + LANES), bf),
             pltpu.VMEM((ROWS, wide), bf),
-            pltpu.SemaphoreType.DMA((16,)),
-            pltpu.SemaphoreType.DMA((width // COLS,)),
+            pltpu.VMEM((HELD, width, PAIR), bf),
+            pltpu.SemaphoreType.DMA((N,)),
+            pltpu.SemaphoreType.DMA((wide // PAIR,)),
+            pltpu.SemaphoreType.DMA((chunks[0],)),
         ],
-        input_output_aliases={7: 6},
-        compiler_params=params(6),
+        compiler_params=params(28),
         cost_estimate=cost(2 * ROWS * width * wide * 3, 40 * MIB),
         name="hidden",
-    )(own, by_core, by_x, by_both, gate, up, down, pin(buf))
-    hid, mix, buf = first[4:]
+    )(own, by_core, by_x, by_both, pin(gate), hbm(up), hbm(down))
+    hid, mix = first[4:6]
     parts = [first[:4]]
     parts.append(
         pl.pallas_call(
-            functools.partial(down_kernel, chunks[0], chunks[0] + chunks[1], deep),
+            functools.partial(down_kernel, chunks[0], chunks[0] + chunks[1]),
             out_shape=[outs[1]] * 4,
-            in_specs=[VMEM, VMEM],
+            in_specs=[anyw, HBM],
             out_specs=[VMEM] * 4,
-            compiler_params=params(6),
+            scratch_shapes=[
+                pltpu.VMEM((chunks[1], deep, PAIR), bf),
+                pltpu.VMEM((PACKED, wide), bf),
+                pltpu.SemaphoreType.DMA((chunks[1],)),
+                pltpu.SemaphoreType.DMA,
+            ],
+            compiler_params=params(28),
             cost_estimate=cost(2 * ROWS * width * wide, 10 * MIB),
             name="down",
-        )(hid, pin(buf))
-    )
-    draws = pl.pallas_call(
-        draw_kernel,
-        out_shape=shape((N, 4, width), jnp.float32),
-        in_specs=[VMEM],
-        out_specs=VMEM,
-        compiler_params=params(6),
-        name="draws",
-    )(dither)
+        )(hid, pltpu.with_memory_space_constraint(down, pltpu.HBM))
+    )
     finals = []
+    after = mix
     for c, part in enumerate(parts):
         got = [part[0]] + [lax.ppermute(part[k], "col", flip(N, k)) for k in (1, 2, 3)]
         value = pl.pallas_call(
             merge_kernel,
-            out_shape=[shape((4, chunks[c] * COLS), bf)] * 4,
-            in_specs=[VMEM] * 5,
+            out_shape=[shape((4, chunks[c] * PAIR), bf)] * 4,
+            in_specs=[VMEM] * 5 + [anyw],
             out_specs=[VMEM] * 4,
             compiler_params=params(6),
+            cost_estimate=cost(0, 8 * MIB),
             name="merge",
-        )(mix, *got)
+        )(mix, *got, after)
+        if c == 0:
+            draws = pl.pallas_call(
+                draw_kernel,
+                out_shape=shape((N, 4, width), jnp.float32),
+                in_specs=[VMEM, anyw],
+                out_specs=VMEM,
+                compiler_params=params(6),
+                cost_estimate=cost(0, 8 * MIB),
+                name="draws",
+            )(dither, value[0])
+            after = draws
         finals += [value[0]] + [lax.ppermute(value[q], "row", flip(N, q)) for q in (1, 2, 3)]
     return pl.pallas_call(
         functools.partial(final_kernel, len(chunks)),

time: 76.7 us -> 65.6 us (0.86)
  Pallas kernels: 41.8 us -> 26.2 us
  waiting for transfers between devices: 7.79 us -> 17 us
  local copies, waits for them, and re-layouts: 4.63 us -> 1.66 us
  starting transfers between devices: 22 us -> 20.4 us
    pallas_call x5 -> x3, Pallas kernels: 35.1 us -> 17.4 us  [the longest x1 17 us: local_grid(): pl.pallas_call(functools.partial(hidden_kernel, chunks[0]), out_shape=[ou...]
    ppermute x1, waiting for transfers between devices: 0.01 us -> 5.2 us  [local_grid(): by_x = lax.ppermute(own, 'row', flip(N, 2))]
    ppermute x3, waiting for transfers between devices: 0.01 us -> 4.45 us  [local_grid(): lax.ppermute(packed, 'col', flip(N, k))]
    unnamed x32 -> x30, local copies, waits for them, and re-layouts: 4.63 us -> 1.66 us
    ppermute x6, waiting for transfers between devices: 5.88 us -> 3.15 us  [local_grid(): lax.ppermute(part[k], 'col', flip(N, k))]
    ppermute x6, waiting for transfers between devices: 0.78 us -> 2.71 us  [local_grid(): lax.ppermute(value[q], 'row', flip(N, q))]
    pallas_call x1, Pallas kernels: 4.45 us -> 5.51 us  [local_grid(): pl.pallas_call(functools.partial(down_kernel, chunks[0], chunks[0] + chun...]
    pallas_call x1, Pallas kernels: 0.07 us -> 1.1 us  [local_grid(): pl.pallas_call(pack_kernel, out_shape=shape((4, width + LANES), bf), in_s...]
  transfers between devices with their start and end apart: 18 -> 18, of which waited for: 5 -> 8; matrix products, arithmetic and copies ran while one was open for 0% -> 0% of each run, Pallas kernels for 23% -> 11%
where the time goes in v2:
time: 65.6 us; the launch traced here: 65.5 us
  Pallas kernels  26.2 us (40%)
  starting transfers between devices  20.4 us (31%)
  waiting for transfers between devices  17 us (26%)
  local copies, waits for them, and re-layouts  1.66 us (3%)
    pallas_call x1, Pallas kernels, local_grid(): pl.pallas_call(functools.partial(hidden_kernel, chunks[0]), out_shape=[ou...  17 us
    ppermute x6, starting transfers between devices, local_grid(): lax.ppermute(part[k], 'col', flip(N, k))  8.9 us
    ppermute x3, starting transfers between devices, local_grid(): lax.ppermute(packed, 'col', flip(N, k))  5.77 us
    pallas_call x1, Pallas kernels, local_grid(): pl.pallas_call(functools.partial(down_kernel, chunks[0], chunks[0] + chun...  5.51 us
    ppermute x1, waiting for transfers between devices, local_grid(): by_x = lax.ppermute(own, 'row', flip(N, 2))  5.2 us
    ppermute x3, waiting for transfers between devices, local_grid(): lax.ppermute(packed, 'col', flip(N, k))  4.45 us
    ppermute x6, starting transfers between devices, local_grid(): lax.ppermute(value[q], 'row', flip(N, q))  4.06 us
    ppermute x6, waiting for transfers between devices, local_grid(): lax.ppermute(part[k], 'col', flip(N, k))  3.15 us
  transfers between devices with their start and end apart: 18, of which 8 were waited for; matrix products, arithmetic and copies ran while one was open for 0% of the time, Pallas kernels for 11%

profile of v2, /device:TPU:0, one launch (start us, length us, event | category | flops | bytes accessed | tf_op | source)
XLA Modules:
  0.0 65.5 jit_solution(8968627283543066361)
XLA Ops:
  0.0 1.1 %pack.1.refs_0_ = bf16[4,7296]{1,0:T(4,128)(2,1)S(1)} custom-call(bf16[4,7168]{1,0:T(4,128)(2,1)} %tok_ref.1, s32[4,8]{1,0:T(4,128)} %ids_ref.1, bf16[4,8]{1,0:T(4,128)(2,1)} %share_ref.1, bf16[7168,2048]{1,0:T(8,128)(2,1)} %bitcast.6), custom_call_target="tpu_custom_call" | custom-call | tf_op jit(solution)/shard_map/pack/pallas_call | solution.py:296
  1.1 5.1 %collective-permute-start.2 = (bf16[4,7296]{1,0:T(4,128)(2,1)S(1)}, bf16[4,7296]{1,0:T(4,128)(2,1)S(1)}, u32[]{:S(2)}, u32[]{:S(2)}) collective-permute-start(bf16[4,7296]{1,0:T(4,128)(2,1)S(1)} %pack.1.refs_0_), channel_id=1, source_target_pairs={{0,3},{1,2},{2,1},{3,0},{4,7},{5,6},{6,5},{7,4},{8,11},{9,10},{10,... | collective-permute-start | bytes 175112 | tf_op jit(solution)/shard_map/ppermute | solution.py:309
  6.3 0.6 collective-permute-start
  6.9 1.8 %collective-permute-done.2.refs_3_ = bf16[4,7296]{1,0:T(4,128)(2,1)S(1)} collective-permute-done((bf16[4,7296]{1,0:T(4,128)(2,1)S(1)}, bf16[4,7296]{1,0:T(4,128)(2,1)S(1)}, u32[]{:S(2)}, u32[]{:S(2)}) %collective-permute-start.2) | collective-permute-done | bytes 58400 | tf_op jit(solution)/shard_map/ppermute | solution.py:309
  8.7 2.7 %collective-permute-done.1.refs_2_ = bf16[4,7296]{1,0:T(4,128)(2,1)S(1)} collective-permute-done((bf16[4,7296]{1,0:T(4,128)(2,1)S(1)}, bf16[4,7296]{1,0:T(4,128)(2,1)S(1)}, u32[]{:S(2)}, u32[]{:S(2)}) %collective-permute-start.1) | collective-permute-done | bytes 58400 | tf_op jit(solution)/shard_map/ppermute | solution.py:309
  11.4 0.1 stack.1.refs_0_
  11.4 1.6 %collective-permute-start.4 = (bf16[16,7296]{1,0:T(8,128)(2,1)S(1)}, bf16[16,7296]{1,0:T(8,128)(2,1)S(1)}, u32[]{:S(2)}, u32[]{:S(2)}) collective-permute-start(bf16[16,7296]{1,0:T(8,128)(2,1)S(1)} %stack.1.refs_0_), channel_id=1, source_target_pairs={{0,8},{4,12},{8,0},{12,4},{1,9},{5,13},{9,1},{13,5},{2,10},{6,14},... | collective-permute-start | bytes 700424 | tf_op jit(solution)/shard_map/ppermute | solution.py:321
  13.1 5.2 %collective-permute-done.4.refs_2_ = bf16[16,7296]{1,0:T(8,128)(2,1)S(1)} collective-permute-done((bf16[16,7296]{1,0:T(8,128)(2,1)S(1)}, bf16[16,7296]{1,0:T(8,128)(2,1)S(1)}, u32[]{:S(2)}, u32[]{:S(2)}) %collective-permute-start.4) | collective-permute-done | bytes 233504 | tf_op jit(solution)/shard_map/ppermute | solution.py:321
  18.3 1.5 %collective-permute-done.5.refs_3_ = bf16[16,7296]{1,0:T(8,128)(2,1)S(1)} collective-permute-done((bf16[16,7296]{1,0:T(8,128)(2,1)S(1)}, bf16[16,7296]{1,0:T(8,128)(2,1)S(1)}, u32[]{:S(2)}, u32[]{:S(2)}) %collective-permute-start.5) | collective-permute-done | bytes 233504 | tf_op jit(solution)/shard_map/ppermute | solution.py:322
  19.8 0.7 %copy-done.7 = bf16[16,7296]{1,0:T(8,128)(2,1)} copy-done((bf16[16,7296]{1,0:T(8,128)(2,1)}, bf16[16,7296]{1,0:T(8,128)(2,1)S(1)}, u32[]{:S(2)}) %copy-start.7) | copy-done | bytes 233496
  20.5 17.0 %hidden.1 = (bf16[3,4,4096]{2,1,0:T(4,128)(2,1)}, bf16[3,4,4096]{2,1,0:T(4,128)(2,1)}, bf16[3,4,4096]{2,1,0:T(4,128)(2,1)}, bf16[3,4,4096]{2,1,0:T(4,128)(2,1)},...) custom-call(bf16[16,7296]{1,0:T(8,128)(2,1)} %copy-done, bf16[16,7296]{1,0:T(8,128)(2,1)} %copy-done.6, ...), custom_call_target="tpu_custom_call" | custom-call | flops 5637144576 | bytes 41943040 | tf_op jit(solution)/shard_map/hidden/pallas_call | solution.py:326
  37.6 0.7 %collective-permute-start.6 = (bf16[3,4,4096]{2,1,0:T(4,128)(2,1)}, bf16[3,4,4096]{2,1,0:T(4,128)(2,1)S(1)}, u32[]{:S(2)}, u32[]{:S(2)}) collective-permute-start(bf16[3,4,4096]{2,1,0:T(4,128)(2,1)} %get-tuple-element.25), channel_id=1, source_target_pairs={{0,1},{1,0},{2,3},{3,2},{4,5},{5,4},{6,7},{7,6},{8,9},{9,8},{10,11... | collective-permute-start | bytes 294920 | tf_op jit(solution)/shard_map/ppermute | solution.py:365
  38.3 2.1 %collective-permute-start.7 = (bf16[3,4,4096]{2,1,0:T(4,128)(2,1)}, bf16[3,4,4096]{2,1,0:T(4,128)(2,1)S(1)}, u32[]{:S(2)}, u32[]{:S(2)}) collective-permute-start(bf16[3,4,4096]{2,1,0:T(4,128)(2,1)} %get-tuple-element.26), channel_id=1, source_target_pairs={{0,2},{1,3},{2,0},{3,1},{4,6},{5,7},{6,4},{7,5},{8,10},{9,11},{10,... | collective-permute-start | bytes 294920 | tf_op jit(solution)/shard_map/ppermute | solution.py:365
  40.4 1.6 %collective-permute-start.8 = (bf16[3,4,4096]{2,1,0:T(4,128)(2,1)}, bf16[3,4,4096]{2,1,0:T(4,128)(2,1)S(1)}, u32[]{:S(2)}, u32[]{:S(2)}) collective-permute-start(bf16[3,4,4096]{2,1,0:T(4,128)(2,1)} %get-tuple-element.27), channel_id=1, source_target_pairs={{0,3},{1,2},{2,1},{3,0},{4,7},{5,6},{6,5},{7,4},{8,11},{9,10},{10,... | collective-permute-start | bytes 294920 | tf_op jit(solution)/shard_map/ppermute | solution.py:365
  42.0 0.9 %copy-done.2 = bf16[48,2048]{1,0:T(8,128)(2,1)S(1)} copy-done((bf16[48,2048]{1,0:T(8,128)(2,1)S(1)}, bf16[48,2048]{1,0:T(8,128)(2,1)}, u32[]{:S(2)}) %copy-start.2) | copy-done | bytes 196632
  42.9 5.5 %down.1 = (bf16[3,4,3072]{2,1,0:T(4,128)(2,1)S(1)}, bf16[3,4,3072]{2,1,0:T(4,128)(2,1)S(1)}, bf16[3,4,3072]{2,1,0:T(4,128)(2,1)S(1)}, bf16[3,4,3072]{2,1,0:T(4,128)(2,1)S(1)}) custom-call(bf16[48,2048]{1,0:T(8,128)(2,1)S(1)} %copy-done.2, bf16[2048,7168]{1,0:T(8,128)(2,1)} %bitcast.10), custom_call_target="tpu_custom_call" | custom-call | flops 1879048192 | bytes 10485760 | tf_op jit(solution)/shard_map/down/pallas_call | solution.py:346
  48.5 0.1 collective-permute-start.12
  48.5 2.7 %collective-permute-start.13 = (bf16[3,4,3072]{2,1,0:T(4,128)(2,1)S(1)}, bf16[3,4,3072]{2,1,0:T(4,128)(2,1)S(1)}, u32[]{:S(2)}, u32[]{:S(2)}) collective-permute-start(bf16[3,4,3072]{2,1,0:T(4,128)(2,1)S(1)} %get-tuple-element.35), channel_id=1, source_target_pairs={{0,2},{1,3},{2,0},{3,1},{4,6},{5,7},{6,4},{7,5},{8,10},{9,11},{10,... | collective-permute-start | bytes 221192 | tf_op jit(solution)/shard_map/ppermute | solution.py:365
  51.3 1.7 %collective-permute-start.14 = (bf16[3,4,3072]{2,1,0:T(4,128)(2,1)S(1)}, bf16[3,4,3072]{2,1,0:T(4,128)(2,1)S(1)}, u32[]{:S(2)}, u32[]{:S(2)}) collective-permute-start(bf16[3,4,3072]{2,1,0:T(4,128)(2,1)S(1)} %get-tuple-element.36), channel_id=1, source_target_pairs={{0,3},{1,2},{2,1},{3,0},{4,7},{5,6},{6,5},{7,4},{8,11},{9,10},{10,... | collective-permute-start | bytes 221192 | tf_op jit(solution)/shard_map/ppermute | solution.py:365
  52.9 0.2 merge.2
  53.2 1.2 %draws.1.refs_4_.draw_ref = f32[4,4,7168]{2,1,0:T(4,128)S(1)} custom-call(bf16[4,4,7168]{2,1,0:T(4,128)(2,1)S(1)} %copy-done.1, bf16[4,4096]{1,0:T(4,128)(2,1)S(1)} %get-tuple-element.28._.refs_0_), custom_call_target="tpu_custom_call" | custom-call | bytes 8388608 | tf_op jit(solution)/shard_map/draws/pallas_call | solution.py:376
  54.4 1.9 %collective-permute-done.13.refs_2_ = bf16[3,4,3072]{2,1,0:T(4,128)(2,1)S(1)} collective-permute-done((bf16[3,4,3072]{2,1,0:T(4,128)(2,1)S(1)}, bf16[3,4,3072]{2,1,0:T(4,128)(2,1)S(1)}, u32[]{:S(2)}, u32[]{:S(2)}) %collective-permute-start.13) | collective-permute-done | bytes 73760 | tf_op jit(solution)/shard_map/ppermute | solution.py:365
  56.3 1.2 %collective-permute-done.14.refs_3_ = bf16[3,4,3072]{2,1,0:T(4,128)(2,1)S(1)} collective-permute-done((bf16[3,4,3072]{2,1,0:T(4,128)(2,1)S(1)}, bf16[3,4,3072]{2,1,0:T(4,128)(2,1)S(1)}, u32[]{:S(2)}, u32[]{:S(2)}) %collective-permute-start.14) | collective-permute-done | bytes 73760 | tf_op jit(solution)/shard_map/ppermute | solution.py:365
  57.5 0.2 merge.3
  57.7 0.1 collective-permute-start.15
  57.8 0.5 collective-permute-start.9
  58.3 1.5 %collective-permute-start.10 = (bf16[4,4096]{1,0:T(4,128)(2,1)S(1)}, bf16[4,4096]{1,0:T(4,128)(2,1)S(1)}, u32[]{:S(2)}, u32[]{:S(2)}) collective-permute-start(bf16[4,4096]{1,0:T(4,128)(2,1)S(1)} %get-tuple-element.30), channel_id=1, source_target_pairs={{0,8},{4,12},{8,0},{12,4},{1,9},{5,13},{9,1},{13,5},{2,10},{6,14},... | collective-permute-start | bytes 98312 | tf_op jit(solution)/shard_map/ppermute | solution.py:386
  59.8 1.4 %collective-permute-start.16 = (bf16[4,3072]{1,0:T(4,128)(2,1)S(1)}, bf16[4,3072]{1,0:T(4,128)(2,1)S(1)}, u32[]{:S(2)}, u32[]{:S(2)}) collective-permute-start(bf16[4,3072]{1,0:T(4,128)(2,1)S(1)} %get-tuple-element.39), channel_id=1, source_target_pairs={{0,8},{4,12},{8,0},{12,4},{1,9},{5,13},{9,1},{13,5},{2,10},{6,14},... | collective-permute-start | bytes 73736 | tf_op jit(solution)/shard_map/ppermute | solution.py:386
  61.2 0.6 collective-permute-start.17
  61.8 2.2 %collective-permute-done.16.refs_6_ = bf16[4,3072]{1,0:T(4,128)(2,1)S(1)} collective-permute-done((bf16[4,3072]{1,0:T(4,128)(2,1)S(1)}, bf16[4,3072]{1,0:T(4,128)(2,1)S(1)}, u32[]{:S(2)}, u32[]{:S(2)}) %collective-permute-start.16) | collective-permute-done | bytes 24608 | tf_op jit(solution)/shard_map/ppermute | solution.py:386
  64.0 0.5 collective-permute-done.17.refs_7_
  64.5 1.0 %final.1 = bf16[4,7168]{1,0:T(4,128)(2,1)} custom-call(f32[4,4,7168]{2,1,0:T(4,128)S(1)} %draws.1.refs_4_.draw_ref, bf16[4,4096]{1,0:T(4,128)(2,1)S(1)} %get-tuple-element.28._.refs_0_, bf16[4,4096]{1,0:T(4,128)(2,1)S(1)} %collective-permute-done.9.refs_1_, bf16[4,4096]{1,0:T(4,128)(2,1)S(1)} %collective-permute-done.10.refs_2_, ...), custom_call_target="tpu_custom_call" | custom-call | tf_op jit(solution)/shard_map/final/pallas_call | solution.py:387
  (43 shorter events, 0.1 us)
Async XLA Ops:
  0.0 20.5 %slice-start = ((s8[29360128]{0:T(1024)(128)(4,1)}), s8[4194304]{0:T(1024)(128)(4,1)S(1)}, s32[]{:S(2)}) async-start(s8[29360128]{0:T(1024)(128)(4,1)} %bitcast.3), calls=%async_computation | async-start | bytes 8388608
  0.0 20.5 %slice-start.1 = ((s8[29360128]{0:T(1024)(128)(4,1)}), s8[4194304]{0:T(1024)(128)(4,1)S(1)}, s32[]{:S(2)}) async-start(s8[29360128]{0:T(1024)(128)(4,1)} %bitcast.3), calls=%async_computation.1 | async-start | bytes 8388608
  0.0 20.5 %slice-start.2 = ((s8[29360128]{0:T(1024)(128)(4,1)}), s8[4194304]{0:T(1024)(128)(4,1)S(1)}, s32[]{:S(2)}) async-start(s8[29360128]{0:T(1024)(128)(4,1)} %bitcast.3), calls=%async_computation.2 | async-start | bytes 8388608
  0.0 20.5 %slice-start.3 = ((s8[29360128]{0:T(1024)(128)(4,1)}), s8[4194304]{0:T(1024)(128)(4,1)S(1)}, s32[]{:S(2)}) async-start(s8[29360128]{0:T(1024)(128)(4,1)} %bitcast.3), calls=%async_computation.3 | async-start | bytes 8388608
  1.1 19.4 %slice-start.4 = ((s8[29360128]{0:T(1024)(128)(4,1)}), s8[4194304]{0:T(1024)(128)(4,1)S(1)}, s32[]{:S(2)}) async-start(s8[29360128]{0:T(1024)(128)(4,1)} %bitcast.3), calls=%async_computation.4 | async-start | bytes 8388608
  1.1 19.4 %slice-start.5 = ((s8[29360128]{0:T(1024)(128)(4,1)}), s8[4194304]{0:T(1024)(128)(4,1)S(1)}, s32[]{:S(2)}) async-start(s8[29360128]{0:T(1024)(128)(4,1)} %bitcast.3), calls=%async_computation.5 | async-start | bytes 8388608
  1.1 19.4 %slice-start.6 = ((s8[29360128]{0:T(1024)(128)(4,1)}), s8[4194304]{0:T(1024)(128)(4,1)S(1)}, s32[]{:S(2)}) async-start(s8[29360128]{0:T(1024)(128)(4,1)} %bitcast.3), calls=%async_computation.6 | async-start | bytes 8388608
  1.1 7.6 %collective-permute-start.2 = (bf16[4,7296]{1,0:T(4,128)(2,1)S(1)}, bf16[4,7296]{1,0:T(4,128)(2,1)S(1)}, u32[]{:S(2)}, u32[]{:S(2)}) collective-permute-start(bf16[4,7296]{1,0:T(4,128)(2,1)S(1)} %pack.1.refs_0_), channel_id=1, source_target_pairs={{0,3},{1,2},{2,1},{3,0},{4,7},{5,6},{6,5},{7,4},{8,11},{9,10},{10,... | collective-permute-start | bytes 175112 | tf_op jit(solution)/shard_map/ppermute | solution.py:309
  6.3 5.1 %collective-permute-start.1 = (bf16[4,7296]{1,0:T(4,128)(2,1)S(1)}, bf16[4,7296]{1,0:T(4,128)(2,1)S(1)}, u32[]{:S(2)}, u32[]{:S(2)}) collective-permute-start(bf16[4,7296]{1,0:T(4,128)(2,1)S(1)} %pack.1.refs_0_), channel_id=1, source_target_pairs={{0,2},{1,3},{2,0},{3,1},{4,6},{5,7},{6,4},{7,5},{8,10},{9,11},{10,... | collective-permute-start | bytes 175112 | tf_op jit(solution)/shard_map/ppermute | solution.py:309
  6.3 5.1 %collective-permute-start = (bf16[4,7296]{1,0:T(4,128)(2,1)S(1)}, bf16[4,7296]{1,0:T(4,128)(2,1)S(1)}, u32[]{:S(2)}, u32[]{:S(2)}) collective-permute-start(bf16[4,7296]{1,0:T(4,128)(2,1)S(1)} %pack.1.refs_0_), channel_id=1, source_target_pairs={{0,1},{1,0},{2,3},{3,2},{4,5},{5,4},{6,7},{7,6},{8,9},{9,8},{10,11... | collective-permute-start | bytes 175112 | tf_op jit(solution)/shard_map/ppermute | solution.py:309
  11.4 8.4 %copy-start = (bf16[16,7296]{1,0:T(8,128)(2,1)}, bf16[16,7296]{1,0:T(8,128)(2,1)S(1)}, u32[]{:S(2)}) copy-start(bf16[16,7296]{1,0:T(8,128)(2,1)S(1)} %stack.1.refs_0_) | copy-start | bytes 700420
  11.4 6.8 %collective-permute-start.4 = (bf16[16,7296]{1,0:T(8,128)(2,1)S(1)}, bf16[16,7296]{1,0:T(8,128)(2,1)S(1)}, u32[]{:S(2)}, u32[]{:S(2)}) collective-permute-start(bf16[16,7296]{1,0:T(8,128)(2,1)S(1)} %stack.1.refs_0_), channel_id=1, source_target_pairs={{0,8},{4,12},{8,0},{12,4},{1,9},{5,13},{9,1},{13,5},{2,10},{6,14},... | collective-permute-start | bytes 700424 | tf_op jit(solution)/shard_map/ppermute | solution.py:321
  13.1 5.2 %collective-permute-start.3 = (bf16[16,7296]{1,0:T(8,128)(2,1)S(1)}, bf16[16,7296]{1,0:T(8,128)(2,1)S(1)}, u32[]{:S(2)}, u32[]{:S(2)}) collective-permute-start(bf16[16,7296]{1,0:T(8,128)(2,1)S(1)} %stack.1.refs_0_), channel_id=1, source_target_pairs={{0,4},{4,0},{8,12},{12,8},{1,5},{5,1},{9,13},{13,9},{2,6},{6,2},{1... | collective-permute-start | bytes 700424 | tf_op jit(solution)/shard_map/ppermute | solution.py:320
  18.3 1.5 %copy-start.5 = (bf16[16,7296]{1,0:T(8,128)(2,1)}, bf16[16,7296]{1,0:T(8,128)(2,1)S(1)}, u32[]{:S(2)}) copy-start(bf16[16,7296]{1,0:T(8,128)(2,1)S(1)} %collective-permute-done.4.refs_2_) | copy-start | bytes 700420
  18.3 1.5 %collective-permute-start.5 = (bf16[16,7296]{1,0:T(8,128)(2,1)S(1)}, bf16[16,7296]{1,0:T(8,128)(2,1)S(1)}, u32[]{:S(2)}, u32[]{:S(2)}) collective-permute-start(bf16[16,7296]{1,0:T(8,128)(2,1)S(1)} %collective-permute-done.4.refs_2_), channel_id=1, source_target_pairs={{0,4},{4,0},{8,12},{12,8},{1,5},{5,1},{9,13},{13,9},{2,6},{6,2},{1... | collective-permute-start | bytes 700424 | tf_op jit(solution)/shard_map/ppermute | solution.py:322
  18.3 1.5 %copy-start.6 = (bf16[16,7296]{1,0:T(8,128)(2,1)}, bf16[16,7296]{1,0:T(8,128)(2,1)S(1)}, u32[]{:S(2)}) copy-start(bf16[16,7296]{1,0:T(8,128)(2,1)S(1)} %collective-permute-done.3.refs_1_) | copy-start | bytes 700420
  37.5 15.6 %copy-start.1 = (bf16[4,4,7168]{2,1,0:T(4,128)(2,1)S(1)}, bf16[4,4,7168]{2,1,0:T(4,128)(2,1)}, u32[]{:S(2)}) copy-start(bf16[4,4,7168]{2,1,0:T(4,128)(2,1)} %dither_ref.1) | copy-start | bytes 688132
  37.6 13.7 %collective-permute-start.6 = (bf16[3,4,4096]{2,1,0:T(4,128)(2,1)}, bf16[3,4,4096]{2,1,0:T(4,128)(2,1)S(1)}, u32[]{:S(2)}, u32[]{:S(2)}) collective-permute-start(bf16[3,4,4096]{2,1,0:T(4,128)(2,1)} %get-tuple-element.25), channel_id=1, source_target_pairs={{0,1},{1,0},{2,3},{3,2},{4,5},{5,4},{6,7},{7,6},{8,9},{9,8},{10,11... | collective-permute-start | bytes 294920 | tf_op jit(solution)/shard_map/ppermute | solution.py:365
  38.3 14.7 %collective-permute-start.7 = (bf16[3,4,4096]{2,1,0:T(4,128)(2,1)}, bf16[3,4,4096]{2,1,0:T(4,128)(2,1)S(1)}, u32[]{:S(2)}, u32[]{:S(2)}) collective-permute-start(bf16[3,4,4096]{2,1,0:T(4,128)(2,1)} %get-tuple-element.26), channel_id=1, source_target_pairs={{0,2},{1,3},{2,0},{3,1},{4,6},{5,7},{6,4},{7,5},{8,10},{9,11},{10,... | collective-permute-start | bytes 294920 | tf_op jit(solution)/shard_map/ppermute | solution.py:365
  40.4 12.6 %collective-permute-start.8 = (bf16[3,4,4096]{2,1,0:T(4,128)(2,1)}, bf16[3,4,4096]{2,1,0:T(4,128)(2,1)S(1)}, u32[]{:S(2)}, u32[]{:S(2)}) collective-permute-start(bf16[3,4,4096]{2,1,0:T(4,128)(2,1)} %get-tuple-element.27), channel_id=1, source_target_pairs={{0,3},{1,2},{2,1},{3,0},{4,7},{5,6},{6,5},{7,4},{8,11},{9,10},{10,... | collective-permute-start | bytes 294920 | tf_op jit(solution)/shard_map/ppermute | solution.py:365
  42.0 0.9 %copy-start.2 = (bf16[48,2048]{1,0:T(8,128)(2,1)S(1)}, bf16[48,2048]{1,0:T(8,128)(2,1)}, u32[]{:S(2)}) copy-start(bf16[48,2048]{1,0:T(8,128)(2,1)} %get-tuple-element.32.hid_from) | copy-start | bytes 589828
  42.9 10.0 %copy-start.3 = (bf16[3,4,4096]{2,1,0:T(4,128)(2,1)S(1)}, bf16[3,4,4096]{2,1,0:T(4,128)(2,1)}, u32[]{:S(2)}) copy-start(bf16[3,4,4096]{2,1,0:T(4,128)(2,1)} %get-tuple-element.24.refs_0_) | copy-start | bytes 294916
  42.9 10.0 %copy-start.4 = (f32[16,48]{1,0:T(8,128)S(1)}, f32[16,48]{1,0:T(8,128)}, u32[]{:S(2)}) copy-start(f32[16,48]{1,0:T(8,128)} %get-tuple-element.23.mix_ref.refs_4_) | copy-start | bytes 9220
  48.5 5.9 %collective-permute-start.12 = (bf16[3,4,3072]{2,1,0:T(4,128)(2,1)S(1)}, bf16[3,4,3072]{2,1,0:T(4,128)(2,1)S(1)}, u32[]{:S(2)}, u32[]{:S(2)}) collective-permute-start(bf16[3,4,3072]{2,1,0:T(4,128)(2,1)S(1)} %get-tuple-element.34), channel_id=1, source_target_pairs={{0,1},{1,0},{2,3},{3,2},{4,5},{5,4},{6,7},{7,6},{8,9},{9,8},{10,11... | collective-permute-start | bytes 221192 | tf_op jit(solution)/shard_map/ppermute | solution.py:365
  48.5 7.8 %collective-permute-start.13 = (bf16[3,4,3072]{2,1,0:T(4,128)(2,1)S(1)}, bf16[3,4,3072]{2,1,0:T(4,128)(2,1)S(1)}, u32[]{:S(2)}, u32[]{:S(2)}) collective-permute-start(bf16[3,4,3072]{2,1,0:T(4,128)(2,1)S(1)} %get-tuple-element.35), channel_id=1, source_target_pairs={{0,2},{1,3},{2,0},{3,1},{4,6},{5,7},{6,4},{7,5},{8,10},{9,11},{10,... | collective-permute-start | bytes 221192 | tf_op jit(solution)/shard_map/ppermute | solution.py:365
  51.3 6.3 %collective-permute-start.14 = (bf16[3,4,3072]{2,1,0:T(4,128)(2,1)S(1)}, bf16[3,4,3072]{2,1,0:T(4,128)(2,1)S(1)}, u32[]{:S(2)}, u32[]{:S(2)}) collective-permute-start(bf16[3,4,3072]{2,1,0:T(4,128)(2,1)S(1)} %get-tuple-element.36), channel_id=1, source_target_pairs={{0,3},{1,2},{2,1},{3,0},{4,7},{5,6},{6,5},{7,4},{8,11},{9,10},{10,... | collective-permute-start | bytes 221192 | tf_op jit(solution)/shard_map/ppermute | solution.py:365
  57.7 3.5 %collective-permute-start.15 = (bf16[4,3072]{1,0:T(4,128)(2,1)S(1)}, bf16[4,3072]{1,0:T(4,128)(2,1)S(1)}, u32[]{:S(2)}, u32[]{:S(2)}) collective-permute-start(bf16[4,3072]{1,0:T(4,128)(2,1)S(1)} %get-tuple-element.38), channel_id=1, source_target_pairs={{0,4},{4,0},{8,12},{12,8},{1,5},{5,1},{9,13},{13,9},{2,6},{6,2},{1... | collective-permute-start | bytes 73736 | tf_op jit(solution)/shard_map/ppermute | solution.py:386
  57.8 6.7 %collective-permute-start.9 = (bf16[4,4096]{1,0:T(4,128)(2,1)S(1)}, bf16[4,4096]{1,0:T(4,128)(2,1)S(1)}, u32[]{:S(2)}, u32[]{:S(2)}) collective-permute-start(bf16[4,4096]{1,0:T(4,128)(2,1)S(1)} %get-tuple-element.29), channel_id=1, source_target_pairs={{0,4},{4,0},{8,12},{12,8},{1,5},{5,1},{9,13},{13,9},{2,6},{6,2},{1... | collective-permute-start | bytes 98312 | tf_op jit(solution)/shard_map/ppermute | solution.py:386
  58.3 6.2 %collective-permute-start.10 = (bf16[4,4096]{1,0:T(4,128)(2,1)S(1)}, bf16[4,4096]{1,0:T(4,128)(2,1)S(1)}, u32[]{:S(2)}, u32[]{:S(2)}) collective-permute-start(bf16[4,4096]{1,0:T(4,128)(2,1)S(1)} %get-tuple-element.30), channel_id=1, source_target_pairs={{0,8},{4,12},{8,0},{12,4},{1,9},{5,13},{9,1},{13,5},{2,10},{6,14},... | collective-permute-start | bytes 98312 | tf_op jit(solution)/shard_map/ppermute | solution.py:386
  59.8 4.7 %collective-permute-start.11 = (bf16[4,4096]{1,0:T(4,128)(2,1)S(1)}, bf16[4,4096]{1,0:T(4,128)(2,1)S(1)}, u32[]{:S(2)}, u32[]{:S(2)}) collective-permute-start(bf16[4,4096]{1,0:T(4,128)(2,1)S(1)} %get-tuple-element.31), channel_id=1, source_target_pairs={{0,12},{4,8},{8,4},{12,0},{1,13},{5,9},{9,5},{13,1},{2,14},{6,10},... | collective-permute-start | bytes 98312 | tf_op jit(solution)/shard_map/ppermute | solution.py:386
  59.8 4.2 %collective-permute-start.16 = (bf16[4,3072]{1,0:T(4,128)(2,1)S(1)}, bf16[4,3072]{1,0:T(4,128)(2,1)S(1)}, u32[]{:S(2)}, u32[]{:S(2)}) collective-permute-start(bf16[4,3072]{1,0:T(4,128)(2,1)S(1)} %get-tuple-element.39), channel_id=1, source_target_pairs={{0,8},{4,12},{8,0},{12,4},{1,9},{5,13},{9,1},{13,5},{2,10},{6,14},... | collective-permute-start | bytes 73736 | tf_op jit(solution)/shard_map/ppermute | solution.py:386
  61.2 3.3 %collective-permute-start.17 = (bf16[4,3072]{1,0:T(4,128)(2,1)S(1)}, bf16[4,3072]{1,0:T(4,128)(2,1)S(1)}, u32[]{:S(2)}, u32[]{:S(2)}) collective-permute-start(bf16[4,3072]{1,0:T(4,128)(2,1)S(1)} %get-tuple-element.40), channel_id=1, source_target_pairs={{0,12},{4,8},{8,4},{12,0},{1,13},{5,9},{9,5},{13,1},{2,14},{6,10},... | collective-permute-start | bytes 73736 | tf_op jit(solution)/shard_map/ppermute | solution.py:386
  (1 other events, 0.7 us)

commit v3 on v2

--- a/solution.py
+++ b/solution.py
@@ -12,6 +12,7 @@
 COLS = 256
 PAIR = 2 * COLS
 MIB = 2**20
+SCOPED = 18
 VMEM = pl.BlockSpec(memory_space=pltpu.VMEM)
 HBM = pl.BlockSpec(memory_space=pltpu.HBM)
 
@@ -102,7 +103,8 @@
 SLOTS = 3
 BLOCKS = N * N
 ROWS = BLOCKS * 4
-HELD = 3
+EARLY = 1
+HELD = 2
 PACKED = N * SLOTS * N
 
 
@@ -129,15 +131,24 @@
 
 
 def stack_kernel(*refs):
-    out_ref = refs[-1]
+    out_ref, mark_ref = refs[-2:]
+    mark_ref[...] = jnp.zeros_like(mark_ref)
     parts = [r[...].astype(jnp.float32) for r in refs[:4]]
     out_ref[...] = jnp.concatenate(parts, axis=0).astype(jnp.bfloat16)
 
 
-def up_copy(up_ref, buf, sem, j):
+def up_copy(up_ref, buf, sem, j, first):
     return pltpu.make_async_copy(
-        up_ref.at[:, pl.ds(j * PAIR, PAIR)], buf.at[j % HELD], sem.at[j]
-    )
+        up_ref.at[:, pl.ds(j * PAIR, PAIR)], buf.at[(j - first) % buf.shape[0]], sem.at[j]
+    )
+
+
+def fill_kernel(up_ref, _, buf, sem):
+    copies = [up_copy(up_ref, buf, sem, j, 0) for j in range(buf.shape[0])]
+    for c in copies:
+        c.start()
+    for c in copies:
+        c.wait()
 
 
 def routing(meta, me_row, me_col):
@@ -166,9 +177,10 @@
 
 def hidden_kernel(blocks, *refs):
     pieces = refs[:4]
-    gate_ref, up_ref, down_ref = refs[4:7]
-    outs, hid_ref, mix_ref = refs[7:11], refs[11], refs[12]
-    x_ref, h_ref, buf, piece_sem, fill_sem, down_sem = refs[13:]
+    gate_ref, up_ref, down_ref, early_ref = refs[4:8]
+    outs, hid_ref, mix_ref = refs[8:12], refs[12], refs[13]
+    x_ref, h_ref, buf, piece_sem, fill_sem, down_sem = refs[14:]
+    early = early_ref.shape[0]
     width = gate_ref.shape[0]
     deep = down_ref.shape[0]
     steps = deep // PAIR
@@ -178,31 +190,40 @@
     ]
     for c in bring:
         c.start()
-    for j in range(HELD):
-        up_copy(up_ref, buf, fill_sem, j).start()
+    for j in range(early, early + buf.shape[0]):
+        up_copy(up_ref, buf, fill_sem, j, early).start()
     x_ref[ROWS:, :] = jnp.zeros((x_ref.shape[0] - ROWS, x_ref.shape[1]), x_ref.dtype)
     for c in bring:
         c.wait()
 
     def down_place(b):
-        return buf.at[(1 + b // 3) % HELD, pl.ds(b % 3 * deep, deep)]
+        slot = (steps - early + b // 3) % buf.shape[0]
+        return buf.at[slot, pl.ds(b % 3 * deep, deep)]
 
     def down_copy(b):
         return pltpu.make_async_copy(
             down_ref.at[:, pl.ds(b * PAIR, PAIR)], down_place(b), down_sem.at[b]
         )
 
+    def load_next(used):
+        j = used + early + buf.shape[0]
+        if j < steps:
+            up_copy(up_ref, buf, fill_sem, j, early).start()
+            return
+        first = 3 * (j - steps)
+        for b in range(first, min(first + 3, blocks)):
+            down_copy(b).start()
+
     for j in range(steps):
         at = pl.ds(j * PAIR, PAIR)
         g = jnp.dot(x_ref[:, :width], gate_ref[:, at], preferred_element_type=jnp.float32)[:ROWS]
-        up_copy(up_ref, buf, fill_sem, j).wait()
-        u = jnp.dot(x_ref[:, :width], buf[j % HELD], preferred_element_type=jnp.float32)[:ROWS]
+        if j >= early:
+            up_copy(up_ref, buf, fill_sem, j, early).wait()
+        right = early_ref[j] if j < early else buf[(j - early) % buf.shape[0]]
+        u = jnp.dot(x_ref[:, :width], right, preferred_element_type=jnp.float32)[:ROWS]
         h_ref[:, at] = (g / (1.0 + jnp.exp(-g)) * u).astype(jnp.bfloat16)
-        if j + HELD < steps:
-            up_copy(up_ref, buf, fill_sem, j + HELD).start()
-        if j > 0:
-            for b in range(3 * (j - 1), min(3 * j, blocks)):
-                down_copy(b).start()
+        if j >= early:
+            load_next(j - early)
 
     meta = x_ref[:ROWS, width:].astype(jnp.float32)
     found, rank, weight = routing(meta, lax.axis_index("row"), lax.axis_index("col"))
@@ -232,6 +253,8 @@
             preferred_element_type=jnp.float32,
         )
         store_outs(value, outs, b * PAIR)
+        if b % 3 == 2:
+            load_next(steps - early + b // 3)
 
 
 def down_kernel(first, last, hid_from, down_ref, *refs):
@@ -252,7 +275,7 @@
 
 
 def merge_kernel(mix_ref, *refs):
-    ins, outs = refs[:4], refs[5:]
+    ins, outs = refs[:4], refs[-4:]
     got = jnp.concatenate(
         [ins[k][s].astype(jnp.float32) for k in range(N) for s in range(SLOTS)], axis=0
     ).astype(jnp.bfloat16)
@@ -309,24 +332,35 @@
     near = [packed] + [lax.ppermute(packed, "col", flip(N, k)) for k in (1, 2, 3)]
 
     hbm = lambda a: pltpu.with_memory_space_constraint(a, pltpu.HBM)
-    own = pl.pallas_call(
+    own, mark = pl.pallas_call(
         stack_kernel,
-        out_shape=shape((16, width + LANES), bf),
+        out_shape=[shape((16, width + LANES), bf), shape((8, LANES), jnp.float32)],
         in_specs=[VMEM] * 4 + [HBM],
-        out_specs=VMEM,
+        out_specs=[VMEM] * 2,
         compiler_params=params(6),
         name="stack",
     )(*near, hbm(up))
     by_core = lax.ppermute(own, "row", flip(N, 1))
     by_x = lax.ppermute(own, "row", flip(N, 2))
+    early = pl.pallas_call(
+        fill_kernel,
+        out_shape=pltpu.VMEM((EARLY, width, PAIR), bf),
+        in_specs=[HBM, anyw],
+        out_specs=VMEM,
+        scratch_shapes=[pltpu.SemaphoreType.DMA((EARLY,))],
+        compiler_params=params(SCOPED),
+        cost_estimate=cost(0, EARLY * width * PAIR * 2),
+        name="fill",
+    )(hbm(up), mark)
+    by_x, early = lax.optimization_barrier((by_x, early))
     by_both = lax.ppermute(by_x, "row", flip(N, 1))
 
     chunks = (8, 6)
     outs = [shape((SLOTS, N, n * PAIR), bf) for n in chunks]
     first = pl.pallas_call(
         functools.partial(hidden_kernel, chunks[0]),
-        out_shape=[outs[0]] * 4 + [shape((PACKED, wide), bf), shape((16, PACKED), jnp.float32)],
-        in_specs=[anyw] * 4 + [VMEM] + [HBM] * 2,
+        out_shape=[outs[0]] * 4 + [pltpu.VMEM((PACKED, wide), bf), pltpu.VMEM((16, PACKED), jnp.float32)],
+        in_specs=[anyw] * 4 + [VMEM] + [HBM] * 2 + [VMEM],
         out_specs=[VMEM] * 6,
         scratch_shapes=[
             pltpu.VMEM((2 * ROWS, width + LANES), bf),
@@ -336,10 +370,10 @@
             pltpu.SemaphoreType.DMA((wide // PAIR,)),
             pltpu.SemaphoreType.DMA((chunks[0],)),
         ],
-        compiler_params=params(28),
+        compiler_params=params(SCOPED),
         cost_estimate=cost(2 * ROWS * width * wide * 3, 40 * MIB),
         name="hidden",
-    )(own, by_core, by_x, by_both, pin(gate), hbm(up), hbm(down))
+    )(own, by_core, by_x, by_both, pin(gate), hbm(up), hbm(down), pin(early))
     hid, mix = first[4:6]
     parts = [first[:4]]
     parts.append(
@@ -360,18 +394,18 @@
         )(hid, pltpu.with_memory_space_constraint(down, pltpu.HBM))
     )
     finals = []
-    after = mix
+    after = []
     for c, part in enumerate(parts):
         got = [part[0]] + [lax.ppermute(part[k], "col", flip(N, k)) for k in (1, 2, 3)]
         value = pl.pallas_call(
             merge_kernel,
             out_shape=[shape((4, chunks[c] * PAIR), bf)] * 4,
-            in_specs=[VMEM] * 5 + [anyw],
+            in_specs=[VMEM] * 5 + [anyw] * len(after),
             out_specs=[VMEM] * 4,
             compiler_params=params(6),
             cost_estimate=cost(0, 8 * MIB),
             name="merge",
-        )(mix, *got, after)
+        )(mix, *got, *after)
         if c == 0:
             draws = pl.pallas_call(
                 draw_kernel,
@@ -382,8 +416,9 @@
                 cost_estimate=cost(0, 8 * MIB),
                 name="draws",
             )(dither, value[0])
-            after = draws
-        finals += [value[0]] + [lax.ppermute(value[q], "row", flip(N, q)) for q in (1, 2, 3)]
+        sent = [lax.ppermute(value[q], "row", flip(N, q)) for q in (1, 2, 3)]
+        finals += [value[0]] + sent
+        after = [draws] + sent
     return pl.pallas_call(
         functools.partial(final_kernel, len(chunks)),
         out_shape=shape((4, width), bf),

time: 65.6 us -> 60.8 us (0.927)
  waiting for transfers between devices: 17 us -> 12.2 us
  Pallas kernels: 26.2 us -> 27.4 us
  local copies, waits for them, and re-layouts: 1.66 us -> 0.73 us
    ppermute x1, waiting for transfers between devices: 5.2 us -> 1.94 us  [local_grid(): by_x = lax.ppermute(own, 'row', flip(N, 2))]
    pallas_call x1 -> x2, Pallas kernels: 0.06 us -> 3.3 us  [the longest x1 3.24 us: local_grid(): pl.pallas_call(fill_kernel, out_shape=pltpu.VMEM((EARLY, width, PAIR), bf...]
    pallas_call x1, Pallas kernels: 17 us -> 14.9 us  [local_grid(): pl.pallas_call(functools.partial(hidden_kernel, chunks[0]), out_shape=[ou...]
    ppermute x6, waiting for transfers between devices: 3.15 us -> 1.28 us  [local_grid(): lax.ppermute(part[k], 'col', flip(N, k))]
    unnamed x30 -> x22, local copies, waits for them, and re-layouts: 1.66 us -> 0.73 us
  transfers between devices with their start and end apart: 18 -> 18, of which waited for: 8 -> 9; matrix products, arithmetic and copies ran while one was open for 0% -> 0% of each run, Pallas kernels for 11% -> 17%
where the time goes in v3:
time: 60.8 us; the launch traced here: 60.7 us
  Pallas kernels  27.4 us (45%)
  starting transfers between devices  20.2 us (33%)
  waiting for transfers between devices  12.2 us (20%)
  local copies, waits for them, and re-layouts  0.73 us (1%)
    pallas_call x1, Pallas kernels, local_grid(): pl.pallas_call(functools.partial(hidden_kernel, chunks[0]), out_shape=[ou...  14.9 us
    ppermute x6, starting transfers between devices, local_grid(): lax.ppermute(part[k], 'col', flip(N, k))  8.9 us
    ppermute x3, starting transfers between devices, local_grid(): lax.ppermute(packed, 'col', flip(N, k))  5.76 us
    pallas_call x1, Pallas kernels, local_grid(): pl.pallas_call(functools.partial(down_kernel, chunks[0], chunks[0] + chun...  5.67 us
    ppermute x3, waiting for transfers between devices, local_grid(): lax.ppermute(packed, 'col', flip(N, k))  4.45 us
    ppermute x6, starting transfers between devices, local_grid(): sent = [lax.ppermute(value[q], 'row', flip(N, q)) for q in (1, 2, 3)]  3.86 us
    pallas_call x1, Pallas kernels, local_grid(): pl.pallas_call(fill_kernel, out_shape=pltpu.VMEM((EARLY, width, PAIR), bf...  3.24 us
    ppermute x6, waiting for transfers between devices, local_grid(): sent = [lax.ppermute(value[q], 'row', flip(N, q)) for q in (1, 2, 3)]  3.06 us
  transfers between devices with their start and end apart: 18, of which 9 were waited for; matrix products, arithmetic and copies ran while one was open for 0% of the time, Pallas kernels for 17%

profile of v3, /device:TPU:0, one launch (start us, length us, event | category | flops | bytes accessed | tf_op | source)
XLA Modules:
  0.0 60.7 jit_solution(5843975925290976840)
XLA Ops:
  0.0 0.9 %pack.1.refs_0_ = bf16[4,7296]{1,0:T(4,128)(2,1)S(1)} custom-call(bf16[4,7168]{1,0:T(4,128)(2,1)} %tok_ref.1, s32[4,8]{1,0:T(4,128)} %ids_ref.1, bf16[4,8]{1,0:T(4,128)(2,1)} %share_ref.1, bf16[7168,2048]{1,0:T(8,128)(2,1)} %bitcast.6), custom_call_target="tpu_custom_call" | custom-call | tf_op jit(solution)/shard_map/pack/pallas_call | solution.py:319
  1.0 5.1 %collective-permute-start.2 = (bf16[4,7296]{1,0:T(4,128)(2,1)S(1)}, bf16[4,7296]{1,0:T(4,128)(2,1)S(1)}, u32[]{:S(2)}, u32[]{:S(2)}) collective-permute-start(bf16[4,7296]{1,0:T(4,128)(2,1)S(1)} %pack.1.refs_0_), channel_id=1, source_target_pairs={{0,3},{1,2},{2,1},{3,0},{4,7},{5,6},{6,5},{7,4},{8,11},{9,10},{10,... | collective-permute-start | bytes 175112 | tf_op jit(solution)/shard_map/ppermute | solution.py:332
  6.1 0.6 %collective-permute-start = (bf16[4,7296]{1,0:T(4,128)(2,1)S(1)}, bf16[4,7296]{1,0:T(4,128)(2,1)S(1)}, u32[]{:S(2)}, u32[]{:S(2)}) collective-permute-start(bf16[4,7296]{1,0:T(4,128)(2,1)S(1)} %pack.1.refs_0_), channel_id=1, source_target_pairs={{0,1},{1,0},{2,3},{3,2},{4,5},{5,4},{6,7},{7,6},{8,9},{9,8},{10,11... | collective-permute-start | bytes 175112 | tf_op jit(solution)/shard_map/ppermute | solution.py:332
  6.8 1.8 %collective-permute-done.2.refs_3_ = bf16[4,7296]{1,0:T(4,128)(2,1)S(1)} collective-permute-done((bf16[4,7296]{1,0:T(4,128)(2,1)S(1)}, bf16[4,7296]{1,0:T(4,128)(2,1)S(1)}, u32[]{:S(2)}, u32[]{:S(2)}) %collective-permute-start.2) | collective-permute-done | bytes 58400 | tf_op jit(solution)/shard_map/ppermute | solution.py:332
  8.5 2.7 %collective-permute-done.1.refs_2_ = bf16[4,7296]{1,0:T(4,128)(2,1)S(1)} collective-permute-done((bf16[4,7296]{1,0:T(4,128)(2,1)S(1)}, bf16[4,7296]{1,0:T(4,128)(2,1)S(1)}, u32[]{:S(2)}, u32[]{:S(2)}) %collective-permute-start.1) | collective-permute-done | bytes 58400 | tf_op jit(solution)/shard_map/ppermute | solution.py:332
  11.3 1.6 %collective-permute-start.4 = (bf16[16,7296]{1,0:T(8,128)(2,1)S(1)}, bf16[16,7296]{1,0:T(8,128)(2,1)S(1)}, u32[]{:S(2)}, u32[]{:S(2)}) collective-permute-start(bf16[16,7296]{1,0:T(8,128)(2,1)S(1)} %get-tuple-element.27.refs_0_), channel_id=1, source_target_pairs={{0,8},{4,12},{8,0},{12,4},{1,9},{5,13},{9,1},{13,5},{2,10},{6,14},... | collective-permute-start | bytes 700424 | tf_op jit(solution)/shard_map/ppermute | solution.py:344
  12.9 3.2 %fill.1.refs_7_ = bf16[1,7168,512]{2,1,0:T(8,128)(2,1)S(1)} custom-call(bf16[7168,2048]{1,0:T(8,128)(2,1)} %bitcast.8, f32[8,128]{1,0:T(8,128)S(1)} %get-tuple-element.28._), custom_call_target="tpu_custom_call" | custom-call | bytes 7340032 | tf_op jit(solution)/shard_map/fill/pallas_call | solution.py:345
  16.2 1.9 %collective-permute-done.4.refs_2_ = bf16[16,7296]{1,0:T(8,128)(2,1)S(1)} collective-permute-done((bf16[16,7296]{1,0:T(8,128)(2,1)S(1)}, bf16[16,7296]{1,0:T(8,128)(2,1)S(1)}, u32[]{:S(2)}, u32[]{:S(2)}) %collective-permute-start.4) | collective-permute-done | bytes 233504 | tf_op jit(solution)/shard_map/ppermute | solution.py:344
  18.1 1.5 %collective-permute-done.5.refs_3_ = bf16[16,7296]{1,0:T(8,128)(2,1)S(1)} collective-permute-done((bf16[16,7296]{1,0:T(8,128)(2,1)S(1)}, bf16[16,7296]{1,0:T(8,128)(2,1)S(1)}, u32[]{:S(2)}, u32[]{:S(2)}) %collective-permute-start.5) | collective-permute-done | bytes 233504 | tf_op jit(solution)/shard_map/ppermute | solution.py:356
  19.6 0.7 %copy-done.3 = bf16[16,7296]{1,0:T(8,128)(2,1)} copy-done((bf16[16,7296]{1,0:T(8,128)(2,1)}, bf16[16,7296]{1,0:T(8,128)(2,1)S(1)}, u32[]{:S(2)}) %copy-start.3) | copy-done | bytes 233496
  20.4 14.9 %hidden.1 = (bf16[3,4,4096]{2,1,0:T(4,128)(2,1)S(1)}, bf16[3,4,4096]{2,1,0:T(4,128)(2,1)S(1)}, bf16[3,4,4096]{2,1,0:T(4,128)(2,1)S(1)}, bf16[3,4,4096]{2,1,0:T(4...) custom-call(bf16[16,7296]{1,0:T(8,128)(2,1)S(1)} %get-tuple-element.27.refs_0_, ...), custom_call_target="tpu_custom_call" | custom-call | flops 5637144576 | bytes 41943040 | tf_op jit(solution)/shard_map/hidden/pallas_call | solution.py:360
  35.3 0.7 %collective-permute-start.6 = (bf16[3,4,4096]{2,1,0:T(4,128)(2,1)S(1)}, bf16[3,4,4096]{2,1,0:T(4,128)(2,1)S(1)}, u32[]{:S(2)}, u32[]{:S(2)}) collective-permute-start(bf16[3,4,4096]{2,1,0:T(4,128)(2,1)S(1)} %get-tuple-element.33), channel_id=1, source_target_pairs={{0,1},{1,0},{2,3},{3,2},{4,5},{5,4},{6,7},{7,6},{8,9},{9,8},{10,11... | collective-permute-start | bytes 294920 | tf_op jit(solution)/shard_map/ppermute | solution.py:399
  36.0 2.1 %collective-permute-start.7 = (bf16[3,4,4096]{2,1,0:T(4,128)(2,1)S(1)}, bf16[3,4,4096]{2,1,0:T(4,128)(2,1)S(1)}, u32[]{:S(2)}, u32[]{:S(2)}) collective-permute-start(bf16[3,4,4096]{2,1,0:T(4,128)(2,1)S(1)} %get-tuple-element.34), channel_id=1, source_target_pairs={{0,2},{1,3},{2,0},{3,1},{4,6},{5,7},{6,4},{7,5},{8,10},{9,11},{10,... | collective-permute-start | bytes 294920 | tf_op jit(solution)/shard_map/ppermute | solution.py:399
  38.1 1.6 %collective-permute-start.8 = (bf16[3,4,4096]{2,1,0:T(4,128)(2,1)S(1)}, bf16[3,4,4096]{2,1,0:T(4,128)(2,1)S(1)}, u32[]{:S(2)}, u32[]{:S(2)}) collective-permute-start(bf16[3,4,4096]{2,1,0:T(4,128)(2,1)S(1)} %get-tuple-element.35), channel_id=1, source_target_pairs={{0,3},{1,2},{2,1},{3,0},{4,7},{5,6},{6,5},{7,4},{8,11},{9,10},{10,... | collective-permute-start | bytes 294920 | tf_op jit(solution)/shard_map/ppermute | solution.py:399
  39.8 5.7 %down.1 = (bf16[3,4,3072]{2,1,0:T(4,128)(2,1)S(1)}, bf16[3,4,3072]{2,1,0:T(4,128)(2,1)S(1)}, bf16[3,4,3072]{2,1,0:T(4,128)(2,1)S(1)}, bf16[3,4,3072]{2,1,0:T(4,128)(2,1)S(1)}) custom-call(bf16[48,2048]{1,0:T(8,128)(2,1)S(1)} %get-tuple-element.40.hid_from, bf16[2048,7168]{1,0:T(8,128)(2,1)} %bitcast.11), custom_call_target="tpu_custom_call" | custom-call | flops 1879048192 | bytes 10485760 | tf_op jit(solution)/shard_map/down/pallas_call | solution.py:380
  45.4 0.1 collective-permute-start.12
  45.5 2.8 %collective-permute-start.13 = (bf16[3,4,3072]{2,1,0:T(4,128)(2,1)S(1)}, bf16[3,4,3072]{2,1,0:T(4,128)(2,1)S(1)}, u32[]{:S(2)}, u32[]{:S(2)}) collective-permute-start(bf16[3,4,3072]{2,1,0:T(4,128)(2,1)S(1)} %get-tuple-element.43), channel_id=1, source_target_pairs={{0,2},{1,3},{2,0},{3,1},{4,6},{5,7},{6,4},{7,5},{8,10},{9,11},{10,... | collective-permute-start | bytes 221192 | tf_op jit(solution)/shard_map/ppermute | solution.py:399
  48.3 1.6 %collective-permute-start.14 = (bf16[3,4,3072]{2,1,0:T(4,128)(2,1)S(1)}, bf16[3,4,3072]{2,1,0:T(4,128)(2,1)S(1)}, u32[]{:S(2)}, u32[]{:S(2)}) collective-permute-start(bf16[3,4,3072]{2,1,0:T(4,128)(2,1)S(1)} %get-tuple-element.44), channel_id=1, source_target_pairs={{0,3},{1,2},{2,1},{3,0},{4,7},{5,6},{6,5},{7,4},{8,11},{9,10},{10,... | collective-permute-start | bytes 221192 | tf_op jit(solution)/shard_map/ppermute | solution.py:399
  49.9 0.2 merge.2
  50.2 1.6 %collective-permute-start.10 = (bf16[4,4096]{1,0:T(4,128)(2,1)S(1)}, bf16[4,4096]{1,0:T(4,128)(2,1)S(1)}, u32[]{:S(2)}, u32[]{:S(2)}) collective-permute-start(bf16[4,4096]{1,0:T(4,128)(2,1)S(1)} %get-tuple-element.38), channel_id=1, source_target_pairs={{0,8},{4,12},{8,0},{12,4},{1,9},{5,13},{9,1},{13,5},{2,10},{6,14},... | collective-permute-start | bytes 98312 | tf_op jit(solution)/shard_map/ppermute | solution.py:419
  51.8 0.2 collective-permute-start.11
  52.1 1.2 %draws.1.refs_4_.draw_ref = f32[4,4,7168]{2,1,0:T(4,128)S(1)} custom-call(bf16[4,4,7168]{2,1,0:T(4,128)(2,1)S(1)} %copy-done, bf16[4,4096]{1,0:T(4,128)(2,1)S(1)} %get-tuple-element.36._.refs_0_), custom_call_target="tpu_custom_call" | custom-call | bytes 8388608 | tf_op jit(solution)/shard_map/draws/pallas_call | solution.py:410
  53.3 0.2 collective-permute-done.13.refs_2_
  53.5 1.0 %collective-permute-done.14.refs_3_ = bf16[3,4,3072]{2,1,0:T(4,128)(2,1)S(1)} collective-permute-done((bf16[3,4,3072]{2,1,0:T(4,128)(2,1)S(1)}, bf16[3,4,3072]{2,1,0:T(4,128)(2,1)S(1)}, u32[]{:S(2)}, u32[]{:S(2)}) %collective-permute-start.14) | collective-permute-done | bytes 73760 | tf_op jit(solution)/shard_map/ppermute | solution.py:399
  54.5 0.6 %collective-permute-done.11.refs_7_.refs_3_ = bf16[4,4096]{1,0:T(4,128)(2,1)S(1)} collective-permute-done((bf16[4,4096]{1,0:T(4,128)(2,1)S(1)}, bf16[4,4096]{1,0:T(4,128)(2,1)S(1)}, u32[]{:S(2)}, u32[]{:S(2)}) %collective-permute-start.11) | collective-permute-done | bytes 32800 | tf_op jit(solution)/shard_map/ppermute | solution.py:419
  55.2 0.2 merge.3
  55.4 0.2 collective-permute-start.15
  55.6 0.8 %collective-permute-start.16 = (bf16[4,3072]{1,0:T(4,128)(2,1)S(1)}, bf16[4,3072]{1,0:T(4,128)(2,1)S(1)}, u32[]{:S(2)}, u32[]{:S(2)}) collective-permute-start(bf16[4,3072]{1,0:T(4,128)(2,1)S(1)} %get-tuple-element.47), channel_id=1, source_target_pairs={{0,8},{4,12},{8,0},{12,4},{1,9},{5,13},{9,1},{13,5},{2,10},{6,14},... | collective-permute-start | bytes 73736 | tf_op jit(solution)/shard_map/ppermute | solution.py:419
  56.4 0.9 %collective-permute-start.17 = (bf16[4,3072]{1,0:T(4,128)(2,1)S(1)}, bf16[4,3072]{1,0:T(4,128)(2,1)S(1)}, u32[]{:S(2)}, u32[]{:S(2)}) collective-permute-start(bf16[4,3072]{1,0:T(4,128)(2,1)S(1)} %get-tuple-element.48), channel_id=1, source_target_pairs={{0,12},{4,8},{8,4},{12,0},{1,13},{5,9},{9,5},{13,1},{2,14},{6,10},... | collective-permute-start | bytes 73736 | tf_op jit(solution)/shard_map/ppermute | solution.py:419
  57.3 2.2 %collective-permute-done.16.refs_6_ = bf16[4,3072]{1,0:T(4,128)(2,1)S(1)} collective-permute-done((bf16[4,3072]{1,0:T(4,128)(2,1)S(1)}, bf16[4,3072]{1,0:T(4,128)(2,1)S(1)}, u32[]{:S(2)}, u32[]{:S(2)}) %collective-permute-start.16) | collective-permute-done | bytes 24608 | tf_op jit(solution)/shard_map/ppermute | solution.py:419
  59.5 0.3 collective-permute-done.17.refs_7_
  59.7 1.0 %final.1 = bf16[4,7168]{1,0:T(4,128)(2,1)} custom-call(f32[4,4,7168]{2,1,0:T(4,128)S(1)} %draws.1.refs_4_.draw_ref, bf16[4,4096]{1,0:T(4,128)(2,1)S(1)} %get-tuple-element.36._.refs_0_, bf16[4,4096]{1,0:T(4,128)(2,1)S(1)} %collective-permute-done.9.refs_5_.refs_1_, bf16[4,4096]{1,0:T(4,128)(2,1)S(1)} %collective-permute-done.10.refs_6_.refs_2_, ...), custom_call_target="tpu_custom_call" | custom-call | tf_op jit(solution)/shard_map/final/pallas_call | solution.py:422
  (36 shorter events, 0.2 us)
Async XLA Ops:
  1.0 19.4 %slice-start = ((s8[29360128]{0:T(1024)(128)(4,1)}), s8[4194304]{0:T(1024)(128)(4,1)S(1)}, s32[]{:S(2)}) async-start(s8[29360128]{0:T(1024)(128)(4,1)} %bitcast.3), calls=%async_computation | async-start | bytes 8388608
  1.0 19.3 %slice-start.1 = ((s8[29360128]{0:T(1024)(128)(4,1)}), s8[4194304]{0:T(1024)(128)(4,1)S(1)}, s32[]{:S(2)}) async-start(s8[29360128]{0:T(1024)(128)(4,1)} %bitcast.3), calls=%async_computation.1 | async-start | bytes 8388608
  1.0 19.3 %slice-start.2 = ((s8[29360128]{0:T(1024)(128)(4,1)}), s8[4194304]{0:T(1024)(128)(4,1)S(1)}, s32[]{:S(2)}) async-start(s8[29360128]{0:T(1024)(128)(4,1)} %bitcast.3), calls=%async_computation.2 | async-start | bytes 8388608
  1.0 19.3 %slice-start.3 = ((s8[29360128]{0:T(1024)(128)(4,1)}), s8[4194304]{0:T(1024)(128)(4,1)S(1)}, s32[]{:S(2)}) async-start(s8[29360128]{0:T(1024)(128)(4,1)} %bitcast.3), calls=%async_computation.3 | async-start | bytes 8388608
  1.0 7.5 %collective-permute-start.2 = (bf16[4,7296]{1,0:T(4,128)(2,1)S(1)}, bf16[4,7296]{1,0:T(4,128)(2,1)S(1)}, u32[]{:S(2)}, u32[]{:S(2)}) collective-permute-start(bf16[4,7296]{1,0:T(4,128)(2,1)S(1)} %pack.1.refs_0_), channel_id=1, source_target_pairs={{0,3},{1,2},{2,1},{3,0},{4,7},{5,6},{6,5},{7,4},{8,11},{9,10},{10,... | collective-permute-start | bytes 175112 | tf_op jit(solution)/shard_map/ppermute | solution.py:332
  6.1 5.1 %collective-permute-start.1 = (bf16[4,7296]{1,0:T(4,128)(2,1)S(1)}, bf16[4,7296]{1,0:T(4,128)(2,1)S(1)}, u32[]{:S(2)}, u32[]{:S(2)}) collective-permute-start(bf16[4,7296]{1,0:T(4,128)(2,1)S(1)} %pack.1.refs_0_), channel_id=1, source_target_pairs={{0,2},{1,3},{2,0},{3,1},{4,6},{5,7},{6,4},{7,5},{8,10},{9,11},{10,... | collective-permute-start | bytes 175112 | tf_op jit(solution)/shard_map/ppermute | solution.py:332
  6.1 5.1 %collective-permute-start = (bf16[4,7296]{1,0:T(4,128)(2,1)S(1)}, bf16[4,7296]{1,0:T(4,128)(2,1)S(1)}, u32[]{:S(2)}, u32[]{:S(2)}) collective-permute-start(bf16[4,7296]{1,0:T(4,128)(2,1)S(1)} %pack.1.refs_0_), channel_id=1, source_target_pairs={{0,1},{1,0},{2,3},{3,2},{4,5},{5,4},{6,7},{7,6},{8,9},{9,8},{10,11... | collective-permute-start | bytes 175112 | tf_op jit(solution)/shard_map/ppermute | solution.py:332
  11.3 6.8 %collective-permute-start.4 = (bf16[16,7296]{1,0:T(8,128)(2,1)S(1)}, bf16[16,7296]{1,0:T(8,128)(2,1)S(1)}, u32[]{:S(2)}, u32[]{:S(2)}) collective-permute-start(bf16[16,7296]{1,0:T(8,128)(2,1)S(1)} %get-tuple-element.27.refs_0_), channel_id=1, source_target_pairs={{0,8},{4,12},{8,0},{12,4},{1,9},{5,13},{9,1},{13,5},{2,10},{6,14},... | collective-permute-start | bytes 700424 | tf_op jit(solution)/shard_map/ppermute | solution.py:344
  12.9 5.2 %collective-permute-start.3 = (bf16[16,7296]{1,0:T(8,128)(2,1)S(1)}, bf16[16,7296]{1,0:T(8,128)(2,1)S(1)}, u32[]{:S(2)}, u32[]{:S(2)}) collective-permute-start(bf16[16,7296]{1,0:T(8,128)(2,1)S(1)} %get-tuple-element.27.refs_0_), channel_id=1, source_target_pairs={{0,4},{4,0},{8,12},{12,8},{1,5},{5,1},{9,13},{13,9},{2,6},{6,2},{1... | collective-permute-start | bytes 700424 | tf_op jit(solution)/shard_map/ppermute | solution.py:343
  12.9 7.4 %slice-start.4 = ((s8[29360128]{0:T(1024)(128)(4,1)}), s8[4194304]{0:T(1024)(128)(4,1)S(1)}, s32[]{:S(2)}) async-start(s8[29360128]{0:T(1024)(128)(4,1)} %bitcast.3), calls=%async_computation.4 | async-start | bytes 8388608
  12.9 7.4 %slice-start.5 = ((s8[29360128]{0:T(1024)(128)(4,1)}), s8[4194304]{0:T(1024)(128)(4,1)S(1)}, s32[]{:S(2)}) async-start(s8[29360128]{0:T(1024)(128)(4,1)} %bitcast.3), calls=%async_computation.5 | async-start | bytes 8388608
  12.9 7.4 %slice-start.6 = ((s8[29360128]{0:T(1024)(128)(4,1)}), s8[4194304]{0:T(1024)(128)(4,1)S(1)}, s32[]{:S(2)}) async-start(s8[29360128]{0:T(1024)(128)(4,1)} %bitcast.3), calls=%async_computation.6 | async-start | bytes 8388608
  18.1 1.5 %copy-start.1 = (bf16[16,7296]{1,0:T(8,128)(2,1)}, bf16[16,7296]{1,0:T(8,128)(2,1)S(1)}, u32[]{:S(2)}) copy-start(bf16[16,7296]{1,0:T(8,128)(2,1)S(1)} %collective-permute-done.4.refs_2_) | copy-start | bytes 700420
  18.1 1.5 %collective-permute-start.5 = (bf16[16,7296]{1,0:T(8,128)(2,1)S(1)}, bf16[16,7296]{1,0:T(8,128)(2,1)S(1)}, u32[]{:S(2)}, u32[]{:S(2)}) collective-permute-start(bf16[16,7296]{1,0:T(8,128)(2,1)S(1)} %collective-permute-done.4.refs_2_), channel_id=1, source_target_pairs={{0,4},{4,0},{8,12},{12,8},{1,5},{5,1},{9,13},{13,9},{2,6},{6,2},{1... | collective-permute-start | bytes 700424 | tf_op jit(solution)/shard_map/ppermute | solution.py:356
  18.1 1.5 %copy-start.2 = (bf16[16,7296]{1,0:T(8,128)(2,1)}, bf16[16,7296]{1,0:T(8,128)(2,1)S(1)}, u32[]{:S(2)}) copy-start(bf16[16,7296]{1,0:T(8,128)(2,1)S(1)} %collective-permute-done.3.refs_1_) | copy-start | bytes 700420
  19.6 0.7 %copy-start.3 = (bf16[16,7296]{1,0:T(8,128)(2,1)}, bf16[16,7296]{1,0:T(8,128)(2,1)S(1)}, u32[]{:S(2)}) copy-start(bf16[16,7296]{1,0:T(8,128)(2,1)S(1)} %collective-permute-done.5.refs_3_) | copy-start | bytes 700420
  35.3 16.8 %copy-start = (bf16[4,4,7168]{2,1,0:T(4,128)(2,1)S(1)}, bf16[4,4,7168]{2,1,0:T(4,128)(2,1)}, u32[]{:S(2)}) copy-start(bf16[4,4,7168]{2,1,0:T(4,128)(2,1)} %dither_ref.1) | copy-start | bytes 688132
  35.3 13.0 %collective-permute-start.6 = (bf16[3,4,4096]{2,1,0:T(4,128)(2,1)S(1)}, bf16[3,4,4096]{2,1,0:T(4,128)(2,1)S(1)}, u32[]{:S(2)}, u32[]{:S(2)}) collective-permute-start(bf16[3,4,4096]{2,1,0:T(4,128)(2,1)S(1)} %get-tuple-element.33), channel_id=1, source_target_pairs={{0,1},{1,0},{2,3},{3,2},{4,5},{5,4},{6,7},{7,6},{8,9},{9,8},{10,11... | collective-permute-start | bytes 294920 | tf_op jit(solution)/shard_map/ppermute | solution.py:399
  36.0 13.9 %collective-permute-start.7 = (bf16[3,4,4096]{2,1,0:T(4,128)(2,1)S(1)}, bf16[3,4,4096]{2,1,0:T(4,128)(2,1)S(1)}, u32[]{:S(2)}, u32[]{:S(2)}) collective-permute-start(bf16[3,4,4096]{2,1,0:T(4,128)(2,1)S(1)} %get-tuple-element.34), channel_id=1, source_target_pairs={{0,2},{1,3},{2,0},{3,1},{4,6},{5,7},{6,4},{7,5},{8,10},{9,11},{10,... | collective-permute-start | bytes 294920 | tf_op jit(solution)/shard_map/ppermute | solution.py:399
  38.1 11.8 %collective-permute-start.8 = (bf16[3,4,4096]{2,1,0:T(4,128)(2,1)S(1)}, bf16[3,4,4096]{2,1,0:T(4,128)(2,1)S(1)}, u32[]{:S(2)}, u32[]{:S(2)}) collective-permute-start(bf16[3,4,4096]{2,1,0:T(4,128)(2,1)S(1)} %get-tuple-element.35), channel_id=1, source_target_pairs={{0,3},{1,2},{2,1},{3,0},{4,7},{5,6},{6,5},{7,4},{8,11},{9,10},{10,... | collective-permute-start | bytes 294920 | tf_op jit(solution)/shard_map/ppermute | solution.py:399
  45.4 6.4 %collective-permute-start.12 = (bf16[3,4,3072]{2,1,0:T(4,128)(2,1)S(1)}, bf16[3,4,3072]{2,1,0:T(4,128)(2,1)S(1)}, u32[]{:S(2)}, u32[]{:S(2)}) collective-permute-start(bf16[3,4,3072]{2,1,0:T(4,128)(2,1)S(1)} %get-tuple-element.42), channel_id=1, source_target_pairs={{0,1},{1,0},{2,3},{3,2},{4,5},{5,4},{6,7},{7,6},{8,9},{9,8},{10,11... | collective-permute-start | bytes 221192 | tf_op jit(solution)/shard_map/ppermute | solution.py:399
  45.5 8.0 %collective-permute-start.13 = (bf16[3,4,3072]{2,1,0:T(4,128)(2,1)S(1)}, bf16[3,4,3072]{2,1,0:T(4,128)(2,1)S(1)}, u32[]{:S(2)}, u32[]{:S(2)}) collective-permute-start(bf16[3,4,3072]{2,1,0:T(4,128)(2,1)S(1)} %get-tuple-element.43), channel_id=1, source_target_pairs={{0,2},{1,3},{2,0},{3,1},{4,6},{5,7},{6,4},{7,5},{8,10},{9,11},{10,... | collective-permute-start | bytes 221192 | tf_op jit(solution)/shard_map/ppermute | solution.py:399
  48.3 6.3 %collective-permute-start.14 = (bf16[3,4,3072]{2,1,0:T(4,128)(2,1)S(1)}, bf16[3,4,3072]{2,1,0:T(4,128)(2,1)S(1)}, u32[]{:S(2)}, u32[]{:S(2)}) collective-permute-start(bf16[3,4,3072]{2,1,0:T(4,128)(2,1)S(1)} %get-tuple-element.44), channel_id=1, source_target_pairs={{0,3},{1,2},{2,1},{3,0},{4,7},{5,6},{6,5},{7,4},{8,11},{9,10},{10,... | collective-permute-start | bytes 221192 | tf_op jit(solution)/shard_map/ppermute | solution.py:399
  50.1 4.4 %collective-permute-start.9 = (bf16[4,4096]{1,0:T(4,128)(2,1)S(1)}, bf16[4,4096]{1,0:T(4,128)(2,1)S(1)}, u32[]{:S(2)}, u32[]{:S(2)}) collective-permute-start(bf16[4,4096]{1,0:T(4,128)(2,1)S(1)} %get-tuple-element.37), channel_id=1, source_target_pairs={{0,4},{4,0},{8,12},{12,8},{1,5},{5,1},{9,13},{13,9},{2,6},{6,2},{1... | collective-permute-start | bytes 98312 | tf_op jit(solution)/shard_map/ppermute | solution.py:419
  50.2 4.4 %collective-permute-start.10 = (bf16[4,4096]{1,0:T(4,128)(2,1)S(1)}, bf16[4,4096]{1,0:T(4,128)(2,1)S(1)}, u32[]{:S(2)}, u32[]{:S(2)}) collective-permute-start(bf16[4,4096]{1,0:T(4,128)(2,1)S(1)} %get-tuple-element.38), channel_id=1, source_target_pairs={{0,8},{4,12},{8,0},{12,4},{1,9},{5,13},{9,1},{13,5},{2,10},{6,14},... | collective-permute-start | bytes 98312 | tf_op jit(solution)/shard_map/ppermute | solution.py:419
  51.8 3.3 %collective-permute-start.11 = (bf16[4,4096]{1,0:T(4,128)(2,1)S(1)}, bf16[4,4096]{1,0:T(4,128)(2,1)S(1)}, u32[]{:S(2)}, u32[]{:S(2)}) collective-permute-start(bf16[4,4096]{1,0:T(4,128)(2,1)S(1)} %get-tuple-element.39), channel_id=1, source_target_pairs={{0,12},{4,8},{8,4},{12,0},{1,13},{5,9},{9,5},{13,1},{2,14},{6,10},... | collective-permute-start | bytes 98312 | tf_op jit(solution)/shard_map/ppermute | solution.py:419
  55.4 1.9 %collective-permute-start.15 = (bf16[4,3072]{1,0:T(4,128)(2,1)S(1)}, bf16[4,3072]{1,0:T(4,128)(2,1)S(1)}, u32[]{:S(2)}, u32[]{:S(2)}) collective-permute-start(bf16[4,3072]{1,0:T(4,128)(2,1)S(1)} %get-tuple-element.46), channel_id=1, source_target_pairs={{0,4},{4,0},{8,12},{12,8},{1,5},{5,1},{9,13},{13,9},{2,6},{6,2},{1... | collective-permute-start | bytes 73736 | tf_op jit(solution)/shard_map/ppermute | solution.py:419
  55.6 3.8 %collective-permute-start.16 = (bf16[4,3072]{1,0:T(4,128)(2,1)S(1)}, bf16[4,3072]{1,0:T(4,128)(2,1)S(1)}, u32[]{:S(2)}, u32[]{:S(2)}) collective-permute-start(bf16[4,3072]{1,0:T(4,128)(2,1)S(1)} %get-tuple-element.47), channel_id=1, source_target_pairs={{0,8},{4,12},{8,0},{12,4},{1,9},{5,13},{9,1},{13,5},{2,10},{6,14},... | collective-permute-start | bytes 73736 | tf_op jit(solution)/shard_map/ppermute | solution.py:419
  56.4 3.3 %collective-permute-start.17 = (bf16[4,3072]{1,0:T(4,128)(2,1)S(1)}, bf16[4,3072]{1,0:T(4,128)(2,1)S(1)}, u32[]{:S(2)}, u32[]{:S(2)}) collective-permute-start(bf16[4,3072]{1,0:T(4,128)(2,1)S(1)} %get-tuple-element.48), channel_id=1, source_target_pairs={{0,12},{4,8},{8,4},{12,0},{1,13},{5,9},{9,5},{13,1},{2,14},{6,10},... | collective-permute-start | bytes 73736 | tf_op jit(solution)/shard_map/ppermute | solution.py:419

commit v4 on v3

--- a/solution.py
+++ b/solution.py
@@ -12,7 +12,7 @@
 COLS = 256
 PAIR = 2 * COLS
 MIB = 2**20
-SCOPED = 18
+SCOPED = 17.3
 VMEM = pl.BlockSpec(memory_space=pltpu.VMEM)
 HBM = pl.BlockSpec(memory_space=pltpu.HBM)
 

time: 60.8 us -> 59.9 us (0.985)
  local copies, waits for them, and re-layouts: 0.73 us -> 0.06 us
    unnamed x22 -> x16, local copies, waits for them, and re-layouts: 0.73 us -> 0.06 us
where the time goes in v4:
time: 59.9 us; the launch traced here: 59.7 us
  Pallas kernels  27.1 us (45%)
  starting transfers between devices  20.2 us (34%)
  waiting for transfers between devices  12.2 us (20%)
    pallas_call x1, Pallas kernels, local_grid(): pl.pallas_call(functools.partial(hidden_kernel, chunks[0]), out_shape=[ou...  14.6 us
    ppermute x6, starting transfers between devices, local_grid(): lax.ppermute(part[k], 'col', flip(N, k))  8.9 us
    ppermute x3, starting transfers between devices, local_grid(): lax.ppermute(packed, 'col', flip(N, k))  5.76 us
    pallas_call x1, Pallas kernels, local_grid(): pl.pallas_call(functools.partial(down_kernel, chunks[0], chunks[0] + chun...  5.67 us
    ppermute x3, waiting for transfers between devices, local_grid(): lax.ppermute(packed, 'col', flip(N, k))  4.45 us
    ppermute x6, starting transfers between devices, local_grid(): sent = [lax.ppermute(value[q], 'row', flip(N, q)) for q in (1, 2, 3)]  3.86 us
    pallas_call x1, Pallas kernels, local_grid(): pl.pallas_call(fill_kernel, out_shape=pltpu.VMEM((EARLY, width, PAIR), bf...  3.24 us
    ppermute x6, waiting for transfers between devices, local_grid(): sent = [lax.ppermute(value[q], 'row', flip(N, q)) for q in (1, 2, 3)]  2.7 us
  transfers between devices with their start and end apart: 18, of which 9 were waited for; matrix products, arithmetic and copies ran while one was open for 0% of the time, Pallas kernels for 17%

profile of v4, /device:TPU:0, one launch (start us, length us, event | category | flops | bytes accessed | tf_op | source)
XLA Modules:
  0.0 59.7 jit_solution(1705170139396102005)
XLA Ops:
  0.0 0.9 %pack.1.refs_0_ = bf16[4,7296]{1,0:T(4,128)(2,1)S(1)} custom-call(bf16[4,7168]{1,0:T(4,128)(2,1)} %tok_ref.1, s32[4,8]{1,0:T(4,128)} %ids_ref.1, bf16[4,8]{1,0:T(4,128)(2,1)} %share_ref.1, bf16[7168,2048]{1,0:T(8,128)(2,1)} %bitcast.6), custom_call_target="tpu_custom_call" | custom-call | tf_op jit(solution)/shard_map/pack/pallas_call | solution.py:319
  1.0 5.1 %collective-permute-start.2 = (bf16[4,7296]{1,0:T(4,128)(2,1)S(1)}, bf16[4,7296]{1,0:T(4,128)(2,1)S(1)}, u32[]{:S(2)}, u32[]{:S(2)}) collective-permute-start(bf16[4,7296]{1,0:T(4,128)(2,1)S(1)} %pack.1.refs_0_), channel_id=1, source_target_pairs={{0,3},{1,2},{2,1},{3,0},{4,7},{5,6},{6,5},{7,4},{8,11},{9,10},{10,... | collective-permute-start | bytes 175112 | tf_op jit(solution)/shard_map/ppermute | solution.py:332
  6.1 0.6 %collective-permute-start = (bf16[4,7296]{1,0:T(4,128)(2,1)S(1)}, bf16[4,7296]{1,0:T(4,128)(2,1)S(1)}, u32[]{:S(2)}, u32[]{:S(2)}) collective-permute-start(bf16[4,7296]{1,0:T(4,128)(2,1)S(1)} %pack.1.refs_0_), channel_id=1, source_target_pairs={{0,1},{1,0},{2,3},{3,2},{4,5},{5,4},{6,7},{7,6},{8,9},{9,8},{10,11... | collective-permute-start | bytes 175112 | tf_op jit(solution)/shard_map/ppermute | solution.py:332
  6.8 1.8 %collective-permute-done.2.refs_3_ = bf16[4,7296]{1,0:T(4,128)(2,1)S(1)} collective-permute-done((bf16[4,7296]{1,0:T(4,128)(2,1)S(1)}, bf16[4,7296]{1,0:T(4,128)(2,1)S(1)}, u32[]{:S(2)}, u32[]{:S(2)}) %collective-permute-start.2) | collective-permute-done | bytes 58400 | tf_op jit(solution)/shard_map/ppermute | solution.py:332
  8.5 2.7 %collective-permute-done.1.refs_2_ = bf16[4,7296]{1,0:T(4,128)(2,1)S(1)} collective-permute-done((bf16[4,7296]{1,0:T(4,128)(2,1)S(1)}, bf16[4,7296]{1,0:T(4,128)(2,1)S(1)}, u32[]{:S(2)}, u32[]{:S(2)}) %collective-permute-start.1) | collective-permute-done | bytes 58400 | tf_op jit(solution)/shard_map/ppermute | solution.py:332
  11.3 1.6 %collective-permute-start.4 = (bf16[16,7296]{1,0:T(8,128)(2,1)S(1)}, bf16[16,7296]{1,0:T(8,128)(2,1)S(1)}, u32[]{:S(2)}, u32[]{:S(2)}) collective-permute-start(bf16[16,7296]{1,0:T(8,128)(2,1)S(1)} %get-tuple-element.27.refs_0_), channel_id=1, source_target_pairs={{0,8},{4,12},{8,0},{12,4},{1,9},{5,13},{9,1},{13,5},{2,10},{6,14},... | collective-permute-start | bytes 700424 | tf_op jit(solution)/shard_map/ppermute | solution.py:344
  12.9 3.2 %fill.1.refs_7_ = bf16[1,7168,512]{2,1,0:T(8,128)(2,1)S(1)} custom-call(bf16[7168,2048]{1,0:T(8,128)(2,1)} %bitcast.8, f32[8,128]{1,0:T(8,128)S(1)} %get-tuple-element.28._), custom_call_target="tpu_custom_call" | custom-call | bytes 7340032 | tf_op jit(solution)/shard_map/fill/pallas_call | solution.py:345
  16.2 1.9 %collective-permute-done.4.refs_2_ = bf16[16,7296]{1,0:T(8,128)(2,1)S(1)} collective-permute-done((bf16[16,7296]{1,0:T(8,128)(2,1)S(1)}, bf16[16,7296]{1,0:T(8,128)(2,1)S(1)}, u32[]{:S(2)}, u32[]{:S(2)}) %collective-permute-start.4) | collective-permute-done | bytes 233504 | tf_op jit(solution)/shard_map/ppermute | solution.py:344
  18.1 1.5 %collective-permute-done.5.refs_3_ = bf16[16,7296]{1,0:T(8,128)(2,1)S(1)} collective-permute-done((bf16[16,7296]{1,0:T(8,128)(2,1)S(1)}, bf16[16,7296]{1,0:T(8,128)(2,1)S(1)}, u32[]{:S(2)}, u32[]{:S(2)}) %collective-permute-start.5) | collective-permute-done | bytes 233504 | tf_op jit(solution)/shard_map/ppermute | solution.py:356
  19.7 14.6 %hidden.1 = (bf16[3,4,4096]{2,1,0:T(4,128)(2,1)S(1)}, bf16[3,4,4096]{2,1,0:T(4,128)(2,1)S(1)}, bf16[3,4,4096]{2,1,0:T(4,128)(2,1)S(1)}, bf16[3,4,4096]{2,1,0:T(4...) custom-call(bf16[16,7296]{1,0:T(8,128)(2,1)S(1)} %get-tuple-element.27.refs_0_, ...), custom_call_target="tpu_custom_call" | custom-call | flops 5637144576 | bytes 41943040 | tf_op jit(solution)/shard_map/hidden/pallas_call | solution.py:360
  34.3 1.1 %collective-permute-start.6 = (bf16[3,4,4096]{2,1,0:T(4,128)(2,1)S(1)}, bf16[3,4,4096]{2,1,0:T(4,128)(2,1)S(1)}, u32[]{:S(2)}, u32[]{:S(2)}) collective-permute-start(bf16[3,4,4096]{2,1,0:T(4,128)(2,1)S(1)} %get-tuple-element.33), channel_id=1, source_target_pairs={{0,1},{1,0},{2,3},{3,2},{4,5},{5,4},{6,7},{7,6},{8,9},{9,8},{10,11... | collective-permute-start | bytes 294920 | tf_op jit(solution)/shard_map/ppermute | solution.py:399
  35.4 2.1 %collective-permute-start.7 = (bf16[3,4,4096]{2,1,0:T(4,128)(2,1)S(1)}, bf16[3,4,4096]{2,1,0:T(4,128)(2,1)S(1)}, u32[]{:S(2)}, u32[]{:S(2)}) collective-permute-start(bf16[3,4,4096]{2,1,0:T(4,128)(2,1)S(1)} %get-tuple-element.34), channel_id=1, source_target_pairs={{0,2},{1,3},{2,0},{3,1},{4,6},{5,7},{6,4},{7,5},{8,10},{9,11},{10,... | collective-permute-start | bytes 294920 | tf_op jit(solution)/shard_map/ppermute | solution.py:399
  37.6 1.2 %collective-permute-start.8 = (bf16[3,4,4096]{2,1,0:T(4,128)(2,1)S(1)}, bf16[3,4,4096]{2,1,0:T(4,128)(2,1)S(1)}, u32[]{:S(2)}, u32[]{:S(2)}) collective-permute-start(bf16[3,4,4096]{2,1,0:T(4,128)(2,1)S(1)} %get-tuple-element.35), channel_id=1, source_target_pairs={{0,3},{1,2},{2,1},{3,0},{4,7},{5,6},{6,5},{7,4},{8,11},{9,10},{10,... | collective-permute-start | bytes 294920 | tf_op jit(solution)/shard_map/ppermute | solution.py:399
  38.8 5.7 %down.1 = (bf16[3,4,3072]{2,1,0:T(4,128)(2,1)S(1)}, bf16[3,4,3072]{2,1,0:T(4,128)(2,1)S(1)}, bf16[3,4,3072]{2,1,0:T(4,128)(2,1)S(1)}, bf16[3,4,3072]{2,1,0:T(4,128)(2,1)S(1)}) custom-call(bf16[48,2048]{1,0:T(8,128)(2,1)S(1)} %get-tuple-element.40.hid_from, bf16[2048,7168]{1,0:T(8,128)(2,1)} %bitcast.11), custom_call_target="tpu_custom_call" | custom-call | flops 1879048192 | bytes 10485760 | tf_op jit(solution)/shard_map/down/pallas_call | solution.py:380
  44.5 0.2 collective-permute-start.12
  44.7 3.0 %collective-permute-start.13 = (bf16[3,4,3072]{2,1,0:T(4,128)(2,1)S(1)}, bf16[3,4,3072]{2,1,0:T(4,128)(2,1)S(1)}, u32[]{:S(2)}, u32[]{:S(2)}) collective-permute-start(bf16[3,4,3072]{2,1,0:T(4,128)(2,1)S(1)} %get-tuple-element.43), channel_id=1, source_target_pairs={{0,2},{1,3},{2,0},{3,1},{4,6},{5,7},{6,4},{7,5},{8,10},{9,11},{10,... | collective-permute-start | bytes 221192 | tf_op jit(solution)/shard_map/ppermute | solution.py:399
  47.7 1.2 %collective-permute-start.14 = (bf16[3,4,3072]{2,1,0:T(4,128)(2,1)S(1)}, bf16[3,4,3072]{2,1,0:T(4,128)(2,1)S(1)}, u32[]{:S(2)}, u32[]{:S(2)}) collective-permute-start(bf16[3,4,3072]{2,1,0:T(4,128)(2,1)S(1)} %get-tuple-element.44), channel_id=1, source_target_pairs={{0,3},{1,2},{2,1},{3,0},{4,7},{5,6},{6,5},{7,4},{8,11},{9,10},{10,... | collective-permute-start | bytes 221192 | tf_op jit(solution)/shard_map/ppermute | solution.py:399
  48.9 0.2 merge.2
  49.1 0.1 collective-permute-start.9
  49.2 1.7 %collective-permute-start.10 = (bf16[4,4096]{1,0:T(4,128)(2,1)S(1)}, bf16[4,4096]{1,0:T(4,128)(2,1)S(1)}, u32[]{:S(2)}, u32[]{:S(2)}) collective-permute-start(bf16[4,4096]{1,0:T(4,128)(2,1)S(1)} %get-tuple-element.38), channel_id=1, source_target_pairs={{0,8},{4,12},{8,0},{12,4},{1,9},{5,13},{9,1},{13,5},{2,10},{6,14},... | collective-permute-start | bytes 98312 | tf_op jit(solution)/shard_map/ppermute | solution.py:419
  50.9 0.2 collective-permute-start.11
  51.1 1.2 %draws.1.refs_4_.draw_ref = f32[4,4,7168]{2,1,0:T(4,128)S(1)} custom-call(bf16[4,4,7168]{2,1,0:T(4,128)(2,1)S(1)} %copy-done, bf16[4,4096]{1,0:T(4,128)(2,1)S(1)} %get-tuple-element.36._.refs_0_), custom_call_target="tpu_custom_call" | custom-call | bytes 8388608 | tf_op jit(solution)/shard_map/draws/pallas_call | solution.py:410
  52.3 0.7 %collective-permute-done.13.refs_2_ = bf16[3,4,3072]{2,1,0:T(4,128)(2,1)S(1)} collective-permute-done((bf16[3,4,3072]{2,1,0:T(4,128)(2,1)S(1)}, bf16[3,4,3072]{2,1,0:T(4,128)(2,1)S(1)}, u32[]{:S(2)}, u32[]{:S(2)}) %collective-permute-start.13) | collective-permute-done | bytes 73760 | tf_op jit(solution)/shard_map/ppermute | solution.py:399
  53.0 1.0 %collective-permute-done.14.refs_3_ = bf16[3,4,3072]{2,1,0:T(4,128)(2,1)S(1)} collective-permute-done((bf16[3,4,3072]{2,1,0:T(4,128)(2,1)S(1)}, bf16[3,4,3072]{2,1,0:T(4,128)(2,1)S(1)}, u32[]{:S(2)}, u32[]{:S(2)}) %collective-permute-start.14) | collective-permute-done | bytes 73760 | tf_op jit(solution)/shard_map/ppermute | solution.py:399
  54.0 0.3 collective-permute-done.11.refs_7_.refs_3_
  54.2 0.2 merge.3
  54.4 0.2 collective-permute-start.15
  54.7 0.8 %collective-permute-start.16 = (bf16[4,3072]{1,0:T(4,128)(2,1)S(1)}, bf16[4,3072]{1,0:T(4,128)(2,1)S(1)}, u32[]{:S(2)}, u32[]{:S(2)}) collective-permute-start(bf16[4,3072]{1,0:T(4,128)(2,1)S(1)} %get-tuple-element.47), channel_id=1, source_target_pairs={{0,8},{4,12},{8,0},{12,4},{1,9},{5,13},{9,1},{13,5},{2,10},{6,14},... | collective-permute-start | bytes 73736 | tf_op jit(solution)/shard_map/ppermute | solution.py:419
  55.5 0.9 %collective-permute-start.17 = (bf16[4,3072]{1,0:T(4,128)(2,1)S(1)}, bf16[4,3072]{1,0:T(4,128)(2,1)S(1)}, u32[]{:S(2)}, u32[]{:S(2)}) collective-permute-start(bf16[4,3072]{1,0:T(4,128)(2,1)S(1)} %get-tuple-element.48), channel_id=1, source_target_pairs={{0,12},{4,8},{8,4},{12,0},{1,13},{5,9},{9,5},{13,1},{2,14},{6,10},... | collective-permute-start | bytes 73736 | tf_op jit(solution)/shard_map/ppermute | solution.py:419
  56.4 2.1 %collective-permute-done.16.refs_6_ = bf16[4,3072]{1,0:T(4,128)(2,1)S(1)} collective-permute-done((bf16[4,3072]{1,0:T(4,128)(2,1)S(1)}, bf16[4,3072]{1,0:T(4,128)(2,1)S(1)}, u32[]{:S(2)}, u32[]{:S(2)}) %collective-permute-start.16) | collective-permute-done | bytes 24608 | tf_op jit(solution)/shard_map/ppermute | solution.py:419
  58.5 0.3 collective-permute-done.17.refs_7_
  58.8 1.0 %final.1 = bf16[4,7168]{1,0:T(4,128)(2,1)} custom-call(f32[4,4,7168]{2,1,0:T(4,128)S(1)} %draws.1.refs_4_.draw_ref, bf16[4,4096]{1,0:T(4,128)(2,1)S(1)} %get-tuple-element.36._.refs_0_, bf16[4,4096]{1,0:T(4,128)(2,1)S(1)} %collective-permute-done.9.refs_5_.refs_1_, bf16[4,4096]{1,0:T(4,128)(2,1)S(1)} %collective-permute-done.10.refs_6_.refs_2_, ...), custom_call_target="tpu_custom_call" | custom-call | tf_op jit(solution)/shard_map/final/pallas_call | solution.py:422
  (30 shorter events, 0.2 us)
Async XLA Ops:
  1.0 18.7 %slice-start = ((s8[29360128]{0:T(1024)(128)(4,1)}), s8[4194304]{0:T(1024)(128)(4,1)S(1)}, s32[]{:S(2)}) async-start(s8[29360128]{0:T(1024)(128)(4,1)} %bitcast.3), calls=%async_computation | async-start | bytes 8388608
  1.0 18.7 %slice-start.1 = ((s8[29360128]{0:T(1024)(128)(4,1)}), s8[4194304]{0:T(1024)(128)(4,1)S(1)}, s32[]{:S(2)}) async-start(s8[29360128]{0:T(1024)(128)(4,1)} %bitcast.3), calls=%async_computation.1 | async-start | bytes 8388608
  1.0 18.6 %slice-start.2 = ((s8[29360128]{0:T(1024)(128)(4,1)}), s8[4194304]{0:T(1024)(128)(4,1)S(1)}, s32[]{:S(2)}) async-start(s8[29360128]{0:T(1024)(128)(4,1)} %bitcast.3), calls=%async_computation.2 | async-start | bytes 8388608
  1.0 18.6 %slice-start.3 = ((s8[29360128]{0:T(1024)(128)(4,1)}), s8[4194304]{0:T(1024)(128)(4,1)S(1)}, s32[]{:S(2)}) async-start(s8[29360128]{0:T(1024)(128)(4,1)} %bitcast.3), calls=%async_computation.3 | async-start | bytes 8388608
  1.0 7.5 %collective-permute-start.2 = (bf16[4,7296]{1,0:T(4,128)(2,1)S(1)}, bf16[4,7296]{1,0:T(4,128)(2,1)S(1)}, u32[]{:S(2)}, u32[]{:S(2)}) collective-permute-start(bf16[4,7296]{1,0:T(4,128)(2,1)S(1)} %pack.1.refs_0_), channel_id=1, source_target_pairs={{0,3},{1,2},{2,1},{3,0},{4,7},{5,6},{6,5},{7,4},{8,11},{9,10},{10,... | collective-permute-start | bytes 175112 | tf_op jit(solution)/shard_map/ppermute | solution.py:332
  6.1 5.1 %collective-permute-start.1 = (bf16[4,7296]{1,0:T(4,128)(2,1)S(1)}, bf16[4,7296]{1,0:T(4,128)(2,1)S(1)}, u32[]{:S(2)}, u32[]{:S(2)}) collective-permute-start(bf16[4,7296]{1,0:T(4,128)(2,1)S(1)} %pack.1.refs_0_), channel_id=1, source_target_pairs={{0,2},{1,3},{2,0},{3,1},{4,6},{5,7},{6,4},{7,5},{8,10},{9,11},{10,... | collective-permute-start | bytes 175112 | tf_op jit(solution)/shard_map/ppermute | solution.py:332
  6.1 5.1 %collective-permute-start = (bf16[4,7296]{1,0:T(4,128)(2,1)S(1)}, bf16[4,7296]{1,0:T(4,128)(2,1)S(1)}, u32[]{:S(2)}, u32[]{:S(2)}) collective-permute-start(bf16[4,7296]{1,0:T(4,128)(2,1)S(1)} %pack.1.refs_0_), channel_id=1, source_target_pairs={{0,1},{1,0},{2,3},{3,2},{4,5},{5,4},{6,7},{7,6},{8,9},{9,8},{10,11... | collective-permute-start | bytes 175112 | tf_op jit(solution)/shard_map/ppermute | solution.py:332
  11.3 6.8 %collective-permute-start.4 = (bf16[16,7296]{1,0:T(8,128)(2,1)S(1)}, bf16[16,7296]{1,0:T(8,128)(2,1)S(1)}, u32[]{:S(2)}, u32[]{:S(2)}) collective-permute-start(bf16[16,7296]{1,0:T(8,128)(2,1)S(1)} %get-tuple-element.27.refs_0_), channel_id=1, source_target_pairs={{0,8},{4,12},{8,0},{12,4},{1,9},{5,13},{9,1},{13,5},{2,10},{6,14},... | collective-permute-start | bytes 700424 | tf_op jit(solution)/shard_map/ppermute | solution.py:344
  12.9 5.2 %collective-permute-start.3 = (bf16[16,7296]{1,0:T(8,128)(2,1)S(1)}, bf16[16,7296]{1,0:T(8,128)(2,1)S(1)}, u32[]{:S(2)}, u32[]{:S(2)}) collective-permute-start(bf16[16,7296]{1,0:T(8,128)(2,1)S(1)} %get-tuple-element.27.refs_0_), channel_id=1, source_target_pairs={{0,4},{4,0},{8,12},{12,8},{1,5},{5,1},{9,13},{13,9},{2,6},{6,2},{1... | collective-permute-start | bytes 700424 | tf_op jit(solution)/shard_map/ppermute | solution.py:343
  12.9 6.7 %slice-start.4 = ((s8[29360128]{0:T(1024)(128)(4,1)}), s8[4194304]{0:T(1024)(128)(4,1)S(1)}, s32[]{:S(2)}) async-start(s8[29360128]{0:T(1024)(128)(4,1)} %bitcast.3), calls=%async_computation.4 | async-start | bytes 8388608
  12.9 6.7 %slice-start.5 = ((s8[29360128]{0:T(1024)(128)(4,1)}), s8[4194304]{0:T(1024)(128)(4,1)S(1)}, s32[]{:S(2)}) async-start(s8[29360128]{0:T(1024)(128)(4,1)} %bitcast.3), calls=%async_computation.5 | async-start | bytes 8388608
  12.9 6.8 %slice-start.6 = ((s8[29360128]{0:T(1024)(128)(4,1)}), s8[4194304]{0:T(1024)(128)(4,1)S(1)}, s32[]{:S(2)}) async-start(s8[29360128]{0:T(1024)(128)(4,1)} %bitcast.3), calls=%async_computation.6 | async-start | bytes 8388608
  18.1 1.5 %collective-permute-start.5 = (bf16[16,7296]{1,0:T(8,128)(2,1)S(1)}, bf16[16,7296]{1,0:T(8,128)(2,1)S(1)}, u32[]{:S(2)}, u32[]{:S(2)}) collective-permute-start(bf16[16,7296]{1,0:T(8,128)(2,1)S(1)} %collective-permute-done.4.refs_2_), channel_id=1, source_target_pairs={{0,4},{4,0},{8,12},{12,8},{1,5},{5,1},{9,13},{13,9},{2,6},{6,2},{1... | collective-permute-start | bytes 700424 | tf_op jit(solution)/shard_map/ppermute | solution.py:356
  34.3 16.8 %copy-start = (bf16[4,4,7168]{2,1,0:T(4,128)(2,1)S(1)}, bf16[4,4,7168]{2,1,0:T(4,128)(2,1)}, u32[]{:S(2)}) copy-start(bf16[4,4,7168]{2,1,0:T(4,128)(2,1)} %dither_ref.1) | copy-start | bytes 688132
  34.3 13.4 %collective-permute-start.6 = (bf16[3,4,4096]{2,1,0:T(4,128)(2,1)S(1)}, bf16[3,4,4096]{2,1,0:T(4,128)(2,1)S(1)}, u32[]{:S(2)}, u32[]{:S(2)}) collective-permute-start(bf16[3,4,4096]{2,1,0:T(4,128)(2,1)S(1)} %get-tuple-element.33), channel_id=1, source_target_pairs={{0,1},{1,0},{2,3},{3,2},{4,5},{5,4},{6,7},{7,6},{8,9},{9,8},{10,11... | collective-permute-start | bytes 294920 | tf_op jit(solution)/shard_map/ppermute | solution.py:399
  35.4 13.5 %collective-permute-start.7 = (bf16[3,4,4096]{2,1,0:T(4,128)(2,1)S(1)}, bf16[3,4,4096]{2,1,0:T(4,128)(2,1)S(1)}, u32[]{:S(2)}, u32[]{:S(2)}) collective-permute-start(bf16[3,4,4096]{2,1,0:T(4,128)(2,1)S(1)} %get-tuple-element.34), channel_id=1, source_target_pairs={{0,2},{1,3},{2,0},{3,1},{4,6},{5,7},{6,4},{7,5},{8,10},{9,11},{10,... | collective-permute-start | bytes 294920 | tf_op jit(solution)/shard_map/ppermute | solution.py:399
  37.6 11.4 %collective-permute-start.8 = (bf16[3,4,4096]{2,1,0:T(4,128)(2,1)S(1)}, bf16[3,4,4096]{2,1,0:T(4,128)(2,1)S(1)}, u32[]{:S(2)}, u32[]{:S(2)}) collective-permute-start(bf16[3,4,4096]{2,1,0:T(4,128)(2,1)S(1)} %get-tuple-element.35), channel_id=1, source_target_pairs={{0,3},{1,2},{2,1},{3,0},{4,7},{5,6},{6,5},{7,4},{8,11},{9,10},{10,... | collective-permute-start | bytes 294920 | tf_op jit(solution)/shard_map/ppermute | solution.py:399
  44.5 6.4 %collective-permute-start.12 = (bf16[3,4,3072]{2,1,0:T(4,128)(2,1)S(1)}, bf16[3,4,3072]{2,1,0:T(4,128)(2,1)S(1)}, u32[]{:S(2)}, u32[]{:S(2)}) collective-permute-start(bf16[3,4,3072]{2,1,0:T(4,128)(2,1)S(1)} %get-tuple-element.42), channel_id=1, source_target_pairs={{0,1},{1,0},{2,3},{3,2},{4,5},{5,4},{6,7},{7,6},{8,9},{9,8},{10,11... | collective-permute-start | bytes 221192 | tf_op jit(solution)/shard_map/ppermute | solution.py:399
  44.7 8.3 %collective-permute-start.13 = (bf16[3,4,3072]{2,1,0:T(4,128)(2,1)S(1)}, bf16[3,4,3072]{2,1,0:T(4,128)(2,1)S(1)}, u32[]{:S(2)}, u32[]{:S(2)}) collective-permute-start(bf16[3,4,3072]{2,1,0:T(4,128)(2,1)S(1)} %get-tuple-element.43), channel_id=1, source_target_pairs={{0,2},{1,3},{2,0},{3,1},{4,6},{5,7},{6,4},{7,5},{8,10},{9,11},{10,... | collective-permute-start | bytes 221192 | tf_op jit(solution)/shard_map/ppermute | solution.py:399
  47.7 6.3 %collective-permute-start.14 = (bf16[3,4,3072]{2,1,0:T(4,128)(2,1)S(1)}, bf16[3,4,3072]{2,1,0:T(4,128)(2,1)S(1)}, u32[]{:S(2)}, u32[]{:S(2)}) collective-permute-start(bf16[3,4,3072]{2,1,0:T(4,128)(2,1)S(1)} %get-tuple-element.44), channel_id=1, source_target_pairs={{0,3},{1,2},{2,1},{3,0},{4,7},{5,6},{6,5},{7,4},{8,11},{9,10},{10,... | collective-permute-start | bytes 221192 | tf_op jit(solution)/shard_map/ppermute | solution.py:399
  49.1 4.8 %collective-permute-start.9 = (bf16[4,4096]{1,0:T(4,128)(2,1)S(1)}, bf16[4,4096]{1,0:T(4,128)(2,1)S(1)}, u32[]{:S(2)}, u32[]{:S(2)}) collective-permute-start(bf16[4,4096]{1,0:T(4,128)(2,1)S(1)} %get-tuple-element.37), channel_id=1, source_target_pairs={{0,4},{4,0},{8,12},{12,8},{1,5},{5,1},{9,13},{13,9},{2,6},{6,2},{1... | collective-permute-start | bytes 98312 | tf_op jit(solution)/shard_map/ppermute | solution.py:419
  49.2 4.7 %collective-permute-start.10 = (bf16[4,4096]{1,0:T(4,128)(2,1)S(1)}, bf16[4,4096]{1,0:T(4,128)(2,1)S(1)}, u32[]{:S(2)}, u32[]{:S(2)}) collective-permute-start(bf16[4,4096]{1,0:T(4,128)(2,1)S(1)} %get-tuple-element.38), channel_id=1, source_target_pairs={{0,8},{4,12},{8,0},{12,4},{1,9},{5,13},{9,1},{13,5},{2,10},{6,14},... | collective-permute-start | bytes 98312 | tf_op jit(solution)/shard_map/ppermute | solution.py:419
  50.9 3.3 %collective-permute-start.11 = (bf16[4,4096]{1,0:T(4,128)(2,1)S(1)}, bf16[4,4096]{1,0:T(4,128)(2,1)S(1)}, u32[]{:S(2)}, u32[]{:S(2)}) collective-permute-start(bf16[4,4096]{1,0:T(4,128)(2,1)S(1)} %get-tuple-element.39), channel_id=1, source_target_pairs={{0,12},{4,8},{8,4},{12,0},{1,13},{5,9},{9,5},{13,1},{2,14},{6,10},... | collective-permute-start | bytes 98312 | tf_op jit(solution)/shard_map/ppermute | solution.py:419
  54.4 1.9 %collective-permute-start.15 = (bf16[4,3072]{1,0:T(4,128)(2,1)S(1)}, bf16[4,3072]{1,0:T(4,128)(2,1)S(1)}, u32[]{:S(2)}, u32[]{:S(2)}) collective-permute-start(bf16[4,3072]{1,0:T(4,128)(2,1)S(1)} %get-tuple-element.46), channel_id=1, source_target_pairs={{0,4},{4,0},{8,12},{12,8},{1,5},{5,1},{9,13},{13,9},{2,6},{6,2},{1... | collective-permute-start | bytes 73736 | tf_op jit(solution)/shard_map/ppermute | solution.py:419
  54.7 3.8 %collective-permute-start.16 = (bf16[4,3072]{1,0:T(4,128)(2,1)S(1)}, bf16[4,3072]{1,0:T(4,128)(2,1)S(1)}, u32[]{:S(2)}, u32[]{:S(2)}) collective-permute-start(bf16[4,3072]{1,0:T(4,128)(2,1)S(1)} %get-tuple-element.47), channel_id=1, source_target_pairs={{0,8},{4,12},{8,0},{12,4},{1,9},{5,13},{9,1},{13,5},{2,10},{6,14},... | collective-permute-start | bytes 73736 | tf_op jit(solution)/shard_map/ppermute | solution.py:419
  55.5 3.3 %collective-permute-start.17 = (bf16[4,3072]{1,0:T(4,128)(2,1)S(1)}, bf16[4,3072]{1,0:T(4,128)(2,1)S(1)}, u32[]{:S(2)}, u32[]{:S(2)}) collective-permute-start(bf16[4,3072]{1,0:T(4,128)(2,1)S(1)} %get-tuple-element.48), channel_id=1, source_target_pairs={{0,12},{4,8},{8,4},{12,0},{1,13},{5,9},{9,5},{13,1},{2,14},{6,10},... | collective-permute-start | bytes 73736 | tf_op jit(solution)/shard_map/ppermute | solution.py:419

commit v5 on v4

--- a/solution.py
+++ b/solution.py
@@ -261,17 +261,22 @@
     outs, buf, hid_ref, sem, hid_sem = refs[:4], refs[4], refs[5], refs[6], refs[7]
     bring = pltpu.make_async_copy(hid_from, hid_ref, hid_sem)
     bring.start()
-    copies = [
-        pltpu.make_async_copy(down_ref.at[:, pl.ds(b * PAIR, PAIR)], buf.at[b - first], sem.at[b - first])
-        for b in range(first, last)
-    ]
+    cuts = [(i * PAIR, PAIR) for i in range(last - first - 1)]
+    cuts += [((last - first) * PAIR - n * COLS, COLS) for n in (2, 1)]
+    copies = []
+    for i, (lo, wide) in enumerate(cuts):
+        into = buf.at[lo // PAIR, :, pl.ds(lo % PAIR, wide)]
+        copies.append(
+            pltpu.make_async_copy(down_ref.at[:, pl.ds(first * PAIR + lo, wide)], into, sem.at[i])
+        )
     for c in copies:
         c.start()
     bring.wait()
-    for i, c in enumerate(copies):
+    for (lo, wide), c in zip(cuts, copies):
         c.wait()
-        value = jnp.dot(hid_ref[...], buf[i], preferred_element_type=jnp.float32)
-        store_outs(value, outs, i * PAIR)
+        right = buf[lo // PAIR, :, lo % PAIR : lo % PAIR + wide]
+        value = jnp.dot(hid_ref[...], right, preferred_element_type=jnp.float32)
+        store_outs(value, outs, lo)
 
 
 def merge_kernel(mix_ref, *refs):
@@ -296,15 +301,18 @@
 
 def final_kernel(chunks, draw_ref, *refs):
     ins, out_ref = refs[:-1], refs[-1]
-    total = None
+    total, ends = [None] * chunks, [0]
+    for c in range(chunks):
+        ends.append(ends[-1] + ins[c * N].shape[1])
     for q in range(N):
-        part = jnp.concatenate(
-            [ins[c * N + q][...].astype(jnp.float32) for c in range(chunks)], axis=1
-        )
-        spread = 0.125 * jnp.max(jnp.abs(part), axis=1, keepdims=True)
-        part = part + spread * draw_ref[q]
-        total = part if total is None else total + part
-    out_ref[...] = total.astype(jnp.bfloat16)
+        part = [ins[c * N + q][...].astype(jnp.float32) for c in range(chunks)]
+        peak = [jnp.max(jnp.abs(p), axis=1, keepdims=True) for p in part]
+        spread = 0.125 * functools.reduce(jnp.maximum, peak)
+        for c in range(chunks):
+            term = part[c] + spread * draw_ref[q, :, ends[c] : ends[c + 1]]
+            total[c] = term if q == 0 else total[c] + term
+    for c in range(chunks):
+        out_ref[:, ends[c] : ends[c + 1]] = total[c].astype(jnp.bfloat16)
 
 
 def local_grid(tokens, expert_ids, route_weight, dither, gate_proj, up_proj, down_proj):
@@ -385,7 +393,7 @@
             scratch_shapes=[
                 pltpu.VMEM((chunks[1], deep, PAIR), bf),
                 pltpu.VMEM((PACKED, wide), bf),
-                pltpu.SemaphoreType.DMA((chunks[1],)),
+                pltpu.SemaphoreType.DMA((chunks[1] + 1,)),
                 pltpu.SemaphoreType.DMA,
             ],
             compiler_params=params(28),

time: 59.9 us -> 60 us (level)
  transfers between devices with their start and end apart: 18 -> 18, of which waited for: 9 -> 9; matrix products, arithmetic and copies ran while one was open for 0% -> 0% of each run, Pallas kernels for 17% -> 18%
where the time goes in v5:
time: 60 us; the launch traced here: 59.8 us
  Pallas kernels  27.2 us (45%)
  starting transfers between devices  20.2 us (34%)
  waiting for transfers between devices  12.2 us (20%)
    pallas_call x1, Pallas kernels, local_grid(): pl.pallas_call(functools.partial(hidden_kernel, chunks[0]), out_shape=[ou...  14.6 us
    ppermute x6, starting transfers between devices, local_grid(): lax.ppermute(part[k], 'col', flip(N, k))  8.9 us
    pallas_call x1, Pallas kernels, local_grid(): pl.pallas_call(functools.partial(down_kernel, chunks[0], chunks[0] + chun...  5.86 us
    ppermute x3, starting transfers between devices, local_grid(): lax.ppermute(packed, 'col', flip(N, k))  5.76 us
    ppermute x3, waiting for transfers between devices, local_grid(): lax.ppermute(packed, 'col', flip(N, k))  4.45 us
    ppermute x6, starting transfers between devices, local_grid(): sent = [lax.ppermute(value[q], 'row', flip(N, q)) for q in (1, 2, 3)]  3.86 us
    pallas_call x1, Pallas kernels, local_grid(): pl.pallas_call(fill_kernel, out_shape=pltpu.VMEM((EARLY, width, PAIR), bf...  3.24 us
    ppermute x6, waiting for transfers between devices, local_grid(): sent = [lax.ppermute(value[q], 'row', flip(N, q)) for q in (1, 2, 3)]  2.69 us
  transfers between devices with their start and end apart: 18, of which 9 were waited for; matrix products, arithmetic and copies ran while one was open for 0% of the time, Pallas kernels for 18%

profile of v5, /device:TPU:0, one launch (start us, length us, event | category | flops | bytes accessed | tf_op | source)
XLA Modules:
  0.0 59.8 jit_solution(12534826628061905444)
XLA Ops:
  0.0 0.9 %pack.1.refs_0_ = bf16[4,7296]{1,0:T(4,128)(2,1)S(1)} custom-call(bf16[4,7168]{1,0:T(4,128)(2,1)} %tok_ref.1, s32[4,8]{1,0:T(4,128)} %ids_ref.1, bf16[4,8]{1,0:T(4,128)(2,1)} %share_ref.1, bf16[7168,2048]{1,0:T(8,128)(2,1)} %bitcast.6), custom_call_target="tpu_custom_call" | custom-call | tf_op jit(solution)/shard_map/pack/pallas_call | solution.py:327
  1.0 5.1 %collective-permute-start.2 = (bf16[4,7296]{1,0:T(4,128)(2,1)S(1)}, bf16[4,7296]{1,0:T(4,128)(2,1)S(1)}, u32[]{:S(2)}, u32[]{:S(2)}) collective-permute-start(bf16[4,7296]{1,0:T(4,128)(2,1)S(1)} %pack.1.refs_0_), channel_id=1, source_target_pairs={{0,3},{1,2},{2,1},{3,0},{4,7},{5,6},{6,5},{7,4},{8,11},{9,10},{10,... | collective-permute-start | bytes 175112 | tf_op jit(solution)/shard_map/ppermute | solution.py:340
  6.1 0.6 %collective-permute-start = (bf16[4,7296]{1,0:T(4,128)(2,1)S(1)}, bf16[4,7296]{1,0:T(4,128)(2,1)S(1)}, u32[]{:S(2)}, u32[]{:S(2)}) collective-permute-start(bf16[4,7296]{1,0:T(4,128)(2,1)S(1)} %pack.1.refs_0_), channel_id=1, source_target_pairs={{0,1},{1,0},{2,3},{3,2},{4,5},{5,4},{6,7},{7,6},{8,9},{9,8},{10,11... | collective-permute-start | bytes 175112 | tf_op jit(solution)/shard_map/ppermute | solution.py:340
  6.8 1.8 %collective-permute-done.2.refs_3_ = bf16[4,7296]{1,0:T(4,128)(2,1)S(1)} collective-permute-done((bf16[4,7296]{1,0:T(4,128)(2,1)S(1)}, bf16[4,7296]{1,0:T(4,128)(2,1)S(1)}, u32[]{:S(2)}, u32[]{:S(2)}) %collective-permute-start.2) | collective-permute-done | bytes 58400 | tf_op jit(solution)/shard_map/ppermute | solution.py:340
  8.5 2.7 %collective-permute-done.1.refs_2_ = bf16[4,7296]{1,0:T(4,128)(2,1)S(1)} collective-permute-done((bf16[4,7296]{1,0:T(4,128)(2,1)S(1)}, bf16[4,7296]{1,0:T(4,128)(2,1)S(1)}, u32[]{:S(2)}, u32[]{:S(2)}) %collective-permute-start.1) | collective-permute-done | bytes 58400 | tf_op jit(solution)/shard_map/ppermute | solution.py:340
  11.3 1.6 %collective-permute-start.4 = (bf16[16,7296]{1,0:T(8,128)(2,1)S(1)}, bf16[16,7296]{1,0:T(8,128)(2,1)S(1)}, u32[]{:S(2)}, u32[]{:S(2)}) collective-permute-start(bf16[16,7296]{1,0:T(8,128)(2,1)S(1)} %get-tuple-element.27.refs_0_), channel_id=1, source_target_pairs={{0,8},{4,12},{8,0},{12,4},{1,9},{5,13},{9,1},{13,5},{2,10},{6,14},... | collective-permute-start | bytes 700424 | tf_op jit(solution)/shard_map/ppermute | solution.py:352
  12.9 3.2 %fill.1.refs_7_ = bf16[1,7168,512]{2,1,0:T(8,128)(2,1)S(1)} custom-call(bf16[7168,2048]{1,0:T(8,128)(2,1)} %bitcast.8, f32[8,128]{1,0:T(8,128)S(1)} %get-tuple-element.28._), custom_call_target="tpu_custom_call" | custom-call | bytes 7340032 | tf_op jit(solution)/shard_map/fill/pallas_call | solution.py:353
  16.2 1.9 %collective-permute-done.4.refs_2_ = bf16[16,7296]{1,0:T(8,128)(2,1)S(1)} collective-permute-done((bf16[16,7296]{1,0:T(8,128)(2,1)S(1)}, bf16[16,7296]{1,0:T(8,128)(2,1)S(1)}, u32[]{:S(2)}, u32[]{:S(2)}) %collective-permute-start.4) | collective-permute-done | bytes 233504 | tf_op jit(solution)/shard_map/ppermute | solution.py:352
  18.1 1.5 %collective-permute-done.5.refs_3_ = bf16[16,7296]{1,0:T(8,128)(2,1)S(1)} collective-permute-done((bf16[16,7296]{1,0:T(8,128)(2,1)S(1)}, bf16[16,7296]{1,0:T(8,128)(2,1)S(1)}, u32[]{:S(2)}, u32[]{:S(2)}) %collective-permute-start.5) | collective-permute-done | bytes 233504 | tf_op jit(solution)/shard_map/ppermute | solution.py:364
  19.7 14.6 %hidden.1 = (bf16[3,4,4096]{2,1,0:T(4,128)(2,1)S(1)}, bf16[3,4,4096]{2,1,0:T(4,128)(2,1)S(1)}, bf16[3,4,4096]{2,1,0:T(4,128)(2,1)S(1)}, bf16[3,4,4096]{2,1,0:T(4...) custom-call(bf16[16,7296]{1,0:T(8,128)(2,1)S(1)} %get-tuple-element.27.refs_0_, ...), custom_call_target="tpu_custom_call" | custom-call | flops 5637144576 | bytes 41943040 | tf_op jit(solution)/shard_map/hidden/pallas_call | solution.py:368
  34.3 1.1 %collective-permute-start.6 = (bf16[3,4,4096]{2,1,0:T(4,128)(2,1)S(1)}, bf16[3,4,4096]{2,1,0:T(4,128)(2,1)S(1)}, u32[]{:S(2)}, u32[]{:S(2)}) collective-permute-start(bf16[3,4,4096]{2,1,0:T(4,128)(2,1)S(1)} %get-tuple-element.33), channel_id=1, source_target_pairs={{0,1},{1,0},{2,3},{3,2},{4,5},{5,4},{6,7},{7,6},{8,9},{9,8},{10,11... | collective-permute-start | bytes 294920 | tf_op jit(solution)/shard_map/ppermute | solution.py:407
  35.4 2.1 %collective-permute-start.7 = (bf16[3,4,4096]{2,1,0:T(4,128)(2,1)S(1)}, bf16[3,4,4096]{2,1,0:T(4,128)(2,1)S(1)}, u32[]{:S(2)}, u32[]{:S(2)}) collective-permute-start(bf16[3,4,4096]{2,1,0:T(4,128)(2,1)S(1)} %get-tuple-element.34), channel_id=1, source_target_pairs={{0,2},{1,3},{2,0},{3,1},{4,6},{5,7},{6,4},{7,5},{8,10},{9,11},{10,... | collective-permute-start | bytes 294920 | tf_op jit(solution)/shard_map/ppermute | solution.py:407
  37.6 1.2 %collective-permute-start.8 = (bf16[3,4,4096]{2,1,0:T(4,128)(2,1)S(1)}, bf16[3,4,4096]{2,1,0:T(4,128)(2,1)S(1)}, u32[]{:S(2)}, u32[]{:S(2)}) collective-permute-start(bf16[3,4,4096]{2,1,0:T(4,128)(2,1)S(1)} %get-tuple-element.35), channel_id=1, source_target_pairs={{0,3},{1,2},{2,1},{3,0},{4,7},{5,6},{6,5},{7,4},{8,11},{9,10},{10,... | collective-permute-start | bytes 294920 | tf_op jit(solution)/shard_map/ppermute | solution.py:407
  38.8 5.9 %down.1 = (bf16[3,4,3072]{2,1,0:T(4,128)(2,1)S(1)}, bf16[3,4,3072]{2,1,0:T(4,128)(2,1)S(1)}, bf16[3,4,3072]{2,1,0:T(4,128)(2,1)S(1)}, bf16[3,4,3072]{2,1,0:T(4,128)(2,1)S(1)}) custom-call(bf16[48,2048]{1,0:T(8,128)(2,1)S(1)} %get-tuple-element.40.hid_from, bf16[2048,7168]{1,0:T(8,128)(2,1)} %bitcast.11), custom_call_target="tpu_custom_call" | custom-call | flops 1879048192 | bytes 10485760 | tf_op jit(solution)/shard_map/down/pallas_call | solution.py:388
  44.7 0.2 collective-permute-start.12
  44.8 3.0 %collective-permute-start.13 = (bf16[3,4,3072]{2,1,0:T(4,128)(2,1)S(1)}, bf16[3,4,3072]{2,1,0:T(4,128)(2,1)S(1)}, u32[]{:S(2)}, u32[]{:S(2)}) collective-permute-start(bf16[3,4,3072]{2,1,0:T(4,128)(2,1)S(1)} %get-tuple-element.43), channel_id=1, source_target_pairs={{0,2},{1,3},{2,0},{3,1},{4,6},{5,7},{6,4},{7,5},{8,10},{9,11},{10,... | collective-permute-start | bytes 221192 | tf_op jit(solution)/shard_map/ppermute | solution.py:407
  47.9 1.2 %collective-permute-start.14 = (bf16[3,4,3072]{2,1,0:T(4,128)(2,1)S(1)}, bf16[3,4,3072]{2,1,0:T(4,128)(2,1)S(1)}, u32[]{:S(2)}, u32[]{:S(2)}) collective-permute-start(bf16[3,4,3072]{2,1,0:T(4,128)(2,1)S(1)} %get-tuple-element.44), channel_id=1, source_target_pairs={{0,3},{1,2},{2,1},{3,0},{4,7},{5,6},{6,5},{7,4},{8,11},{9,10},{10,... | collective-permute-start | bytes 221192 | tf_op jit(solution)/shard_map/ppermute | solution.py:407
  49.1 0.2 merge.2
  49.3 0.1 collective-permute-start.9
  49.4 1.7 %collective-permute-start.10 = (bf16[4,4096]{1,0:T(4,128)(2,1)S(1)}, bf16[4,4096]{1,0:T(4,128)(2,1)S(1)}, u32[]{:S(2)}, u32[]{:S(2)}) collective-permute-start(bf16[4,4096]{1,0:T(4,128)(2,1)S(1)} %get-tuple-element.38), channel_id=1, source_target_pairs={{0,8},{4,12},{8,0},{12,4},{1,9},{5,13},{9,1},{13,5},{2,10},{6,14},... | collective-permute-start | bytes 98312 | tf_op jit(solution)/shard_map/ppermute | solution.py:427
  51.1 0.2 collective-permute-start.11
  51.3 1.2 %draws.1.refs_4_.draw_ref = f32[4,4,7168]{2,1,0:T(4,128)S(1)} custom-call(bf16[4,4,7168]{2,1,0:T(4,128)(2,1)S(1)} %copy-done, bf16[4,4096]{1,0:T(4,128)(2,1)S(1)} %get-tuple-element.36._.refs_0_), custom_call_target="tpu_custom_call" | custom-call | bytes 8388608 | tf_op jit(solution)/shard_map/draws/pallas_call | solution.py:418
  52.5 0.7 %collective-permute-done.13.refs_2_ = bf16[3,4,3072]{2,1,0:T(4,128)(2,1)S(1)} collective-permute-done((bf16[3,4,3072]{2,1,0:T(4,128)(2,1)S(1)}, bf16[3,4,3072]{2,1,0:T(4,128)(2,1)S(1)}, u32[]{:S(2)}, u32[]{:S(2)}) %collective-permute-start.13) | collective-permute-done | bytes 73760 | tf_op jit(solution)/shard_map/ppermute | solution.py:407
  53.2 1.0 %collective-permute-done.14.refs_3_ = bf16[3,4,3072]{2,1,0:T(4,128)(2,1)S(1)} collective-permute-done((bf16[3,4,3072]{2,1,0:T(4,128)(2,1)S(1)}, bf16[3,4,3072]{2,1,0:T(4,128)(2,1)S(1)}, u32[]{:S(2)}, u32[]{:S(2)}) %collective-permute-start.14) | collective-permute-done | bytes 73760 | tf_op jit(solution)/shard_map/ppermute | solution.py:407
  54.1 0.3 collective-permute-done.11.refs_7_.refs_3_
  54.4 0.2 merge.3
  54.6 0.2 collective-permute-start.15
  54.8 0.8 %collective-permute-start.16 = (bf16[4,3072]{1,0:T(4,128)(2,1)S(1)}, bf16[4,3072]{1,0:T(4,128)(2,1)S(1)}, u32[]{:S(2)}, u32[]{:S(2)}) collective-permute-start(bf16[4,3072]{1,0:T(4,128)(2,1)S(1)} %get-tuple-element.47), channel_id=1, source_target_pairs={{0,8},{4,12},{8,0},{12,4},{1,9},{5,13},{9,1},{13,5},{2,10},{6,14},... | collective-permute-start | bytes 73736 | tf_op jit(solution)/shard_map/ppermute | solution.py:427
  55.7 0.9 %collective-permute-start.17 = (bf16[4,3072]{1,0:T(4,128)(2,1)S(1)}, bf16[4,3072]{1,0:T(4,128)(2,1)S(1)}, u32[]{:S(2)}, u32[]{:S(2)}) collective-permute-start(bf16[4,3072]{1,0:T(4,128)(2,1)S(1)} %get-tuple-element.48), channel_id=1, source_target_pairs={{0,12},{4,8},{8,4},{12,0},{1,13},{5,9},{9,5},{13,1},{2,14},{6,10},... | collective-permute-start | bytes 73736 | tf_op jit(solution)/shard_map/ppermute | solution.py:427
  56.5 2.1 %collective-permute-done.16.refs_6_ = bf16[4,3072]{1,0:T(4,128)(2,1)S(1)} collective-permute-done((bf16[4,3072]{1,0:T(4,128)(2,1)S(1)}, bf16[4,3072]{1,0:T(4,128)(2,1)S(1)}, u32[]{:S(2)}, u32[]{:S(2)}) %collective-permute-start.16) | collective-permute-done | bytes 24608 | tf_op jit(solution)/shard_map/ppermute | solution.py:427
  58.7 0.3 collective-permute-done.17.refs_7_
  59.0 0.9 %final.1 = bf16[4,7168]{1,0:T(4,128)(2,1)} custom-call(f32[4,4,7168]{2,1,0:T(4,128)S(1)} %draws.1.refs_4_.draw_ref, bf16[4,4096]{1,0:T(4,128)(2,1)S(1)} %get-tuple-element.36._.refs_0_, bf16[4,4096]{1,0:T(4,128)(2,1)S(1)} %collective-permute-done.9.refs_5_.refs_1_, bf16[4,4096]{1,0:T(4,128)(2,1)S(1)} %collective-permute-done.10.refs_6_.refs_2_, ...), custom_call_target="tpu_custom_call" | custom-call | tf_op jit(solution)/shard_map/final/pallas_call | solution.py:430
  (30 shorter events, 0.2 us)
Async XLA Ops:
  1.0 18.7 %slice-start = ((s8[29360128]{0:T(1024)(128)(4,1)}), s8[4194304]{0:T(1024)(128)(4,1)S(1)}, s32[]{:S(2)}) async-start(s8[29360128]{0:T(1024)(128)(4,1)} %bitcast.3), calls=%async_computation | async-start | bytes 8388608
  1.0 18.7 %slice-start.1 = ((s8[29360128]{0:T(1024)(128)(4,1)}), s8[4194304]{0:T(1024)(128)(4,1)S(1)}, s32[]{:S(2)}) async-start(s8[29360128]{0:T(1024)(128)(4,1)} %bitcast.3), calls=%async_computation.1 | async-start | bytes 8388608
  1.0 18.6 %slice-start.2 = ((s8[29360128]{0:T(1024)(128)(4,1)}), s8[4194304]{0:T(1024)(128)(4,1)S(1)}, s32[]{:S(2)}) async-start(s8[29360128]{0:T(1024)(128)(4,1)} %bitcast.3), calls=%async_computation.2 | async-start | bytes 8388608
  1.0 18.6 %slice-start.3 = ((s8[29360128]{0:T(1024)(128)(4,1)}), s8[4194304]{0:T(1024)(128)(4,1)S(1)}, s32[]{:S(2)}) async-start(s8[29360128]{0:T(1024)(128)(4,1)} %bitcast.3), calls=%async_computation.3 | async-start | bytes 8388608
  1.0 7.5 %collective-permute-start.2 = (bf16[4,7296]{1,0:T(4,128)(2,1)S(1)}, bf16[4,7296]{1,0:T(4,128)(2,1)S(1)}, u32[]{:S(2)}, u32[]{:S(2)}) collective-permute-start(bf16[4,7296]{1,0:T(4,128)(2,1)S(1)} %pack.1.refs_0_), channel_id=1, source_target_pairs={{0,3},{1,2},{2,1},{3,0},{4,7},{5,6},{6,5},{7,4},{8,11},{9,10},{10,... | collective-permute-start | bytes 175112 | tf_op jit(solution)/shard_map/ppermute | solution.py:340
  6.1 5.1 %collective-permute-start.1 = (bf16[4,7296]{1,0:T(4,128)(2,1)S(1)}, bf16[4,7296]{1,0:T(4,128)(2,1)S(1)}, u32[]{:S(2)}, u32[]{:S(2)}) collective-permute-start(bf16[4,7296]{1,0:T(4,128)(2,1)S(1)} %pack.1.refs_0_), channel_id=1, source_target_pairs={{0,2},{1,3},{2,0},{3,1},{4,6},{5,7},{6,4},{7,5},{8,10},{9,11},{10,... | collective-permute-start | bytes 175112 | tf_op jit(solution)/shard_map/ppermute | solution.py:340
  6.1 5.1 %collective-permute-start = (bf16[4,7296]{1,0:T(4,128)(2,1)S(1)}, bf16[4,7296]{1,0:T(4,128)(2,1)S(1)}, u32[]{:S(2)}, u32[]{:S(2)}) collective-permute-start(bf16[4,7296]{1,0:T(4,128)(2,1)S(1)} %pack.1.refs_0_), channel_id=1, source_target_pairs={{0,1},{1,0},{2,3},{3,2},{4,5},{5,4},{6,7},{7,6},{8,9},{9,8},{10,11... | collective-permute-start | bytes 175112 | tf_op jit(solution)/shard_map/ppermute | solution.py:340
  11.3 6.8 %collective-permute-start.4 = (bf16[16,7296]{1,0:T(8,128)(2,1)S(1)}, bf16[16,7296]{1,0:T(8,128)(2,1)S(1)}, u32[]{:S(2)}, u32[]{:S(2)}) collective-permute-start(bf16[16,7296]{1,0:T(8,128)(2,1)S(1)} %get-tuple-element.27.refs_0_), channel_id=1, source_target_pairs={{0,8},{4,12},{8,0},{12,4},{1,9},{5,13},{9,1},{13,5},{2,10},{6,14},... | collective-permute-start | bytes 700424 | tf_op jit(solution)/shard_map/ppermute | solution.py:352
  12.9 5.2 %collective-permute-start.3 = (bf16[16,7296]{1,0:T(8,128)(2,1)S(1)}, bf16[16,7296]{1,0:T(8,128)(2,1)S(1)}, u32[]{:S(2)}, u32[]{:S(2)}) collective-permute-start(bf16[16,7296]{1,0:T(8,128)(2,1)S(1)} %get-tuple-element.27.refs_0_), channel_id=1, source_target_pairs={{0,4},{4,0},{8,12},{12,8},{1,5},{5,1},{9,13},{13,9},{2,6},{6,2},{1... | collective-permute-start | bytes 700424 | tf_op jit(solution)/shard_map/ppermute | solution.py:351
  12.9 6.7 %slice-start.4 = ((s8[29360128]{0:T(1024)(128)(4,1)}), s8[4194304]{0:T(1024)(128)(4,1)S(1)}, s32[]{:S(2)}) async-start(s8[29360128]{0:T(1024)(128)(4,1)} %bitcast.3), calls=%async_computation.4 | async-start | bytes 8388608
  12.9 6.7 %slice-start.5 = ((s8[29360128]{0:T(1024)(128)(4,1)}), s8[4194304]{0:T(1024)(128)(4,1)S(1)}, s32[]{:S(2)}) async-start(s8[29360128]{0:T(1024)(128)(4,1)} %bitcast.3), calls=%async_computation.5 | async-start | bytes 8388608
  12.9 6.8 %slice-start.6 = ((s8[29360128]{0:T(1024)(128)(4,1)}), s8[4194304]{0:T(1024)(128)(4,1)S(1)}, s32[]{:S(2)}) async-start(s8[29360128]{0:T(1024)(128)(4,1)} %bitcast.3), calls=%async_computation.6 | async-start | bytes 8388608
  18.1 1.5 %collective-permute-start.5 = (bf16[16,7296]{1,0:T(8,128)(2,1)S(1)}, bf16[16,7296]{1,0:T(8,128)(2,1)S(1)}, u32[]{:S(2)}, u32[]{:S(2)}) collective-permute-start(bf16[16,7296]{1,0:T(8,128)(2,1)S(1)} %collective-permute-done.4.refs_2_), channel_id=1, source_target_pairs={{0,4},{4,0},{8,12},{12,8},{1,5},{5,1},{9,13},{13,9},{2,6},{6,2},{1... | collective-permute-start | bytes 700424 | tf_op jit(solution)/shard_map/ppermute | solution.py:364
  34.3 17.0 %copy-start = (bf16[4,4,7168]{2,1,0:T(4,128)(2,1)S(1)}, bf16[4,4,7168]{2,1,0:T(4,128)(2,1)}, u32[]{:S(2)}) copy-start(bf16[4,4,7168]{2,1,0:T(4,128)(2,1)} %dither_ref.1) | copy-start | bytes 688132
  34.3 13.5 %collective-permute-start.6 = (bf16[3,4,4096]{2,1,0:T(4,128)(2,1)S(1)}, bf16[3,4,4096]{2,1,0:T(4,128)(2,1)S(1)}, u32[]{:S(2)}, u32[]{:S(2)}) collective-permute-start(bf16[3,4,4096]{2,1,0:T(4,128)(2,1)S(1)} %get-tuple-element.33), channel_id=1, source_target_pairs={{0,1},{1,0},{2,3},{3,2},{4,5},{5,4},{6,7},{7,6},{8,9},{9,8},{10,11... | collective-permute-start | bytes 294920 | tf_op jit(solution)/shard_map/ppermute | solution.py:407
  35.4 13.7 %collective-permute-start.7 = (bf16[3,4,4096]{2,1,0:T(4,128)(2,1)S(1)}, bf16[3,4,4096]{2,1,0:T(4,128)(2,1)S(1)}, u32[]{:S(2)}, u32[]{:S(2)}) collective-permute-start(bf16[3,4,4096]{2,1,0:T(4,128)(2,1)S(1)} %get-tuple-element.34), channel_id=1, source_target_pairs={{0,2},{1,3},{2,0},{3,1},{4,6},{5,7},{6,4},{7,5},{8,10},{9,11},{10,... | collective-permute-start | bytes 294920 | tf_op jit(solution)/shard_map/ppermute | solution.py:407
  37.6 11.6 %collective-permute-start.8 = (bf16[3,4,4096]{2,1,0:T(4,128)(2,1)S(1)}, bf16[3,4,4096]{2,1,0:T(4,128)(2,1)S(1)}, u32[]{:S(2)}, u32[]{:S(2)}) collective-permute-start(bf16[3,4,4096]{2,1,0:T(4,128)(2,1)S(1)} %get-tuple-element.35), channel_id=1, source_target_pairs={{0,3},{1,2},{2,1},{3,0},{4,7},{5,6},{6,5},{7,4},{8,11},{9,10},{10,... | collective-permute-start | bytes 294920 | tf_op jit(solution)/shard_map/ppermute | solution.py:407
  44.7 6.4 %collective-permute-start.12 = (bf16[3,4,3072]{2,1,0:T(4,128)(2,1)S(1)}, bf16[3,4,3072]{2,1,0:T(4,128)(2,1)S(1)}, u32[]{:S(2)}, u32[]{:S(2)}) collective-permute-start(bf16[3,4,3072]{2,1,0:T(4,128)(2,1)S(1)} %get-tuple-element.42), channel_id=1, source_target_pairs={{0,1},{1,0},{2,3},{3,2},{4,5},{5,4},{6,7},{7,6},{8,9},{9,8},{10,11... | collective-permute-start | bytes 221192 | tf_op jit(solution)/shard_map/ppermute | solution.py:407
  44.8 8.3 %collective-permute-start.13 = (bf16[3,4,3072]{2,1,0:T(4,128)(2,1)S(1)}, bf16[3,4,3072]{2,1,0:T(4,128)(2,1)S(1)}, u32[]{:S(2)}, u32[]{:S(2)}) collective-permute-start(bf16[3,4,3072]{2,1,0:T(4,128)(2,1)S(1)} %get-tuple-element.43), channel_id=1, source_target_pairs={{0,2},{1,3},{2,0},{3,1},{4,6},{5,7},{6,4},{7,5},{8,10},{9,11},{10,... | collective-permute-start | bytes 221192 | tf_op jit(solution)/shard_map/ppermute | solution.py:407
  47.9 6.3 %collective-permute-start.14 = (bf16[3,4,3072]{2,1,0:T(4,128)(2,1)S(1)}, bf16[3,4,3072]{2,1,0:T(4,128)(2,1)S(1)}, u32[]{:S(2)}, u32[]{:S(2)}) collective-permute-start(bf16[3,4,3072]{2,1,0:T(4,128)(2,1)S(1)} %get-tuple-element.44), channel_id=1, source_target_pairs={{0,3},{1,2},{2,1},{3,0},{4,7},{5,6},{6,5},{7,4},{8,11},{9,10},{10,... | collective-permute-start | bytes 221192 | tf_op jit(solution)/shard_map/ppermute | solution.py:407
  49.3 4.8 %collective-permute-start.9 = (bf16[4,4096]{1,0:T(4,128)(2,1)S(1)}, bf16[4,4096]{1,0:T(4,128)(2,1)S(1)}, u32[]{:S(2)}, u32[]{:S(2)}) collective-permute-start(bf16[4,4096]{1,0:T(4,128)(2,1)S(1)} %get-tuple-element.37), channel_id=1, source_target_pairs={{0,4},{4,0},{8,12},{12,8},{1,5},{5,1},{9,13},{13,9},{2,6},{6,2},{1... | collective-permute-start | bytes 98312 | tf_op jit(solution)/shard_map/ppermute | solution.py:427
  49.4 4.7 %collective-permute-start.10 = (bf16[4,4096]{1,0:T(4,128)(2,1)S(1)}, bf16[4,4096]{1,0:T(4,128)(2,1)S(1)}, u32[]{:S(2)}, u32[]{:S(2)}) collective-permute-start(bf16[4,4096]{1,0:T(4,128)(2,1)S(1)} %get-tuple-element.38), channel_id=1, source_target_pairs={{0,8},{4,12},{8,0},{12,4},{1,9},{5,13},{9,1},{13,5},{2,10},{6,14},... | collective-permute-start | bytes 98312 | tf_op jit(solution)/shard_map/ppermute | solution.py:427
  51.1 3.3 %collective-permute-start.11 = (bf16[4,4096]{1,0:T(4,128)(2,1)S(1)}, bf16[4,4096]{1,0:T(4,128)(2,1)S(1)}, u32[]{:S(2)}, u32[]{:S(2)}) collective-permute-start(bf16[4,4096]{1,0:T(4,128)(2,1)S(1)} %get-tuple-element.39), channel_id=1, source_target_pairs={{0,12},{4,8},{8,4},{12,0},{1,13},{5,9},{9,5},{13,1},{2,14},{6,10},... | collective-permute-start | bytes 98312 | tf_op jit(solution)/shard_map/ppermute | solution.py:427
  54.6 1.9 %collective-permute-start.15 = (bf16[4,3072]{1,0:T(4,128)(2,1)S(1)}, bf16[4,3072]{1,0:T(4,128)(2,1)S(1)}, u32[]{:S(2)}, u32[]{:S(2)}) collective-permute-start(bf16[4,3072]{1,0:T(4,128)(2,1)S(1)} %get-tuple-element.46), channel_id=1, source_target_pairs={{0,4},{4,0},{8,12},{12,8},{1,5},{5,1},{9,13},{13,9},{2,6},{6,2},{1... | collective-permute-start | bytes 73736 | tf_op jit(solution)/shard_map/ppermute | solution.py:427
  54.8 3.8 %collective-permute-start.16 = (bf16[4,3072]{1,0:T(4,128)(2,1)S(1)}, bf16[4,3072]{1,0:T(4,128)(2,1)S(1)}, u32[]{:S(2)}, u32[]{:S(2)}) collective-permute-start(bf16[4,3072]{1,0:T(4,128)(2,1)S(1)} %get-tuple-element.47), channel_id=1, source_target_pairs={{0,8},{4,12},{8,0},{12,4},{1,9},{5,13},{9,1},{13,5},{2,10},{6,14},... | collective-permute-start | bytes 73736 | tf_op jit(solution)/shard_map/ppermute | solution.py:427
  55.7 3.3 %collective-permute-start.17 = (bf16[4,3072]{1,0:T(4,128)(2,1)S(1)}, bf16[4,3072]{1,0:T(4,128)(2,1)S(1)}, u32[]{:S(2)}, u32[]{:S(2)}) collective-permute-start(bf16[4,3072]{1,0:T(4,128)(2,1)S(1)} %get-tuple-element.48), channel_id=1, source_target_pairs={{0,12},{4,8},{8,4},{12,0},{1,13},{5,9},{9,5},{13,1},{2,14},{6,10},... | collective-permute-start | bytes 73736 | tf_op jit(solution)/shard_map/ppermute | solution.py:427
